TPU v7x, 32 devices: a whole 2x2x4 slice. The times are simulated.
32 devices in a mesh: gx: 8 (over z, x), gy: 4 (over y, core).
Axes of the slice: x: 2, y: 2, z: 4, core: 2. Of those that a mesh axis runs over, the one named last changes fastest.
Arguments:
- velocity: float32 [3, 128, 64, 128], P(None, 'gx', 'gy'), may hold values from -6 to 6
- velocity_old: float32 [3, 128, 64, 128], P(None, 'gx', 'gy'), may hold values from -6 to 6
- station_cell: int32 [131072], P(('gx', 'gy')), may hold values from 0 to 32767
- station_member: int32 [131072, 1], P(('gx', 'gy')), may hold values from 0 to 511, as said below
- drag_coef: float32 [131072], P(('gx', 'gy')), may hold values from 0.1 to 1
- inertia_coef: float32 [131072], P(('gx', 'gy')), may hold values from 0.3 to 3
- member_velocity: float32 [3, 512], P(None, ('gx', 'gy')), may hold values from -6 to 6
- member_inv_mass: float32 [512], P(('gx', 'gy')), may hold values from 0.002 to 0.02
Outputs:
- velocity_out: float32 [3, 128, 64, 128], P(None, 'gx', 'gy')
- member_out: float32 [3, 512], P(None, ('gx', 'gy'))
Inputs may be any that keep to these rules, and one draw needn't show every extreme that they name: `station_member`: members m with m // 16 = d belong to the device d of the joined axis gx+gy, which holds brick d. The stations of a brick name only members of that brick's device or of the devices beside it along gx (same gy index). Among the 4096 stations of one brick no member is named more than 128 times, and some member exactly 128 times; every member has stations in its own brick.
All inputs are finite; a program needn't handle non-finite values.
Results may differ from a plain program's by a relative error of at most 0.00014.
Values sent between devices are 32-bit elements; how exact they have to be, the bound alone decides.
No kernel may reach another device: no remote copies, remote signals or barrier semaphores. Data moves between devices by JAX's collectives and lax.ppermute only.
A program may use at most 64 MiB of HBM per device.

v0:
```python
import jax
import jax.numpy as jnp
from jax import lax
from jax.sharding import PartitionSpec as P

MOST = 128
STEPS = 2


viscous = 0.125
softening = 0.01


def extended(block, sides, width):
    for axis, dim in sides:
        count = lax.axis_size(axis)
        forward = [(i, i + 1) for i in range(count - 1)]
        backward = [(target, source) for source, target in forward]
        low = lax.ppermute(
            lax.slice_in_dim(block, block.shape[dim] - width, None, axis=dim), axis, forward
        )
        high = lax.ppermute(lax.slice_in_dim(block, 0, width, axis=dim), axis, backward)
        block = jnp.concatenate([low, block, high], axis=dim)
    return block


def smooth_local(field, axis):
    length = field.shape[axis] - 2
    lower = lax.slice_in_dim(field, 0, length, axis=axis)
    middle = lax.slice_in_dim(field, 1, length + 1, axis=axis)
    upper = lax.slice_in_dim(field, 2, length + 2, axis=axis)
    return 0.25 * lower + 0.5 * middle + 0.25 * upper


def station_forces(samples, old_samples, relative, drag, inertia):
    speeds = jnp.sqrt(jnp.sum(relative * relative, axis=0) + softening)
    return drag * speeds * relative + inertia * (samples - old_samples)


def sample_both(velocity, velocity_old, station_cell):
    both = jnp.concatenate([velocity, velocity_old], axis=0)
    flat_cells = both.reshape(6, -1)
    values = jnp.take(flat_cells, station_cell, axis=1)
    return (values[0:3], values[3:6])


def deposit(station_load, station_cell, cell_count):
    return jnp.zeros((3, cell_count), jnp.float32).at[:, station_cell].add(station_load)


def per_device(
    velocity,
    velocity_old,
    station_cell,
    station_member,
    drag_coef,
    inertia_coef,
    member_velocity,
    member_inv_mass,
):
    size_y = lax.axis_size("gy")
    mem_local = member_velocity.shape[1]
    slot_count = mem_local * MOST
    stations = station_cell.shape[0]
    shape_x, shape_y, shape_z = (velocity.shape[1], velocity.shape[2], velocity.shape[3])
    members = station_member[:, 0]
    ordering = jnp.argsort(members, stable=True)
    sorted_members = members[ordering]
    leading = jnp.searchsorted(sorted_members, sorted_members, side="left")
    ranks_sorted = jnp.arange(stations, dtype=jnp.int32) - leading
    ranks = jnp.zeros((stations,), jnp.int32).at[ordering].set(ranks_sorted)
    own_x = lax.axis_index("gx")
    owner_x = members // mem_local // size_y
    direction = jnp.where(owner_x == own_x, 0, jnp.where(owner_x == own_x + 1, 1, 2)).astype(
        jnp.int32
    )
    slot_index = direction * slot_count + members % mem_local * MOST + ranks
    for step_index in range(STEPS):
        samples, old_samples = sample_both(velocity, velocity_old, station_cell)
        payload = jnp.concatenate(
            [samples, old_samples, drag_coef[None], inertia_coef[None]], axis=0
        )
        outgoing = jnp.zeros((8, 3 * slot_count), jnp.float32).at[:, slot_index].set(payload)
        outgoing = outgoing.reshape(8, 3, slot_count)
        sending = jnp.stack([outgoing[:, 2], outgoing[:, 1]], axis=1)
        received = extended(sending, (("gx", 1),), 1)
        arrived = jnp.stack([outgoing[:, 0], received[:, 0], received[:, 3]], axis=1)
        arrived = arrived.reshape(8, 3, mem_local, MOST)
        relative = arrived[0:3] - member_velocity[:, None, :, None]
        forces = station_forces(arrived[0:3], arrived[3:6], relative, arrived[6], arrived[7])
        totals = jnp.sum(forces, axis=(1, 3))
        reaction = (-forces).reshape(3, 3, slot_count)
        backward = jnp.stack([reaction[:, 1], reaction[:, 2]], axis=1)
        came_back = extended(backward, (("gx", 1),), 1)
        returned = jnp.stack([reaction[:, 0], came_back[:, 3], came_back[:, 0]], axis=1)
        station_load = returned.reshape(3, -1)[:, slot_index]
        member_velocity = member_velocity + member_inv_mass * totals
        point_force = deposit(station_load, station_cell, shape_x * shape_y * shape_z)
        point_force = point_force.reshape(3, shape_x, shape_y, shape_z)
        padded_field = extended(velocity, (("gx", 1), ("gy", 2)), 1)
        padded_force = extended(point_force, (("gx", 1), ("gy", 2)), 1)
        smoothed = smooth_local(smooth_local(padded_force, 1), 2)
        smoothed = smooth_local(jnp.pad(smoothed, ((0, 0), (0, 0), (0, 0), (1, 1))), 3)
        center = padded_field[:, 1:-1, 1:-1]
        depth_pad = jnp.pad(center, ((0, 0), (0, 0), (0, 0), (1, 1)))
        beside_all = padded_field[:, 2:, 1:-1] + padded_field[:, :-2, 1:-1]
        beside_all = beside_all + padded_field[:, 1:-1, 2:] + padded_field[:, 1:-1, :-2]
        beside_all = beside_all + depth_pad[:, :, :, 2:] + depth_pad[:, :, :, :-2]
        updated = velocity + viscous * (beside_all - 6.0 * velocity) + smoothed
        velocity_old = velocity
        velocity = updated
    return (velocity, member_velocity)


def solution(mesh):
    return jax.shard_map(
        per_device,
        mesh=mesh,
        in_specs=(
            P(None, "gx", "gy", None),
            P(None, "gx", "gy", None),
            P(("gx", "gy")),
            P(("gx", "gy"), None),
            P(("gx", "gy")),
            P(("gx", "gy")),
            P(None, ("gx", "gy")),
            P(("gx", "gy")),
        ),
        out_specs=(P(None, "gx", "gy", None), P(None, ("gx", "gy"))),
        check_vma=False,
    )
```

profile of v0, /device:TPU:0, one launch (start us, length us, event | category | flops | bytes accessed | tf_op | source)
XLA Modules:
  0.0 652.1 jit_solution(9894619773364393882)
XLA Ops:
  0.7 6.5 %sort.17 = (s32[4096]{0:T(1024)}, s32[4096]{0:T(1024)S(1)}) sort(s32[4096]{0:T(1024)} %bitcast.47, s32[4096]{0:T(1024)S(1)} %iota.7), dimensions={0}, to_apply=%region_0.0 | sort | flops 49152 | bytes 65536 | tf_op jit(solution)/shard_map/jit(argsort)/sort | solution.py:67
  7.2 23.0 %gather_fusion.1 = s32[4096]{0:T(1024)S(1)} fusion(s32[4096]{0:T(1024)S(1)} %bitcast.48, s32[4096]{0:T(1024)S(1)} %get-tuple-element.134), kind=kCustom, calls=%fused_computation.3 | custom fusion | bytes 49152 | tf_op jit(solution)/shard_map/gather | solution.py:68
  30.3 300.6 %while.25 = (s32[]{:T(128)}, u32[4096]{0:T(1024)S(1)}, u32[4096]{0:T(1024)S(1)}, s32[4096]{0:T(1024)S(1)}, s32[]{:T(128)}, /*index=5*/s32[]{:T(128)}, s32[]{}) while((s32[]{:T(128)}, u32[4096]{0:T(1024)S(1)}, u32[4096]{0:T(1024)S(1)}, s32[4096]{0:T(1024)S(1)}, s32[]{:T(128)}, /*index=5*/s32[]{:T(128)}, s32[]{}) %tuple.64), condition=%wide.region_2.3_spmd.clone, body=%wide.region_1.2_spmd.clone.sunk | while | flops 77828 | bytes 270445 | solution.py:69
  30.3 23.0 %gather_fusion = s32[4096]{0:T(1024)S(1)} fusion(s32[4096]{0:T(1024)S(1)} %get-tuple-element.184, u32[4096]{0:T(1024)S(1)} %broadcast_clamp_fusion.5), kind=kCustom, calls=%fused_computation.clone.clone.1 | custom fusion | bytes 49152 | tf_op jit(solution)/shard_map/jit(searchsorted)/jit(_searchsorted_scan_impl)/vmap(jit(_searchsorted_scan_impl))/while/body/eval_jaxpr/gather | solution.py:69
  53.4 23.0 %gather_fusion = s32[4096]{0:T(1024)S(1)} fusion(s32[4096]{0:T(1024)S(1)} %get-tuple-element.184, u32[4096]{0:T(1024)S(1)} %broadcast_clamp_fusion.5), kind=kCustom, calls=%fused_computation.clone.clone.1 | custom fusion | bytes 49152 | tf_op jit(solution)/shard_map/jit(searchsorted)/jit(_searchsorted_scan_impl)/vmap(jit(_searchsorted_scan_impl))/while/body/eval_jaxpr/gather | solution.py:69
  76.6 23.0 %gather_fusion = s32[4096]{0:T(1024)S(1)} fusion(s32[4096]{0:T(1024)S(1)} %get-tuple-element.184, u32[4096]{0:T(1024)S(1)} %broadcast_clamp_fusion.5), kind=kCustom, calls=%fused_computation.clone.clone.1 | custom fusion | bytes 49152 | tf_op jit(solution)/shard_map/jit(searchsorted)/jit(_searchsorted_scan_impl)/vmap(jit(_searchsorted_scan_impl))/while/body/eval_jaxpr/gather | solution.py:69
  99.7 23.0 %gather_fusion = s32[4096]{0:T(1024)S(1)} fusion(s32[4096]{0:T(1024)S(1)} %get-tuple-element.184, u32[4096]{0:T(1024)S(1)} %broadcast_clamp_fusion.5), kind=kCustom, calls=%fused_computation.clone.clone.1 | custom fusion | bytes 49152 | tf_op jit(solution)/shard_map/jit(searchsorted)/jit(_searchsorted_scan_impl)/vmap(jit(_searchsorted_scan_impl))/while/body/eval_jaxpr/gather | solution.py:69
  122.8 23.0 %gather_fusion = s32[4096]{0:T(1024)S(1)} fusion(s32[4096]{0:T(1024)S(1)} %get-tuple-element.184, u32[4096]{0:T(1024)S(1)} %broadcast_clamp_fusion.5), kind=kCustom, calls=%fused_computation.clone.clone.1 | custom fusion | bytes 49152 | tf_op jit(solution)/shard_map/jit(searchsorted)/jit(_searchsorted_scan_impl)/vmap(jit(_searchsorted_scan_impl))/while/body/eval_jaxpr/gather | solution.py:69
  145.9 23.0 %gather_fusion = s32[4096]{0:T(1024)S(1)} fusion(s32[4096]{0:T(1024)S(1)} %get-tuple-element.184, u32[4096]{0:T(1024)S(1)} %broadcast_clamp_fusion.5), kind=kCustom, calls=%fused_computation.clone.clone.1 | custom fusion | bytes 49152 | tf_op jit(solution)/shard_map/jit(searchsorted)/jit(_searchsorted_scan_impl)/vmap(jit(_searchsorted_scan_impl))/while/body/eval_jaxpr/gather | solution.py:69
  169.1 23.0 %gather_fusion = s32[4096]{0:T(1024)S(1)} fusion(s32[4096]{0:T(1024)S(1)} %get-tuple-element.184, u32[4096]{0:T(1024)S(1)} %broadcast_clamp_fusion.5), kind=kCustom, calls=%fused_computation.clone.clone.1 | custom fusion | bytes 49152 | tf_op jit(solution)/shard_map/jit(searchsorted)/jit(_searchsorted_scan_impl)/vmap(jit(_searchsorted_scan_impl))/while/body/eval_jaxpr/gather | solution.py:69
  192.2 23.0 %gather_fusion = s32[4096]{0:T(1024)S(1)} fusion(s32[4096]{0:T(1024)S(1)} %get-tuple-element.184, u32[4096]{0:T(1024)S(1)} %broadcast_clamp_fusion.5), kind=kCustom, calls=%fused_computation.clone.clone.1 | custom fusion | bytes 49152 | tf_op jit(solution)/shard_map/jit(searchsorted)/jit(_searchsorted_scan_impl)/vmap(jit(_searchsorted_scan_impl))/while/body/eval_jaxpr/gather | solution.py:69
  215.3 23.0 %gather_fusion = s32[4096]{0:T(1024)S(1)} fusion(s32[4096]{0:T(1024)S(1)} %get-tuple-element.184, u32[4096]{0:T(1024)S(1)} %broadcast_clamp_fusion.5), kind=kCustom, calls=%fused_computation.clone.clone.1 | custom fusion | bytes 49152 | tf_op jit(solution)/shard_map/jit(searchsorted)/jit(_searchsorted_scan_impl)/vmap(jit(_searchsorted_scan_impl))/while/body/eval_jaxpr/gather | solution.py:69
  238.4 23.0 %gather_fusion = s32[4096]{0:T(1024)S(1)} fusion(s32[4096]{0:T(1024)S(1)} %get-tuple-element.184, u32[4096]{0:T(1024)S(1)} %broadcast_clamp_fusion.5), kind=kCustom, calls=%fused_computation.clone.clone.1 | custom fusion | bytes 49152 | tf_op jit(solution)/shard_map/jit(searchsorted)/jit(_searchsorted_scan_impl)/vmap(jit(_searchsorted_scan_impl))/while/body/eval_jaxpr/gather | solution.py:69
  261.6 23.0 %gather_fusion = s32[4096]{0:T(1024)S(1)} fusion(s32[4096]{0:T(1024)S(1)} %get-tuple-element.184, u32[4096]{0:T(1024)S(1)} %broadcast_clamp_fusion.5), kind=kCustom, calls=%fused_computation.clone.clone.1 | custom fusion | bytes 49152 | tf_op jit(solution)/shard_map/jit(searchsorted)/jit(_searchsorted_scan_impl)/vmap(jit(_searchsorted_scan_impl))/while/body/eval_jaxpr/gather | solution.py:69
  284.7 23.0 %gather_fusion = s32[4096]{0:T(1024)S(1)} fusion(s32[4096]{0:T(1024)S(1)} %get-tuple-element.184, u32[4096]{0:T(1024)S(1)} %broadcast_clamp_fusion.5), kind=kCustom, calls=%fused_computation.clone.clone.1 | custom fusion | bytes 49152 | tf_op jit(solution)/shard_map/jit(searchsorted)/jit(_searchsorted_scan_impl)/vmap(jit(_searchsorted_scan_impl))/while/body/eval_jaxpr/gather | solution.py:69
  307.8 23.0 %gather_fusion = s32[4096]{0:T(1024)S(1)} fusion(s32[4096]{0:T(1024)S(1)} %get-tuple-element.184, u32[4096]{0:T(1024)S(1)} %broadcast_clamp_fusion.5), kind=kCustom, calls=%fused_computation.clone.clone.1 | custom fusion | bytes 49152 | tf_op jit(solution)/shard_map/jit(searchsorted)/jit(_searchsorted_scan_impl)/vmap(jit(_searchsorted_scan_impl))/while/body/eval_jaxpr/gather | solution.py:69
  331.0 8.8 %copy.63 = f32[6,16,16,128]{0,3,2,1:T(8,128)} copy(f32[6,16,16,128]{3,2,1,0:T(8,128)S(1)} %pad_maximum_fusion) | data formatting | bytes 1572864 | tf_op jit(solution)/shard_map/concatenate | solution.py:41
  339.8 15.5 %scatter_custom_fusion = s32[4096]{0:T(1024)S(1)} fusion(s32[4096]{0:T(1024)S(1)} %get-tuple-element.135, s32[4096]{0:T(1024)S(1)} %convert_subtract_fusion, s32[]{:T(128)} %constant.99.clone.1), kind=kCustom, calls=%fused_computation.163 | custom fusion | bytes 16388 | tf_op jit(solution)/shard_map/scatter | solution.py:71
  356.0 19.9 %gather_fusion.2 = f32[4096,6]{1,0:T(8,128)} fusion(f32[6,32768]{0,1:T(8,128)} %bitcast.52, s32[4096]{0:T(1024)S(1)} %get-tuple-element.137), kind=kCustom, calls=%fused_computation.1.clone | custom fusion | bytes 212992 | tf_op jit(solution)/shard_map/jit(_take)/gather | solution.py:43
  376.0 3.6 select_bitcast_fusion.1
  380.3 2.0 copy.65
  382.2 11.7 %scatter_custom_fusion.1 = f32[8,6144]{0,1:T(8,128)S(1)} fusion(s32[4096]{0:T(1024)} %get-tuple-element.103, f32[4096,8]{1,0:T(8,128)} %copy.65, f32[]{:T(128)} %constant.96.clone.1), kind=kCustom, calls=%fused_computation.25 | custom fusion | bytes 197120 | tf_op jit(solution)/shard_map/scatter | solution.py:83
  393.9 1.7 fusion.65
  395.7 1.5 copy.85
  397.2 1.3 collective-permute-start.5
  398.5 1.5 copy.84
  400.0 5.5 collective-permute-start.4
  405.5 4.8 collective-permute-start.1
  412.4 1.5 copy.83
  414.0 2.0 collective-permute-done
  416.8 1.9 collective-permute-start.3
  420.6 3.5 collective-permute-start.7
  424.1 1.5 collective-permute-start.6
  426.2 3.6 collective-permute-done.6
  430.5 1.8 copy.69
  432.3 41.2 %scatter_custom_fusion.2 = f32[3,32768]{0,1:T(8,128)} fusion(s32[4096]{0:T(1024)} %get-tuple-element.136, f32[]{:T(128)} %constant.96.clone.1, f32[3,6144]{0,1:T(8,128)S(1)} %bitcast.57, s32[4096]{0:T(1024)} %get-tuple-element.102), kind=kCustom, calls=%fused_computation.17 | custom fusion | flops 12288 | bytes 393728 | tf_op jit(solution)/shard_map/scatter-add | solution.py:48
  473.5 10.0 %copy.70 = f32[3,16,16,128]{3,2,1,0:T(8,128)S(1)} copy(f32[3,16,16,128]{0,3,2,1:T(8,128)} %bitcast.51) | data formatting | bytes 786432 | tf_op jit(solution)/shard_map/reshape | solution.py:99
  483.6 1.4 collective-permute-start.9
  485.0 4.9 collective-permute-start.8
  490.0 1.4 collective-permute-done.8
  492.8 3.0 collective-permute-start.10
  499.1 8.8 %copy.73 = f32[6,16,16,128]{0,3,2,1:T(8,128)} copy(f32[6,16,16,128]{3,2,1,0:T(8,128)S(1)} %pad_maximum_fusion.1) | data formatting | bytes 1572864 | tf_op jit(solution)/shard_map/concatenate | solution.py:41
  507.8 19.9 %gather_fusion.3 = f32[4096,6]{1,0:T(8,128)} fusion(f32[6,32768]{0,1:T(8,128)} %bitcast.53, s32[4096]{0:T(1024)S(1)} %get-tuple-element.137), kind=kCustom, calls=%fused_computation.2.clone | custom fusion | bytes 212992 | tf_op jit(solution)/shard_map/jit(_take)/gather | solution.py:43
  527.8 3.6 select_bitcast_fusion
  532.1 2.0 copy.75
  534.1 11.9 %scatter_custom_fusion.3 = f32[8,6144]{0,1:T(8,128)S(1)} fusion(s32[4096]{0:T(1024)} %get-tuple-element.103, f32[4096,8]{1,0:T(8,128)} %copy.75, f32[]{:T(128)} %constant.96.clone.1), kind=kCustom, calls=%fused_computation.23 | custom fusion | bytes 197120 | tf_op jit(solution)/shard_map/scatter | solution.py:83
  546.0 1.7 fusion.64
  547.7 1.5 copy.88
  549.2 1.3 collective-permute-start.17
  550.6 1.5 copy.87
  552.1 5.5 collective-permute-start.16
  557.6 1.5 copy.86
  559.1 1.3 collective-permute-start.12
  560.4 5.7 collective-permute-start.13
  567.4 4.8 collective-permute-start.19
  574.2 5.0 collective-permute-start.15
  581.3 1.8 copy.79
  583.1 41.2 %scatter_custom_fusion.4 = f32[3,32768]{0,1:T(8,128)} fusion(s32[4096]{0:T(1024)} %get-tuple-element.136, f32[]{:T(128)} %constant.96.clone.1, f32[3,6144]{0,1:T(8,128)S(1)} %bitcast.56, s32[4096]{0:T(1024)} %get-tuple-element.102), kind=kCustom, calls=%fused_computation.15 | custom fusion | flops 12288 | bytes 393728 | tf_op jit(solution)/shard_map/scatter-add | solution.py:48
  624.2 10.0 %copy.80 = f32[3,16,16,128]{3,2,1,0:T(8,128)S(1)} copy(f32[3,16,16,128]{0,3,2,1:T(8,128)} %bitcast.50) | data formatting | bytes 786432 | tf_op jit(solution)/shard_map/reshape | solution.py:99
  634.3 1.4 collective-permute-start.21
  635.7 4.9 collective-permute-start.20
  640.7 1.4 collective-permute-done.20
  643.4 5.4 collective-permute-start.22
  650.1 2.0 fusion.29
  (193 shorter events, 21.0 us)
Async XLA Ops:
  0.6 6.6 %copy-start = (s32[4096,1]{0,1:T(1,128)S(1)}, s32[4096,1]{0,1:T(1,128)}, u32[]{:S(2)}) copy-start(s32[4096,1]{0,1:T(1,128)} %param.15) | copy-start | bytes 49156
  30.3 300.7 %copy-start.1 = (f32[3,16,16,128]{3,2,1,0:T(8,128)S(1)}, f32[3,16,16,128]{3,2,1,0:T(8,128)}, u32[]{:S(2)}) copy-start(f32[3,16,16,128]{3,2,1,0:T(8,128)} %param.12) | copy-start | bytes 1179652
  30.3 300.7 %copy-start.6 = (f32[3,16,16,128]{3,2,1,0:T(8,128)S(1)}, f32[3,16,16,128]{3,2,1,0:T(8,128)}, u32[]{:S(2)}) copy-start(f32[3,16,16,128]{3,2,1,0:T(8,128)} %param.13) | copy-start | bytes 1179652
  331.0 8.8 %copy-start.21 = (s32[4096]{0:T(1024)S(1)}, s32[4096]{0:T(1024)}, u32[]{:S(2)}) copy-start(s32[4096]{0:T(1024)} %param.14) | copy-start | bytes 49156
  339.8 36.1 %copy-start.22 = (pred[4096]{0:T(1024)(128)(4,1)}, pred[4096]{0:T(1024)(128)(4,1)S(1)}, u32[]{:S(2)}) copy-start(pred[4096]{0:T(1024)(128)(4,1)S(1)} %compare_and_fusion) | copy-start | bytes 12292
  376.0 4.3 copy-start.17
  376.0 4.3 copy-start.19
  397.2 22.8 %collective-permute-start.5 = (f32[8,1,2048]{2,1,0:T(1,128)S(1)}, f32[8,1,2048]{2,1,0:T(1,128)S(1)}, u32[]{:S(2)}, u32[]{:S(2)}) collective-permute-start(f32[8,1,2048]{2,1,0:T(1,128)S(1)} %copy.85), channel_id=1, source_target_pairs={{4,0},{8,4},{12,8},{16,12},{20,16},{24,20},{28,24},{5,1},{9,5},{13... | collective-permute-start | bytes 196616 | tf_op jit(solution)/shard_map/ppermute | solution.py:22
  400.0 20.0 %collective-permute-start.4 = (f32[8,1,2048]{2,1,0:T(1,128)S(1)}, f32[8,1,2048]{2,1,0:T(1,128)S(1)}, u32[]{:S(2)}, u32[]{:S(2)}) collective-permute-start(f32[8,1,2048]{2,1,0:T(1,128)S(1)} %copy.84), channel_id=1, source_target_pairs={{0,4},{4,8},{8,12},{12,16},{16,20},{20,24},{24,28},{1,5},{5,9},{9,... | collective-permute-start | bytes 196616 | tf_op jit(solution)/shard_map/ppermute | solution.py:19
  405.5 8.4 %collective-permute-start.1 = (f32[3,1,16,128]{3,2,1,0:T(8,128)S(1)}, f32[3,1,16,128]{3,2,1,0:T(8,128)S(1)}, u32[]{:S(2)}, u32[]{:S(2)}) collective-permute-start(f32[3,1,16,128]{3,2,1,0:T(8,128)S(1)} %get-tuple-element.123), channel_id=1, source_target_pairs={{0,4},{4,8},{8,12},{12,16},{16,20},{20,24},{24,28},{1,5},{5,9},{9,... | collective-permute-start | bytes 73736 | tf_op jit(solution)/shard_map/ppermute | solution.py:19
  410.4 5.7 collective-permute-start
  414.0 6.3 copy-start.13
  416.1 4.2 copy-start.15
  416.1 3.9 copy-start.4
  416.8 80.1 %collective-permute-start.3 = (f32[3,18,1,128]{3,2,1,0:T(1,128)}, f32[3,18,1,128]{3,2,1,0:T(1,128)}, u32[]{:S(2)}, u32[]{:S(2)}) collective-permute-start(f32[3,18,1,128]{3,2,1,0:T(1,128)} %get-tuple-element.115), channel_id=1, source_target_pairs={{0,1},{1,2},{2,3},{4,5},{5,6},{6,7},{8,9},{9,10},{10,11},{12,13},{... | collective-permute-start | bytes 82952 | tf_op jit(solution)/shard_map/ppermute | solution.py:19
  418.7 78.3 %collective-permute-start.2 = (f32[3,18,1,128]{3,2,1,0:T(1,128)}, f32[3,18,1,128]{3,2,1,0:T(1,128)}, u32[]{:S(2)}, u32[]{:S(2)}) collective-permute-start(f32[3,18,1,128]{3,2,1,0:T(1,128)} %get-tuple-element.114), channel_id=1, source_target_pairs={{1,0},{2,1},{3,2},{5,4},{6,5},{7,6},{9,8},{10,9},{11,10},{13,12},{... | collective-permute-start | bytes 82952 | tf_op jit(solution)/shard_map/ppermute | solution.py:22
  420.6 5.6 collective-permute-start.7
  424.1 5.7 collective-permute-start.6
  473.5 16.4 %copy-start.26 = (f32[3,16]{1,0:T(4,128)S(1)}, f32[3,16]{1,0:T(4,128)}, u32[]{:S(2)}) copy-start(f32[3,16]{1,0:T(4,128)} %bitcast_reduce_fusion.1) | copy-start | bytes 580
  473.5 16.4 %copy-start.27 = (f32[3,16]{1,0:T(4,128)S(1)}, f32[3,16]{1,0:T(4,128)}, u32[]{:S(2)}) copy-start(f32[3,16]{1,0:T(4,128)} %param.18) | copy-start | bytes 580
  473.5 16.5 %copy-start.28 = (f32[16]{0:T(128)S(1)}, f32[16]{0:T(128)}, u32[]{:S(2)}) copy-start(f32[16]{0:T(128)} %param.19) | copy-start | bytes 196
  483.5 13.5 %copy-start.5 = (f32[3,18,16,128]{3,2,1,0:T(8,128)S(1)}, f32[3,18,16,128]{3,2,1,0:T(8,128)}, u32[]{:S(2)}) copy-start(f32[3,18,16,128]{3,2,1,0:T(8,128)} %copy-done.4) | copy-start | bytes 1327108
  483.5 13.5 %copy-start.14 = (f32[3,1,16,128]{3,2,1,0:T(8,128)S(1)}, f32[3,1,16,128]{3,2,1,0:T(8,128)}, u32[]{:S(2)}) copy-start(f32[3,1,16,128]{3,2,1,0:T(8,128)} %copy-done.13) | copy-start | bytes 73732
  483.5 13.5 %copy-start.16 = (f32[3,1,16,128]{3,2,1,0:T(8,128)S(1)}, f32[3,1,16,128]{3,2,1,0:T(8,128)}, u32[]{:S(2)}) copy-start(f32[3,1,16,128]{3,2,1,0:T(8,128)} %copy-done.15) | copy-start | bytes 73732
  483.6 6.4 collective-permute-start.9
  485.0 6.4 collective-permute-start.8
  490.0 6.5 %copy-start.24 = (f32[3,16]{1,0:T(4,128)}, f32[3,16]{1,0:T(4,128)S(1)}, u32[]{:S(2)}) copy-start(f32[3,16]{1,0:T(4,128)S(1)} %multiply_add_fusion.1) | copy-start | bytes 580
  491.5 5.0 collective-permute-start.11
  492.8 3.9 collective-permute-start.10
  498.3 0.7 copy-start.2
  499.1 28.7 %copy-start.23 = (pred[4096]{0:T(1024)(128)(4,1)S(1)}, pred[4096]{0:T(1024)(128)(4,1)}, u32[]{:S(2)}) copy-start(pred[4096]{0:T(1024)(128)(4,1)} %copy-done.22) | copy-start | bytes 12292
  527.8 4.3 copy-start.18
  527.8 4.3 copy-start.20
  546.0 11.6 %copy-start.3 = (f32[3,16,16,128]{3,2,1,0:T(8,128)S(1)}, f32[3,16,16,128]{3,2,1,0:T(8,128)}, u32[]{:S(2)}) copy-start(f32[3,16,16,128]{3,2,1,0:T(8,128)} %copy-done.2) | copy-start | bytes 1179652
  547.7 18.6 %copy-start.7 = (f32[1,3,16,128]{3,1,2,0:T(4,128)S(1)}, f32[1,3,16,128]{3,1,2,0:T(4,128)}, u32[]{:S(2)}) copy-start(f32[1,3,16,128]{3,1,2,0:T(4,128)} %copy.97) | copy-start | bytes 73732
  549.2 16.9 %collective-permute-start.17 = (f32[8,1,2048]{2,1,0:T(1,128)S(1)}, f32[8,1,2048]{2,1,0:T(1,128)S(1)}, u32[]{:S(2)}, u32[]{:S(2)}) collective-permute-start(f32[8,1,2048]{2,1,0:T(1,128)S(1)} %copy.88), channel_id=1, source_target_pairs={{4,0},{8,4},{12,8},{16,12},{20,16},{24,20},{28,24},{5,1},{9,5},{13... | collective-permute-start | bytes 196616 | tf_op jit(solution)/shard_map/ppermute | solution.py:22
  552.1 14.1 %collective-permute-start.16 = (f32[8,1,2048]{2,1,0:T(1,128)S(1)}, f32[8,1,2048]{2,1,0:T(1,128)S(1)}, u32[]{:S(2)}, u32[]{:S(2)}) collective-permute-start(f32[8,1,2048]{2,1,0:T(1,128)S(1)} %copy.87), channel_id=1, source_target_pairs={{0,4},{4,8},{8,12},{12,16},{16,20},{20,24},{24,28},{1,5},{5,9},{9,... | collective-permute-start | bytes 196616 | tf_op jit(solution)/shard_map/ppermute | solution.py:19
  559.1 14.4 %collective-permute-start.12 = (f32[3,1,16,128]{3,2,1,0:T(8,128)S(1)}, f32[3,1,16,128]{3,2,1,0:T(8,128)S(1)}, u32[]{:S(2)}, u32[]{:S(2)}) collective-permute-start(f32[3,1,16,128]{3,2,1,0:T(8,128)S(1)} %get-tuple-element.119), channel_id=1, source_target_pairs={{4,0},{8,4},{12,8},{16,12},{20,16},{24,20},{28,24},{5,1},{9,5},{13... | collective-permute-start | bytes 73736 | tf_op jit(solution)/shard_map/ppermute | solution.py:22
  560.4 13.1 %collective-permute-start.13 = (f32[3,1,16,128]{3,2,1,0:T(8,128)S(1)}, f32[3,1,16,128]{3,2,1,0:T(8,128)S(1)}, u32[]{:S(2)}, u32[]{:S(2)}) collective-permute-start(f32[3,1,16,128]{3,2,1,0:T(8,128)S(1)} %get-tuple-element.118), channel_id=1, source_target_pairs={{0,4},{4,8},{8,12},{12,16},{16,20},{20,24},{24,28},{1,5},{5,9},{9,... | collective-permute-start | bytes 73736 | tf_op jit(solution)/shard_map/ppermute | solution.py:19
  567.4 13.2 %collective-permute-start.19 = (f32[3,1,2048]{2,1,0:T(1,128)S(1)}, f32[3,1,2048]{2,1,0:T(1,128)S(1)}, u32[]{:S(2)}, u32[]{:S(2)}) collective-permute-start(f32[3,1,2048]{2,1,0:T(1,128)S(1)} %get-tuple-element.127), channel_id=1, source_target_pairs={{0,4},{4,8},{8,12},{12,16},{16,20},{20,24},{24,28},{1,5},{5,9},{9,... | collective-permute-start | bytes 73736 | tf_op jit(solution)/shard_map/ppermute | solution.py:19
  572.2 8.3 %collective-permute-start.18 = (f32[3,1,2048]{2,1,0:T(1,128)S(1)}, f32[3,1,2048]{2,1,0:T(1,128)S(1)}, u32[]{:S(2)}, u32[]{:S(2)}) collective-permute-start(f32[3,1,2048]{2,1,0:T(1,128)S(1)} %get-tuple-element.128), channel_id=1, source_target_pairs={{4,0},{8,4},{12,8},{16,12},{20,16},{24,20},{28,24},{5,1},{9,5},{13... | collective-permute-start | bytes 73736 | tf_op jit(solution)/shard_map/ppermute | solution.py:22
  573.5 7.0 %copy-start.9 = (f32[3,1,16,128]{3,2,1,0:T(8,128)}, f32[3,1,16,128]{3,2,1,0:T(8,128)S(1)}, u32[]{:S(2)}) copy-start(f32[3,1,16,128]{3,2,1,0:T(8,128)S(1)} %collective-permute-done.12) | copy-start | bytes 73732
  573.5 7.0 %copy-start.11 = (f32[3,1,16,128]{3,2,1,0:T(8,128)}, f32[3,1,16,128]{3,2,1,0:T(8,128)S(1)}, u32[]{:S(2)}) copy-start(f32[3,1,16,128]{3,2,1,0:T(8,128)S(1)} %collective-permute-done.13) | copy-start | bytes 73732
  574.2 75.9 %collective-permute-start.15 = (f32[3,18,1,128]{3,2,1,0:T(1,128)}, f32[3,18,1,128]{3,2,1,0:T(1,128)}, u32[]{:S(2)}, u32[]{:S(2)}) collective-permute-start(f32[3,18,1,128]{3,2,1,0:T(1,128)} %get-tuple-element.111), channel_id=1, source_target_pairs={{0,1},{1,2},{2,3},{4,5},{5,6},{6,7},{8,9},{9,10},{10,11},{12,13},{... | collective-permute-start | bytes 82952 | tf_op jit(solution)/shard_map/ppermute | solution.py:19
  579.2 70.8 %collective-permute-start.14 = (f32[3,18,1,128]{3,2,1,0:T(1,128)}, f32[3,18,1,128]{3,2,1,0:T(1,128)}, u32[]{:S(2)}, u32[]{:S(2)}) collective-permute-start(f32[3,18,1,128]{3,2,1,0:T(1,128)} %get-tuple-element.110), channel_id=1, source_target_pairs={{1,0},{2,1},{3,2},{5,4},{6,5},{7,6},{9,8},{10,9},{11,10},{13,12},{... | collective-permute-start | bytes 82952 | tf_op jit(solution)/shard_map/ppermute | solution.py:22
  624.2 16.4 %copy-start.8 = (f32[3,2048]{1,0:T(4,128)S(1)}, f32[3,2048]{1,0:T(4,128)}, u32[]{:S(2)}) copy-start(f32[3,2048]{1,0:T(4,128)} %get-tuple-element.98) | copy-start | bytes 73732
  624.2 24.7 %copy-start.25 = (f32[3,16]{1,0:T(4,128)S(1)}, f32[3,16]{1,0:T(4,128)}, u32[]{:S(2)}) copy-start(f32[3,16]{1,0:T(4,128)} %copy-done.24) | copy-start | bytes 580
  624.2 24.7 %copy-start.29 = (f32[16]{0:T(128)S(1)}, f32[16]{0:T(128)}, u32[]{:S(2)}) copy-start(f32[16]{0:T(128)} %param.19) | copy-start | bytes 196
  634.2 15.8 %copy-start.10 = (f32[3,1,16,128]{3,2,1,0:T(8,128)S(1)}, f32[3,1,16,128]{3,2,1,0:T(8,128)}, u32[]{:S(2)}) copy-start(f32[3,1,16,128]{3,2,1,0:T(8,128)} %copy-done.9) | copy-start | bytes 73732
  634.2 15.8 %copy-start.12 = (f32[3,1,16,128]{3,2,1,0:T(8,128)S(1)}, f32[3,1,16,128]{3,2,1,0:T(8,128)}, u32[]{:S(2)}) copy-start(f32[3,1,16,128]{3,2,1,0:T(8,128)} %copy-done.11) | copy-start | bytes 73732
  634.3 6.4 collective-permute-start.21
  635.7 6.4 collective-permute-start.20
  642.1 7.3 %collective-permute-start.23 = (f32[3,18,1,128]{3,2,1,0:T(1,128)S(1)}, f32[3,18,1,128]{3,2,1,0:T(1,128)S(1)}, u32[]{:S(2)}, u32[]{:S(2)}) collective-permute-start(f32[3,18,1,128]{3,2,1,0:T(1,128)S(1)} %get-tuple-element.113), channel_id=1, source_target_pairs={{1,0},{2,1},{3,2},{5,4},{6,5},{7,6},{9,8},{10,9},{11,10},{13,12},{... | collective-permute-start | bytes 82952 | tf_op jit(solution)/shard_map/ppermute | solution.py:22
  643.4 6.3 collective-permute-start.22
where the time goes:
time: 659 us; the launch traced here: 652 us
  local copies, waits for them, and re-layouts  464 us (70%)
  other arithmetic  106 us (16%)
  starting transfers between devices  71 us (11%)
  waiting for transfers between devices  8.86 us (1%)
    gather x13, local copies, waits for them, and re-layouts, per_device(): leading = jnp.searchsorted(sorted_members, sorted_members, side='left')  299 us
    scatter-add x2, other arithmetic, deposit(): jnp.zeros((3, cell_count), jnp.float32).at[:, station_cell]  82.3 us
    ppermute x12, starting transfers between devices, extended(): lax.ppermute(lax.slice_in_dim(block, block.shape[dim] - width, None, axis...  55 us
    gather x2, local copies, waits for them, and re-layouts, sample_both(): values = jnp.take(flat_cells, station_cell, axis=1)  39.8 us
    scatter x2, local copies, waits for them, and re-layouts, per_device(): jnp.zeros((8, 3 * slot_count), jnp.float32).at[:, slot_index].set(payload)  23.6 us
    gather x1, local copies, waits for them, and re-layouts, per_device(): sorted_members = members[ordering]  23 us
    reshape x2, local copies, waits for them, and re-layouts, per_device(): point_force = point_force.reshape(3, shape_x, shape_y, shape_z)  20 us
    concatenate x2, local copies, waits for them, and re-layouts, sample_both(): both = jnp.concatenate([velocity, velocity_old], axis=0)  17.5 us
  transfers between devices with their start and end apart: 24, of which 6 were waited for; matrix products, arithmetic and copies ran while one was open for 18% of the time, Pallas kernels for 0%

commit v1 on v0

v1 whole, which is shorter than its diff:
```python
import functools

import jax
import jax.numpy as jnp
from jax import lax
from jax.experimental import pallas as pl
from jax.experimental.pallas import tpu as pltpu
from jax.sharding import PartitionSpec as P

STEPS = 2
LANES = 128
WIDE = 256

viscous = 0.125
softening = 0.01

f32 = jnp.float32
bf16 = jnp.bfloat16
VMEM = pltpu.VMEM


def call(body, outs, scratch=(), flops=0, size=0, limit=24):
    return pl.pallas_call(
        body,
        out_shape=[jax.ShapeDtypeStruct(s, f32) for s in outs],
        scratch_shapes=list(scratch),
        compiler_params=pltpu.CompilerParams(vmem_limit_bytes=limit << 20),
        cost_estimate=pl.CostEstimate(flops=flops, bytes_accessed=size, transcendentals=0),
    )


def split(x):
    top = x.astype(bf16)
    return top, (x - top.astype(f32)).astype(bf16)


def one_hot_t(index_row, count):
    ids = lax.broadcasted_iota(jnp.int32, (count, index_row.shape[1]), 0)
    return jnp.where(ids == index_row, 1.0, 0.0).astype(bf16)


def wide_row(ref, first):
    return jnp.concatenate([ref[pl.ds(first, 1), :], ref[pl.ds(first + 1, 1), :]], axis=1)


def pick_depth(product, depth_row, shape_z):
    ids = lax.broadcasted_iota(jnp.int32, (shape_z, depth_row.shape[1]), 0)
    hit = ids == depth_row
    count = product.shape[0] // shape_z
    return [
        jnp.sum(jnp.where(hit, product[k * shape_z : (k + 1) * shape_z], 0.0), axis=0, keepdims=True)
        for k in range(count)
    ]


def gather_columns(tables, table_ref, cell_ref, write, onehot_ref=None):
    rows, shape_z = tables[0].shape
    count = len(tables)
    for k, table in enumerate(tables):
        top, low = split(table.T)
        table_ref[0, k * shape_z : (k + 1) * shape_z, :] = top
        table_ref[1, k * shape_z : (k + 1) * shape_z, :] = low
    chunks = cell_ref.shape[0] // 2

    def step(j, carry):
        cell = wide_row(cell_ref, 2 * j)
        hot = one_hot_t(cell // shape_z, rows)
        product = jnp.dot(table_ref[0, : count * shape_z], hot, preferred_element_type=f32)
        product = product + jnp.dot(table_ref[1, : count * shape_z], hot, preferred_element_type=f32)
        for k, picked in enumerate(pick_depth(product, cell % shape_z, shape_z)):
            write(k, j, picked)
        return carry

    lax.fori_loop(0, chunks, step, 0, unroll=2)


def sample_kernel(v_ref, old_ref, cell_ref, inertia_ref, s_ref, acc_ref, table_ref):
    shape = v_ref.shape
    rows = shape[1] * shape[2]
    tables = [r[k].reshape(rows, shape[3]) for r in (v_ref, old_ref) for k in range(3)]

    def write(k, j, picked):
        ref = s_ref if k < 3 else acc_ref
        ref[k % 3, pl.ds(2 * j, 1), :] = picked[:, :LANES]
        ref[k % 3, pl.ds(2 * j + 1, 1), :] = picked[:, LANES:]

    gather_columns(tables, table_ref, cell_ref, write)
    for k in range(3):
        acc_ref[k] = inertia_ref[...] * (s_ref[k] - acc_ref[k])


def member_lookup(table, slot):
    wide = jnp.broadcast_to(table, slot.shape)
    return jnp.take_along_axis(wide, slot, axis=1)


def forces_deposit(samples, acc, slot, drag, table, cell_ref, force_ref, column_ref, field_ref, slot_ref):
    relative = [samples[k] - member_lookup(table[k : k + 1], slot) for k in range(3)]
    square = relative[0] * relative[0] + relative[1] * relative[1] + relative[2] * relative[2]
    speed = drag * jnp.sqrt(square + softening)
    for k in range(3):
        force = speed * relative[k] + acc[k]
        top = force.astype(bf16).astype(f32)
        force_ref[k] = top
        force_ref[3 + k] = force - top
    slot_ref[...] = slot
    rows, width = field_ref.shape
    shape_z = width // 6
    chunks = cell_ref.shape[0] // 2
    total0 = jnp.zeros((8, LANES), f32)
    field_ref[...] = jnp.zeros_like(field_ref)

    def step(j, total):
        cell = wide_row(cell_ref, 2 * j)
        hot = one_hot_t(cell // shape_z, rows)
        depth = one_hot_t(cell % shape_z, shape_z) > 0
        pieces = [wide_row(force_ref.at[k], 2 * j) for k in range(6)]
        for k in range(6):
            wide = jnp.broadcast_to(pieces[k].astype(bf16), depth.shape)
            column_ref[k * shape_z : (k + 1) * shape_z] = jnp.where(depth, wide, jnp.zeros_like(wide))
        field_ref[...] += lax.dot_general(
            hot, column_ref[...], (((1,), (1,)), ((), ())), preferred_element_type=f32
        )
        members = one_hot_t(wide_row(slot_ref, 2 * j), LANES)
        stack = jnp.concatenate(pieces + [jnp.zeros((2, WIDE), f32)], axis=0).astype(bf16)
        return total + lax.dot_general(
            stack, members, (((1,), (1,)), ((), ())), preferred_element_type=f32
        )

    total = lax.fori_loop(0, chunks, step, total0, unroll=2)
    total = total + pltpu.roll(total, 5, axis=0)
    half = width // 2
    return total, -(field_ref[:, :half] + field_ref[:, half:])


def shift(x, axis, by):
    n = x.shape[axis]
    if axis == x.ndim - 1 or axis == x.ndim - 2:
        moved = pltpu.roll(x, by % n, axis=axis)
        ids = lax.broadcasted_iota(jnp.int32, x.shape, axis)
        return jnp.where(ids == (0 if by > 0 else n - 1), 0.0, moved)
    zero = jnp.zeros_like(lax.slice_in_dim(x, 0, 1, axis=axis))
    if by > 0:
        return jnp.concatenate([zero, lax.slice_in_dim(x, 0, n - 1, axis=axis)], axis=axis)
    return jnp.concatenate([lax.slice_in_dim(x, 1, n, axis=axis), zero], axis=axis)


def both(x, axis):
    return shift(x, axis, 1) + shift(x, axis, -1)


def local_update(v_ref, field, l_ref, spill_ref, y_refs, own_y):
    comps, nx, ny, nz = v_ref.shape
    for c in range(comps):
        v = v_ref[c]
        w = field[:, c * nz : (c + 1) * nz].reshape(nx, ny, nz)
        w = 0.5 * w + 0.25 * both(w, 2)
        w_y = 0.5 * w + 0.25 * both(w, 1)
        w_x = 0.5 * w_y + 0.25 * both(w_y, 0)
        beside = both(v, 0) + both(v, 1) + both(v, 2)
        l_ref[c] = v + viscous * (beside - 6.0 * v) + w_x
        spill_ref[0, c] = 0.25 * w_y[0] + viscous * v[0]
        spill_ref[1, c] = 0.25 * w_y[nx - 1] + viscous * v[nx - 1]
        ends = []
        for y in (0, ny - 1):
            edge = 0.25 * w[:, y, :]
            end = 0.5 * edge + 0.25 * both(edge, 0) + viscous * v[:, y, :]
            ends.append((end, 0.25 * edge[0:1], 0.25 * edge[nx - 1 : nx]))
        even = own_y % 2 == 0
        for ref, flip in zip(y_refs, (even, jnp.logical_not(even))):
            for part, (low, high) in enumerate(zip(*ends)):
                chosen = jnp.where(flip, high, low)
                if part == 0:
                    ref[c] = chosen
                else:
                    ref[comps, 3 * (part - 1) + c : 3 * (part - 1) + c + 1, :] = chosen


def beside(even_msg, odd_msg, own, count):
    even = own % 2 == 0
    low = jnp.where(own > 0, jnp.where(even, odd_msg, even_msg), 0.0)
    high = jnp.where(own < count - 1, jnp.where(even, even_msg, odd_msg), 0.0)
    return low, high


def member_table(own, low, high, held):
    return low + pltpu.roll(own, held, axis=1) + pltpu.roll(high, 2 * held, axis=1)


def first_kernel(held, count_x, v_ref, s_ref, acc_ref, slot_ref, drag_ref, cell_ref, own_ref, even_ref, odd_ref,
                 l_ref, spill_ref, ye_ref, yo_ref, total_ref, table_ref,
                 force_ref, column_ref, field_ref, slot_copy):
    own_x = lax.axis_index("gx")
    low, high = beside(even_ref[...], odd_ref[...], own_x, count_x)
    table = member_table(own_ref[...], low, high, held)
    table_ref[...] = table
    samples = [s_ref[k] for k in range(3)]
    acc = [acc_ref[k] for k in range(3)]
    total, field = forces_deposit(samples, acc, slot_ref[...], drag_ref[...], table, cell_ref,
                                  force_ref, column_ref, field_ref, slot_copy)
    total_ref[...] = total
    local_update(v_ref, field, l_ref, spill_ref, (ye_ref, yo_ref), lax.axis_index("gy"))


def y_kernel(count_y, l_ref, spill_ref, even_ref, odd_ref, total_ref, l_out, xe_ref, xo_ref):
    comps, nx, ny, nz = l_ref.shape
    own_y = lax.axis_index("gy")
    low, high = beside(even_ref[...], odd_ref[...], own_y, count_y)
    l_out[...] = l_ref[...]
    even = lax.axis_index("gx") % 2 == 0
    ids = lax.broadcasted_iota(jnp.int32, (ny, nz), 0)
    for c in range(comps):
        l_out[c, :, 0, :] += low[c]
        l_out[c, :, ny - 1, :] += high[c]
        sides = []
        for side in range(2):
            row = 3 * side + c
            face = spill_ref[side, c]
            face = face + jnp.where(ids == 0, low[comps, row : row + 1], 0.0)
            face = face + jnp.where(ids == ny - 1, high[comps, row : row + 1], 0.0)
            sides.append(face)
        xe_ref[c] = jnp.where(even, sides[1], sides[0])
        xo_ref[c] = jnp.where(even, sides[0], sides[1])
    for ref in (xe_ref, xo_ref):
        ref[comps, 0:8, :] = total_ref[...]
        ref[comps, 8:16, :] = jnp.zeros_like(total_ref)


def second_kernel(held, count_x, s_ref, slot_ref, drag_ref, inertia_ref, cell_ref, mtable_ref, total_ref,
                  l_ref, xe_ref, xo_ref, te_ref, to_ref,
                  l_out, spill_ref, ye_ref, yo_ref, total_out, mtable_out,
                  v_ref, table_ref, sample_ref, force_ref, column_ref, field_ref, slot_copy):
    comps, nx, ny, nz = l_ref.shape
    own_x = lax.axis_index("gx")
    low, high = beside(xe_ref[...], xo_ref[...], own_x, count_x)
    v_ref[...] = l_ref[...]
    for c in range(comps):
        v_ref[c, 0] += low[c]
        v_ref[c, nx - 1] += high[c]
    second_even = own_x // 2 % 2 == 0
    low2 = jnp.where(own_x > 1, jnp.where(second_even, to_ref[...], te_ref[...]), 0.0)
    high2 = jnp.where(own_x < count_x - 2, jnp.where(second_even, te_ref[...], to_ref[...]), 0.0)
    low1, high1 = low[comps, 0:8], high[comps, 0:8]
    lane = lax.broadcasted_iota(jnp.int32, (8, LANES), 1)
    total = total_ref[...]
    total = total + pltpu.roll(low1, LANES - held, axis=1) + pltpu.roll(high1, held, axis=1)
    total = total + jnp.where(lane < held, pltpu.roll(low2, LANES - 2 * held, axis=1), 0.0)
    total = total + jnp.where(lane // held == 2, pltpu.roll(high2, 2 * held, axis=1), 0.0)
    old = mtable_ref[...]
    row = lax.broadcasted_iota(jnp.int32, (8, LANES), 0)
    table = jnp.where((row < 3) & (lane < 3 * held), old + old[3:4] * total, old)
    mtable_out[...] = table
    tables = [v_ref[k].reshape(nx * ny, nz) for k in range(comps)]

    def write(k, j, picked):
        sample_ref[k, pl.ds(2 * j, 1), :] = picked[:, :LANES]
        sample_ref[k, pl.ds(2 * j + 1, 1), :] = picked[:, LANES:]

    gather_columns(tables, table_ref, cell_ref, write)
    samples = [sample_ref[k] for k in range(3)]
    acc = [inertia_ref[...] * (samples[k] - s_ref[k]) for k in range(3)]
    total, field = forces_deposit(samples, acc, slot_ref[...], drag_ref[...], table, cell_ref,
                                  force_ref, column_ref, field_ref, slot_copy)
    total_out[...] = total
    local_update(v_ref, field, l_out, spill_ref, (ye_ref, yo_ref), lax.axis_index("gy"))


def last_kernel(held, count_x, l_ref, xe_ref, xo_ref, mtable_ref, total_ref, v_out, m_out):
    comps, nx, ny, nz = l_ref.shape
    low, high = beside(xe_ref[...], xo_ref[...], lax.axis_index("gx"), count_x)
    v_out[...] = l_ref[...]
    for c in range(comps):
        v_out[c, 0] += low[c]
        v_out[c, nx - 1] += high[c]
    total = total_ref[...] + pltpu.roll(low[comps, 0:8], LANES - held, axis=1)
    total = total + pltpu.roll(high[comps, 0:8], held, axis=1)
    table = mtable_ref[...]
    table = table + table[3:4] * total
    m_out[...] = pltpu.roll(table, LANES - held, axis=1)[0:3, :held]


def swaps(count, stride):
    even = [(i, i ^ stride) for i in range(count)]
    odd = [(i, (((i + stride) ^ stride) - stride) % count) for i in range(count)]
    return even, odd


def exchange(even_msg, odd_msg, axis, stride=1):
    even, odd = swaps(lax.axis_size(axis), stride)
    return lax.ppermute(even_msg, axis, even), lax.ppermute(odd_msg, axis, odd)


def per_device(velocity, velocity_old, station_cell, station_member, drag_coef, inertia_coef, member_velocity,
               member_inv_mass):
    count_x, count_y = lax.axis_size("gx"), lax.axis_size("gy")
    held = member_velocity.shape[1]
    comps, nx, ny, nz = velocity.shape
    rows = nx * ny
    stations = station_cell.shape[0]
    lines = (stations // LANES, LANES)
    cell = station_cell.reshape(lines)
    drag = drag_coef.reshape(lines)
    inertia = inertia_coef.reshape(lines)
    member = station_member.reshape(lines)
    offset = member // held // count_y - lax.axis_index("gx") + 1
    slot = offset * held + member % held
    own = jnp.concatenate([member_velocity, member_inv_mass[None]], axis=0)
    own = jnp.pad(own, ((0, 4), (0, LANES - held)))
    own_even, own_odd = exchange(own, own, "gx")

    def gather_flops(c):
        return 4 * c * nz * rows * stations

    table = lambda c: pltpu.VMEM((2, c * nz, rows), bf16)
    work = [
        pltpu.VMEM((6,) + lines, f32),
        pltpu.VMEM((6 * nz, WIDE), bf16),
        pltpu.VMEM((rows, 6 * nz), f32),
        pltpu.VMEM(lines, jnp.int32),
    ]
    face = (comps + 1, nx, nz)
    grid = velocity.shape
    samples, acc = call(
        sample_kernel, [(3,) + lines] * 2, [table(6)], gather_flops(6), 1 << 21
    )(velocity, velocity_old, cell, inertia)
    parts = [grid, (2, comps, ny, nz), face, face, (8, LANES), (8, LANES)]
    local, spill, y_even, y_odd, total, mtable = call(
        functools.partial(first_kernel, held, count_x), parts, work, gather_flops(3), 1 << 21
    )(velocity, samples, acc, slot, drag, cell, own, own_even, own_odd)

    def y_stage(local, spill, y_even, y_odd, total):
        y_even, y_odd = exchange(y_even, y_odd, "gy")
        return call(functools.partial(y_kernel, count_y), [grid, face, face], (), 1 << 20, 1 << 19)(
            local, spill, y_even, y_odd, total
        )

    second_even, second_odd = exchange(total, total, "gx", 2)
    local, x_even, x_odd = y_stage(local, spill, y_even, y_odd, total)
    x_even, x_odd = exchange(x_even, x_odd, "gx")
    local, spill, y_even, y_odd, total, mtable = call(
        functools.partial(second_kernel, held, count_x),
        parts,
        [pltpu.VMEM(grid, f32), table(3), pltpu.VMEM((3,) + lines, f32)] + work,
        gather_flops(6),
        1 << 21,
    )(samples, slot, drag, inertia, cell, mtable, total, local, x_even, x_odd, second_even, second_odd)
    local, x_even, x_odd = y_stage(local, spill, y_even, y_odd, total)
    x_even, x_odd = exchange(x_even, x_odd, "gx")
    velocity, members = call(functools.partial(last_kernel, held, count_x), [grid, (3, held)], (), 1 << 20, 1 << 20)(
        local, x_even, x_odd, mtable, total
    )
    return velocity, members


def solution(mesh):
    return jax.shard_map(
        per_device,
        mesh=mesh,
        in_specs=(
            P(None, "gx", "gy", None),
            P(None, "gx", "gy", None),
            P(("gx", "gy")),
            P(("gx", "gy"), None),
            P(("gx", "gy")),
            P(("gx", "gy")),
            P(None, ("gx", "gy")),
            P(("gx", "gy")),
        ),
        out_specs=(P(None, "gx", "gy", None), P(None, ("gx", "gy"))),
        check_vma=False,
    )
```

time: 659 us -> 56 us (0.08)
  local copies, waits for them, and re-layouts: 464 us -> 4 us
  other arithmetic: 106 us -> 0.73 us
  starting transfers between devices: 71 us -> 17.2 us
  Pallas kernels: 0 us -> 19.5 us
    gather x16 -> x0, local copies, waits for them, and re-layouts: 362 us -> none  [the longest x13 299 us: per_device(): leading = jnp.searchsorted(sorted_members, sorted_members, side='left')]
    scatter-add x2 -> x0, other arithmetic: 82.3 us -> none  [deposit(): jnp.zeros((3, cell_count), jnp.float32).at[:, station_cell]]
    ppermute x24 -> x12, starting transfers between devices: 71 us -> 17.2 us  [the longest x6 12.6 us: exchange(): lax.ppermute(odd_msg, axis, odd)]
    scatter x3 -> x0, local copies, waits for them, and re-layouts: 39.1 us -> none  [the longest x2 23.6 us: per_device(): jnp.zeros((8, 3 * slot_count), jnp.float32).at[:, slot_index].set(payload)]
    concatenate x5 -> x0, local copies, waits for them, and re-layouts: 21.4 us -> none  [the longest x2 17.5 us: sample_both(): both = jnp.concatenate([velocity, velocity_old], axis=0)]
    reshape x2 -> x0, local copies, waits for them, and re-layouts: 20 us -> none  [per_device(): point_force = point_force.reshape(3, shape_x, shape_y, shape_z)]
    pallas_call x0 -> x6, Pallas kernels: none -> 19.5 us  [the longest x1 8.37 us: per_device(): call(functools.partial(second_kernel, held, count_x), parts, [pltpu.VMEM(...]
    select_n x28 -> x0, other arithmetic: 7.57 us -> none  [the longest x2 7.26 us: sample_both(): values = jnp.take(flat_cells, station_cell, axis=1)]
  transfers between devices with their start and end apart: 24 -> 12, of which waited for: 6 -> 7; matrix products, arithmetic and copies ran while one was open for 18% -> 0% of each run, Pallas kernels for 0% -> 10%
where the time goes in v1:
time: 56 us; the launch traced here: 55.6 us
  Pallas kernels  19.5 us (35%)
  starting transfers between devices  17.2 us (31%)
  waiting for transfers between devices  13.4 us (24%)
  local copies, waits for them, and re-layouts  4 us (7%)
  between operations  0.74 us (1%)
  other arithmetic  0.73 us (1%)
    ppermute x6, waiting for transfers between devices, exchange(): lax.ppermute(odd_msg, axis, odd)  12.6 us
    ppermute x6, starting transfers between devices, exchange(): lax.ppermute(odd_msg, axis, odd)  12.6 us
    pallas_call x1, Pallas kernels, per_device(): call(functools.partial(second_kernel, held, count_x), parts, [pltpu.VMEM(...  8.37 us
    pallas_call x1, Pallas kernels, per_device(): call(sample_kernel, [(3,) + lines] * 2, [table(6)], gather_flops(6), 1 <<...  5.3 us
    pallas_call x1, Pallas kernels, per_device(): call(functools.partial(first_kernel, held, count_x), parts, work, gather_...  4.85 us
    ppermute x6, starting transfers between devices, exchange(): lax.ppermute(even_msg, axis, even)  4.59 us
    unnamed x14, local copies, waits for them, and re-layouts  4 us
  transfers between devices with their start and end apart: 12, of which 7 were waited for; matrix products, arithmetic and copies ran while one was open for 0% of the time, Pallas kernels for 10%

profile of v1, /device:TPU:0, one launch (start us, length us, event | category | flops | bytes accessed | tf_op | source)
XLA Modules:
  0.0 55.6 jit_solution(9319926416226533386)
XLA Ops:
  0.6 0.0 copy-start.6
  0.6 0.0 copy-start.2
  0.7 0.6 %copy-done.6 = f32[16]{0:T(128)S(1)} copy-done((f32[16]{0:T(128)S(1)}, f32[16]{0:T(128)}, u32[]{:S(2)}) %copy-start.6) | copy-done | bytes 88
  1.3 0.7 %select_maximum_fusion.own_ref = f32[8,128]{1,0:T(8,128)S(1)} fusion(f32[1,16]{1,0:T(1,128)S(1)} %bitcast.13, f32[3,16]{1,0:T(4,128)} %param.14), kind=kLoop, calls=%fused_computation.19 | loop fusion | flops 8192 | bytes 4352 | tf_op jit(solution)/shard_map/concatenate | solution.py:307
  2.0 6.0 %collective-permute-start.1 = (f32[8,128]{1,0:T(8,128)S(1)}, f32[8,128]{1,0:T(8,128)S(1)}, u32[]{:S(2)}, u32[]{:S(2)}) collective-permute-start(f32[8,128]{1,0:T(8,128)S(1)} %select_maximum_fusion.own_ref), channel_id=1, source_target_pairs={{0,28},{4,8},{8,4},{12,16},{16,12},{20,24},{24,20},{28,0},{1,29},{... | collective-permute-start | bytes 12296 | tf_op jit(solution)/shard_map/ppermute | solution.py:290
  8.0 0.0 collective-permute-start
  8.0 0.0 copy-done.2
  8.0 0.0 copy-start
  8.0 1.0 %copy-done = f32[3,16,16,128]{3,2,1,0:T(8,128)S(1)} copy-done((f32[3,16,16,128]{3,2,1,0:T(8,128)S(1)}, f32[3,16,16,128]{3,2,1,0:T(8,128)}, u32[]{:S(2)}) %copy-start) | copy-done | bytes 393240
  9.0 0.0 copy-start.1
  9.0 1.0 %copy-done.1 = f32[3,16,16,128]{3,2,1,0:T(8,128)S(1)} copy-done((f32[3,16,16,128]{3,2,1,0:T(8,128)S(1)}, f32[3,16,16,128]{3,2,1,0:T(8,128)}, u32[]{:S(2)}) %copy-start.1) | copy-done | bytes 393240
  10.0 0.0 copy-start.3
  10.0 0.7 %copy-done.3 = f32[4096]{0:T(1024)S(1)} copy-done((f32[4096]{0:T(1024)S(1)}, f32[4096]{0:T(1024)}, u32[]{:S(2)}) %copy-start.3) | copy-done | bytes 16408
  10.7 0.0 copy-start.5
  10.7 5.3 %shard_map.95 = (f32[3,32,128]{2,1,0:T(8,128)S(1)}, f32[3,32,128]{2,1,0:T(8,128)S(1)}) custom-call(f32[3,16,16,128]{3,2,1,0:T(8,128)S(1)} %copy-done.1, f32[3,16,16,128]{3,2,1,0:T(8,128)S(1)} %copy-done, s32[32,128]{1,0:T(8,128)S(1)} %bitcast.5, f32[32,128]{1,0:T(8,128)S(1)} %bitcast.8), custom_call_target="tpu_custom_call" | custom-call | flops 3221225472 | bytes 2097152 | tf_op jit(solution)/shard_map/pallas_call | solution.py:323
  16.0 0.0 copy-done.5
  16.0 0.0 copy-start.4
  16.0 0.0 collective-permute-done.1.odd_ref
  16.1 0.0 collective-permute-done.even_ref
  16.1 0.6 %copy-done.4 = f32[4096]{0:T(1024)S(1)} copy-done((f32[4096]{0:T(1024)S(1)}, f32[4096]{0:T(1024)}, u32[]{:S(2)}) %copy-start.4) | copy-done | bytes 16408
  16.7 4.9 %shard_map.96 = (f32[3,16,16,128]{3,2,1,0:T(8,128)S(1)}, f32[2,3,16,128]{3,2,1,0:T(8,128)S(1)}, f32[4,16,128]{2,1,0:T(8,128)S(1)}, f32[4,16,128]{2,1,0:T(8,128)S...) custom-call(f32[3,16,16,128]{3,2,1,0:T(8,128)S(1)} %copy-done.1, f32[3,32,128]{2,1,0:T(8,128)S(1)} %get-tuple-element.22.s_ref, ...), custom_call_target="tpu_custom_call" | custom-call | flops 1610612736 | bytes 2097152 | tf_op jit(solution)/shard_map/pallas_call | solution.py:327
  21.6 0.1 collective-permute-start.2
  21.6 1.6 %collective-permute-start.3 = (f32[4,16,128]{2,1,0:T(8,128)S(1)}, f32[4,16,128]{2,1,0:T(8,128)S(1)}, u32[]{:S(2)}, u32[]{:S(2)}) collective-permute-start(f32[4,16,128]{2,1,0:T(8,128)S(1)} %get-tuple-element.29), channel_id=1, source_target_pairs={{0,3},{1,2},{2,1},{3,0},{4,7},{5,6},{6,5},{7,4},{8,11},{9,10},{10,... | collective-permute-start | bytes 98312 | tf_op jit(solution)/shard_map/ppermute | solution.py:290
  23.3 0.0 collective-permute-done.2.even_ref
  23.3 1.8 %collective-permute-done.3.odd_ref = f32[4,16,128]{2,1,0:T(8,128)S(1)} collective-permute-done((f32[4,16,128]{2,1,0:T(8,128)S(1)}, f32[4,16,128]{2,1,0:T(8,128)S(1)}, u32[]{:S(2)}, u32[]{:S(2)}) %collective-permute-start.3) | collective-permute-done | bytes 32800 | tf_op jit(solution)/shard_map/ppermute | solution.py:290
  25.1 0.1 shard_map.97
  25.1 2.1 %collective-permute-start.4 = (f32[4,16,128]{2,1,0:T(8,128)S(1)}, f32[4,16,128]{2,1,0:T(8,128)S(1)}, u32[]{:S(2)}, u32[]{:S(2)}) collective-permute-start(f32[4,16,128]{2,1,0:T(8,128)S(1)} %get-tuple-element.31), channel_id=1, source_target_pairs={{0,4},{4,0},{8,12},{12,8},{16,20},{20,16},{24,28},{28,24},{1,5},{5... | collective-permute-start | bytes 98312 | tf_op jit(solution)/shard_map/ppermute | solution.py:290
  27.2 0.1 collective-permute-start.5
  27.3 1.9 %collective-permute-start.7 = (f32[8,128]{1,0:T(8,128)S(1)}, f32[8,128]{1,0:T(8,128)S(1)}, u32[]{:S(2)}, u32[]{:S(2)}) collective-permute-start(f32[8,128]{1,0:T(8,128)S(1)} %get-tuple-element.25.total_ref), channel_id=1, source_target_pairs={{0,24},{4,28},{8,16},{12,20},{16,8},{20,12},{24,0},{28,4},{1,25},{... | collective-permute-start | bytes 12296 | tf_op jit(solution)/shard_map/ppermute | solution.py:290
  29.2 0.0 collective-permute-start.6
  29.2 3.5 %collective-permute-done.7.to_ref = f32[8,128]{1,0:T(8,128)S(1)} collective-permute-done((f32[8,128]{1,0:T(8,128)S(1)}, f32[8,128]{1,0:T(8,128)S(1)}, u32[]{:S(2)}, u32[]{:S(2)}) %collective-permute-start.7) | collective-permute-done | bytes 4128 | tf_op jit(solution)/shard_map/ppermute | solution.py:290
  32.7 0.1 collective-permute-done.6.te_ref
  32.8 0.0 collective-permute-done.4.xe_ref
  32.8 1.0 %collective-permute-done.5.xo_ref = f32[4,16,128]{2,1,0:T(8,128)S(1)} collective-permute-done((f32[4,16,128]{2,1,0:T(8,128)S(1)}, f32[4,16,128]{2,1,0:T(8,128)S(1)}, u32[]{:S(2)}, u32[]{:S(2)}) %collective-permute-start.5) | collective-permute-done | bytes 32800 | tf_op jit(solution)/shard_map/ppermute | solution.py:290
  33.8 8.4 %shard_map.98 = (f32[3,16,16,128]{3,2,1,0:T(8,128)S(1)}, f32[2,3,16,128]{3,2,1,0:T(8,128)S(1)}, f32[4,16,128]{2,1,0:T(8,128)S(1)}, f32[4,16,128]{2,1,0:T(8,128)S...) custom-call(f32[3,32,128]{2,1,0:T(8,128)S(1)} %get-tuple-element.22.s_ref, s32[32,128]{1,0:T(8,128)S(1)} %fusion.4.slot_ref, ...), custom_call_target="tpu_custom_call" | custom-call | flops 3221225472 | bytes 2097152 | tf_op jit(solution)/shard_map/pallas_call | solution.py:340
  42.2 0.1 collective-permute-start.8
  42.3 1.6 %collective-permute-start.9 = (f32[4,16,128]{2,1,0:T(8,128)S(1)}, f32[4,16,128]{2,1,0:T(8,128)S(1)}, u32[]{:S(2)}, u32[]{:S(2)}) collective-permute-start(f32[4,16,128]{2,1,0:T(8,128)S(1)} %get-tuple-element.36), channel_id=1, source_target_pairs={{0,3},{1,2},{2,1},{3,0},{4,7},{5,6},{6,5},{7,4},{8,11},{9,10},{10,... | collective-permute-start | bytes 98312 | tf_op jit(solution)/shard_map/ppermute | solution.py:290
  43.9 0.0 collective-permute-done.8.even_ref
  43.9 1.8 %collective-permute-done.9.odd_ref = f32[4,16,128]{2,1,0:T(8,128)S(1)} collective-permute-done((f32[4,16,128]{2,1,0:T(8,128)S(1)}, f32[4,16,128]{2,1,0:T(8,128)S(1)}, u32[]{:S(2)}, u32[]{:S(2)}) %collective-permute-start.9) | collective-permute-done | bytes 32800 | tf_op jit(solution)/shard_map/ppermute | solution.py:290
  45.7 0.1 shard_map.99
  45.8 2.4 %collective-permute-start.10 = (f32[4,16,128]{2,1,0:T(8,128)S(1)}, f32[4,16,128]{2,1,0:T(8,128)S(1)}, u32[]{:S(2)}, u32[]{:S(2)}) collective-permute-start(f32[4,16,128]{2,1,0:T(8,128)S(1)} %get-tuple-element.39), channel_id=1, source_target_pairs={{0,4},{4,0},{8,12},{12,8},{16,20},{20,16},{24,28},{28,24},{1,5},{5... | collective-permute-start | bytes 98312 | tf_op jit(solution)/shard_map/ppermute | solution.py:290
  48.2 1.3 %collective-permute-start.11 = (f32[4,16,128]{2,1,0:T(8,128)S(1)}, f32[4,16,128]{2,1,0:T(8,128)S(1)}, u32[]{:S(2)}, u32[]{:S(2)}) collective-permute-start(f32[4,16,128]{2,1,0:T(8,128)S(1)} %get-tuple-element.40), channel_id=1, source_target_pairs={{0,28},{4,8},{8,4},{12,16},{16,12},{20,24},{24,20},{28,0},{1,29},{... | collective-permute-start | bytes 98312 | tf_op jit(solution)/shard_map/ppermute | solution.py:290
  49.5 0.7 %collective-permute-done.10.xe_ref = f32[4,16,128]{2,1,0:T(8,128)S(1)} collective-permute-done((f32[4,16,128]{2,1,0:T(8,128)S(1)}, f32[4,16,128]{2,1,0:T(8,128)S(1)}, u32[]{:S(2)}, u32[]{:S(2)}) %collective-permute-start.10) | collective-permute-done | bytes 32800 | tf_op jit(solution)/shard_map/ppermute | solution.py:290
  50.2 4.6 %collective-permute-done.11.xo_ref = f32[4,16,128]{2,1,0:T(8,128)S(1)} collective-permute-done((f32[4,16,128]{2,1,0:T(8,128)S(1)}, f32[4,16,128]{2,1,0:T(8,128)S(1)}, u32[]{:S(2)}, u32[]{:S(2)}) %collective-permute-start.11) | collective-permute-done | bytes 32800 | tf_op jit(solution)/shard_map/ppermute | solution.py:290
  54.8 0.8 %shard_map.100 = (f32[3,16,16,128]{3,2,1,0:T(8,128)}, f32[3,16]{1,0:T(4,128)}) custom-call(f32[3,16,16,128]{3,2,1,0:T(8,128)S(1)} %get-tuple-element.38.l_ref, f32[4,16,128]{2,1,0:T(8,128)S(1)} %collective-permute-done.10.xe_ref, f32[4,16,128]{2,1,0:T(8,128)S(1)} %collective-permute-done.11.xo_ref, f32[8,128]{1,0:T(8,128)S(1)} %get-tuple-element.41.mtable_ref, ...), custom_call_target="tpu_custom_call" | custom-call | flops 1048576 | bytes 1048576 | tf_op jit(solution)/shard_map/pallas_call | solution.py:349
  (1 shorter events, 0.0 us)
Async XLA Ops:
  0.6 0.7 %copy-start.6 = (f32[16]{0:T(128)S(1)}, f32[16]{0:T(128)}, u32[]{:S(2)}) copy-start(f32[16]{0:T(128)} %param.15) | copy-start | bytes 196
  0.6 7.3 %copy-start.2 = (s32[4096]{0:T(1024)S(1)}, s32[4096]{0:T(1024)}, u32[]{:S(2)}) copy-start(s32[4096]{0:T(1024)} %param.10) | copy-start | bytes 49156
  2.0 14.1 %collective-permute-start.1 = (f32[8,128]{1,0:T(8,128)S(1)}, f32[8,128]{1,0:T(8,128)S(1)}, u32[]{:S(2)}, u32[]{:S(2)}) collective-permute-start(f32[8,128]{1,0:T(8,128)S(1)} %select_maximum_fusion.own_ref), channel_id=1, source_target_pairs={{0,28},{4,8},{8,4},{12,16},{16,12},{20,24},{24,20},{28,0},{1,29},{... | collective-permute-start | bytes 12296 | tf_op jit(solution)/shard_map/ppermute | solution.py:290
  8.0 8.1 %collective-permute-start = (f32[8,128]{1,0:T(8,128)S(1)}, f32[8,128]{1,0:T(8,128)S(1)}, u32[]{:S(2)}, u32[]{:S(2)}) collective-permute-start(f32[8,128]{1,0:T(8,128)S(1)} %select_maximum_fusion.own_ref), channel_id=1, source_target_pairs={{0,4},{4,0},{8,12},{12,8},{16,20},{20,16},{24,28},{28,24},{1,5},{5... | collective-permute-start | bytes 12296 | tf_op jit(solution)/shard_map/ppermute | solution.py:290
  8.0 1.0 %copy-start = (f32[3,16,16,128]{3,2,1,0:T(8,128)S(1)}, f32[3,16,16,128]{3,2,1,0:T(8,128)}, u32[]{:S(2)}) copy-start(f32[3,16,16,128]{3,2,1,0:T(8,128)} %old_ref.1) | copy-start | bytes 1179652
  9.0 1.0 %copy-start.1 = (f32[3,16,16,128]{3,2,1,0:T(8,128)S(1)}, f32[3,16,16,128]{3,2,1,0:T(8,128)}, u32[]{:S(2)}) copy-start(f32[3,16,16,128]{3,2,1,0:T(8,128)} %v_ref.3) | copy-start | bytes 1179652
  10.0 0.7 %copy-start.3 = (f32[4096]{0:T(1024)S(1)}, f32[4096]{0:T(1024)}, u32[]{:S(2)}) copy-start(f32[4096]{0:T(1024)} %param.13) | copy-start | bytes 49156
  10.7 5.3 %copy-start.5 = (s32[4096,1]{0,1:T(1,128)S(1)}, s32[4096,1]{0,1:T(1,128)}, u32[]{:S(2)}) copy-start(s32[4096,1]{0,1:T(1,128)} %param.11) | copy-start | bytes 49156
  16.0 0.7 %copy-start.4 = (f32[4096]{0:T(1024)S(1)}, f32[4096]{0:T(1024)}, u32[]{:S(2)}) copy-start(f32[4096]{0:T(1024)} %param.12) | copy-start | bytes 49156
  21.6 1.7 %collective-permute-start.2 = (f32[4,16,128]{2,1,0:T(8,128)S(1)}, f32[4,16,128]{2,1,0:T(8,128)S(1)}, u32[]{:S(2)}, u32[]{:S(2)}) collective-permute-start(f32[4,16,128]{2,1,0:T(8,128)S(1)} %get-tuple-element.28), channel_id=1, source_target_pairs={{0,1},{1,0},{2,3},{3,2},{4,5},{5,4},{6,7},{7,6},{8,9},{9,8},{10,11... | collective-permute-start | bytes 98312 | tf_op jit(solution)/shard_map/ppermute | solution.py:290
  21.6 3.4 %collective-permute-start.3 = (f32[4,16,128]{2,1,0:T(8,128)S(1)}, f32[4,16,128]{2,1,0:T(8,128)S(1)}, u32[]{:S(2)}, u32[]{:S(2)}) collective-permute-start(f32[4,16,128]{2,1,0:T(8,128)S(1)} %get-tuple-element.29), channel_id=1, source_target_pairs={{0,3},{1,2},{2,1},{3,0},{4,7},{5,6},{6,5},{7,4},{8,11},{9,10},{10,... | collective-permute-start | bytes 98312 | tf_op jit(solution)/shard_map/ppermute | solution.py:290
  25.1 7.7 %collective-permute-start.4 = (f32[4,16,128]{2,1,0:T(8,128)S(1)}, f32[4,16,128]{2,1,0:T(8,128)S(1)}, u32[]{:S(2)}, u32[]{:S(2)}) collective-permute-start(f32[4,16,128]{2,1,0:T(8,128)S(1)} %get-tuple-element.31), channel_id=1, source_target_pairs={{0,4},{4,0},{8,12},{12,8},{16,20},{20,16},{24,28},{28,24},{1,5},{5... | collective-permute-start | bytes 98312 | tf_op jit(solution)/shard_map/ppermute | solution.py:290
  27.2 6.6 %collective-permute-start.5 = (f32[4,16,128]{2,1,0:T(8,128)S(1)}, f32[4,16,128]{2,1,0:T(8,128)S(1)}, u32[]{:S(2)}, u32[]{:S(2)}) collective-permute-start(f32[4,16,128]{2,1,0:T(8,128)S(1)} %get-tuple-element.32), channel_id=1, source_target_pairs={{0,28},{4,8},{8,4},{12,16},{16,12},{20,24},{24,20},{28,0},{1,29},{... | collective-permute-start | bytes 98312 | tf_op jit(solution)/shard_map/ppermute | solution.py:290
  27.3 5.4 %collective-permute-start.7 = (f32[8,128]{1,0:T(8,128)S(1)}, f32[8,128]{1,0:T(8,128)S(1)}, u32[]{:S(2)}, u32[]{:S(2)}) collective-permute-start(f32[8,128]{1,0:T(8,128)S(1)} %get-tuple-element.25.total_ref), channel_id=1, source_target_pairs={{0,24},{4,28},{8,16},{12,20},{16,8},{20,12},{24,0},{28,4},{1,25},{... | collective-permute-start | bytes 12296 | tf_op jit(solution)/shard_map/ppermute | solution.py:290
  29.2 3.6 %collective-permute-start.6 = (f32[8,128]{1,0:T(8,128)S(1)}, f32[8,128]{1,0:T(8,128)S(1)}, u32[]{:S(2)}, u32[]{:S(2)}) collective-permute-start(f32[8,128]{1,0:T(8,128)S(1)} %get-tuple-element.25.total_ref), channel_id=1, source_target_pairs={{0,8},{4,12},{8,0},{12,4},{16,24},{20,28},{24,16},{28,20},{1,9},{5... | collective-permute-start | bytes 12296 | tf_op jit(solution)/shard_map/ppermute | solution.py:290
  42.2 1.7 %collective-permute-start.8 = (f32[4,16,128]{2,1,0:T(8,128)S(1)}, f32[4,16,128]{2,1,0:T(8,128)S(1)}, u32[]{:S(2)}, u32[]{:S(2)}) collective-permute-start(f32[4,16,128]{2,1,0:T(8,128)S(1)} %get-tuple-element.35), channel_id=1, source_target_pairs={{0,1},{1,0},{2,3},{3,2},{4,5},{5,4},{6,7},{7,6},{8,9},{9,8},{10,11... | collective-permute-start | bytes 98312 | tf_op jit(solution)/shard_map/ppermute | solution.py:290
  42.3 3.4 %collective-permute-start.9 = (f32[4,16,128]{2,1,0:T(8,128)S(1)}, f32[4,16,128]{2,1,0:T(8,128)S(1)}, u32[]{:S(2)}, u32[]{:S(2)}) collective-permute-start(f32[4,16,128]{2,1,0:T(8,128)S(1)} %get-tuple-element.36), channel_id=1, source_target_pairs={{0,3},{1,2},{2,1},{3,0},{4,7},{5,6},{6,5},{7,4},{8,11},{9,10},{10,... | collective-permute-start | bytes 98312 | tf_op jit(solution)/shard_map/ppermute | solution.py:290
  45.8 4.4 %collective-permute-start.10 = (f32[4,16,128]{2,1,0:T(8,128)S(1)}, f32[4,16,128]{2,1,0:T(8,128)S(1)}, u32[]{:S(2)}, u32[]{:S(2)}) collective-permute-start(f32[4,16,128]{2,1,0:T(8,128)S(1)} %get-tuple-element.39), channel_id=1, source_target_pairs={{0,4},{4,0},{8,12},{12,8},{16,20},{20,16},{24,28},{28,24},{1,5},{5... | collective-permute-start | bytes 98312 | tf_op jit(solution)/shard_map/ppermute | solution.py:290
  48.2 6.6 %collective-permute-start.11 = (f32[4,16,128]{2,1,0:T(8,128)S(1)}, f32[4,16,128]{2,1,0:T(8,128)S(1)}, u32[]{:S(2)}, u32[]{:S(2)}) collective-permute-start(f32[4,16,128]{2,1,0:T(8,128)S(1)} %get-tuple-element.40), channel_id=1, source_target_pairs={{0,28},{4,8},{8,4},{12,16},{16,12},{20,24},{24,20},{28,0},{1,29},{... | collective-permute-start | bytes 98312 | tf_op jit(solution)/shard_map/ppermute | solution.py:290

commit v2 on v0

v2 whole, which is shorter than its diff:
```python
import functools

import jax
import jax.numpy as jnp
from jax import lax
from jax.experimental import pallas as pl
from jax.experimental.pallas import tpu as pltpu
from jax.sharding import PartitionSpec as P

STEPS = 2
LANES = 128
WIDE = 256

viscous = 0.125
softening = 0.01

f32 = jnp.float32
i32 = jnp.int32
bf16 = jnp.bfloat16
HBM = pl.BlockSpec(memory_space=pltpu.HBM)
NT = (((1,), (1,)), ((), ()))


def call(name, body, ins, outs, scratch=(), in_hbm=(), out_hbm=(), flops=0, size=1 << 18, aliases=None):
    whole = pl.BlockSpec(memory_space=pltpu.VMEM)
    ins = [pltpu.with_memory_space_constraint(x, pltpu.HBM) if k in in_hbm else x for k, x in enumerate(ins)]
    outs = [pltpu.HBM(x.shape, x.dtype) if k in out_hbm else x for k, x in enumerate(outs)]
    return pl.pallas_call(
        body,
        name=name,
        out_shape=outs,
        in_specs=[HBM if k in in_hbm else whole for k in range(len(ins))],
        out_specs=[HBM if k in out_hbm else whole for k in range(len(outs))],
        scratch_shapes=list(scratch),
        input_output_aliases=aliases or {},
        compiler_params=pltpu.CompilerParams(vmem_limit_bytes=24 << 20),
        cost_estimate=pl.CostEstimate(flops=flops, bytes_accessed=size, transcendentals=0),
    )(*ins)


def real(*shape):
    return jax.ShapeDtypeStruct(shape, f32)


def split(x):
    top = x.astype(bf16)
    return top, (x - top.astype(f32)).astype(bf16)


def hot_rows(index, count):
    ids = lax.broadcasted_iota(i32, (count, index.shape[1]), 0).astype(f32).astype(bf16)
    wide = jnp.broadcast_to(index.astype(f32).astype(bf16), ids.shape)
    return jnp.where(ids == wide, jnp.ones_like(wide), jnp.zeros_like(wide))


def wide_row(ref, j):
    return jnp.concatenate([ref[2 * j : 2 * j + 1, :], ref[2 * j + 1 : 2 * j + 2, :]], axis=1)


def store_row(ref, k, j, row):
    ref[k, 2 * j : 2 * j + 1, :] = row[:, :LANES]
    ref[k, 2 * j + 1 : 2 * j + 2, :] = row[:, LANES:]


def pick(product, depth_row, count):
    z = product.shape[0] // count
    hit = lax.broadcasted_iota(i32, (z, depth_row.shape[1]), 0) == depth_row
    return [
        jnp.sum(jnp.where(hit, product[k * z : (k + 1) * z], 0.0), axis=0, keepdims=True) for k in range(count)
    ]


def gather(fields, table_ref, row_ref, depth_ref, out_ref):
    rows, z = fields[0].shape
    count = len(fields)
    for k, field in enumerate(fields):
        table_ref[0, k * z : (k + 1) * z, :], table_ref[1, k * z : (k + 1) * z, :] = split(field.T)
    for j in range(row_ref.shape[0] // 2):
        hot = hot_rows(wide_row(row_ref, j), rows)
        product = jnp.dot(table_ref[0], hot, preferred_element_type=f32)
        product = product + jnp.dot(table_ref[1], hot, preferred_element_type=f32)
        for k, row in enumerate(pick(product, wide_row(depth_ref, j), count)):
            store_row(out_ref, k, j, row)


def columns(ref, force_ref, depth_row, z, j, groups):
    hit = hot_rows(depth_row, z) > 0
    for c in range(3):
        for p, piece in enumerate(split(wide_row(force_ref.at[c], j))):
            wide = jnp.broadcast_to(piece, hit.shape)
            at = (p * groups + c) * z
            ref[at : at + z, :] = jnp.where(hit, wide, jnp.zeros_like(wide))


def moved(x, axis, by):
    n = x.shape[axis]
    if axis >= x.ndim - 2:
        ids = lax.broadcasted_iota(i32, x.shape, axis)
        return jnp.where(ids == (0 if by > 0 else n - 1), 0.0, pltpu.roll(x, by % n, axis=axis))
    zero = jnp.zeros_like(lax.slice_in_dim(x, 0, 1, axis=axis))
    if by > 0:
        return jnp.concatenate([zero, lax.slice_in_dim(x, 0, n - 1, axis=axis)], axis=axis)
    return jnp.concatenate([lax.slice_in_dim(x, 1, n, axis=axis), zero], axis=axis)


def both(x, axis):
    return moved(x, axis, 1) + moved(x, axis, -1)


def smooth(x, axis):
    return 0.5 * x + 0.25 * both(x, axis)


def beside(even_msg, odd_msg, own, count):
    even = own % 2 == 0
    low = jnp.where(own > 0, jnp.where(even, odd_msg, even_msg), 0.0)
    high = jnp.where(own < count - 1, jnp.where(even, even_msg, odd_msg), 0.0)
    return low, high


def add_y(c, face_low, face_high, ref):
    ny = ref.shape[2]
    ref[c, :, 0, :] += face_low[c]
    ref[c, :, ny - 1, :] += face_high[c]


def edges(v_ref, force_ref, key_ref, low_ref, col_ref, acc_ref, spill_ref, y_refs):
    comps, nx, ny, nz = v_ref.shape
    ring = 2 * (nx + ny)
    parts = WIDE // ring
    z = nz // parts
    col_ref[...] = jnp.zeros_like(col_ref)
    for j in range(key_ref.shape[0] // 2):
        hot = hot_rows(wide_row(key_ref, j), WIDE)
        columns(col_ref, force_ref, wide_row(low_ref, j), z, j, 4)
        part = lax.dot_general(hot, col_ref[...], NT, preferred_element_type=f32)
        acc_ref[...] = part if j == 0 else acc_ref[...] + part
    found = -(acc_ref[:, :LANES] + acc_ref[:, LANES:])
    lane = lax.broadcasted_iota(i32, (ring, LANES), 1) // z
    yid = lax.broadcasted_iota(i32, (ny, nz), 0)
    even = lax.axis_index("gy") % 2 == 0
    for c in range(comps):
        w = jnp.zeros((ring, nz), f32)
        for h in range(parts):
            block = found[h * ring : (h + 1) * ring]
            by = (h - c) * z % LANES
            block = pltpu.roll(block, by, axis=1) if by else block
            w = jnp.where(lane == h, block, w)
        w = smooth(w, 1)
        y_ends = (w[:nx], w[nx : 2 * nx])
        for side, x in ((0, 0), (1, nx - 1)):
            face = w[2 * nx + side * ny : 2 * nx + (side + 1) * ny]
            face = jnp.where(yid == 0, y_ends[0][x : x + 1], face)
            face = jnp.where(yid == ny - 1, y_ends[1][x : x + 1], face)
            spill_ref[side, c] = 0.25 * smooth(face, 0) + viscous * v_ref[c, x]
        low, high = [
            (smooth(0.25 * w_y, 0) + viscous * v_ref[c, :, y, :], 0.0625 * w_y[0:1], 0.0625 * w_y[nx - 1 : nx])
            for y, w_y in zip((0, ny - 1), y_ends)
        ]
        for ref, flip in zip(y_refs, (even, jnp.logical_not(even))):
            ref[c] = jnp.where(flip, high[0], low[0])
            for side in range(2):
                at = 3 * side + c
                ref[comps, at : at + 1, :] = jnp.where(flip, high[1 + side], low[1 + side])


def forces(samples, acc, slot, drag, table, force_ref):
    relative = [
        samples[c] - jnp.take_along_axis(jnp.broadcast_to(table[c : c + 1], slot.shape), slot, axis=1)
        for c in range(3)
    ]
    square = relative[0] * relative[0] + relative[1] * relative[1] + relative[2] * relative[2]
    speed = drag * jnp.sqrt(square + softening)
    for c in range(3):
        force_ref[c] = speed * relative[c] + acc[c]


def totals_kernel(force_ref, slot_ref, after_ref, total_ref):
    total = jnp.zeros((8, LANES), f32)
    for j in range(slot_ref.shape[0] // 2):
        rows = [wide_row(force_ref.at[c], j) for c in range(3)]
        tops = [r.astype(bf16).astype(f32) for r in rows]
        rest = [r - t for r, t in zip(rows, tops)]
        stack = jnp.concatenate(tops + rest + [jnp.zeros((2, WIDE), f32)], axis=0).astype(bf16)
        total = total + lax.dot_general(
            stack, hot_rows(wide_row(slot_ref, j), LANES), NT, preferred_element_type=f32
        )
    total_ref[...] = total + pltpu.roll(total, 5, axis=0)


def start_kernel(held, count_y, v_any, old_any, cell_any, member_any, drag_any, inertia_any, mv_any, mass_any,
                 v_ref, old_ref, drag_ref, inertia_ref, slot_ref, row_ref, depth_ref, key_ref, low_ref, xkey_ref,
                 xlow_ref, own_ref, s_ref, cell_ref, member_ref, mv_ref, mass_ref, table_ref, sem):
    pairs = [(cell_any, cell_ref), (v_any, v_ref), (member_any, member_ref), (mv_any, mv_ref), (mass_any, mass_ref),
             (drag_any, drag_ref), (inertia_any, inertia_ref), (old_any, old_ref)]
    copies = [pltpu.make_async_copy(a, b, sem.at[k]) for k, (a, b) in enumerate(pairs)]
    for copy in copies:
        copy.start()
    comps, nx, ny, nz = v_ref.shape
    copies[0].wait()
    cell = cell_ref[...]
    row, depth = lax.div(cell, nz), lax.rem(cell, nz)
    row_ref[...] = row
    depth_ref[...] = depth
    x, y = lax.div(row, ny), lax.rem(row, ny)
    ring = 2 * (nx + ny)
    edge = jnp.where(x == 0, 2 * nx + y, jnp.where(x == nx - 1, 2 * nx + ny + y, -1))
    edge = jnp.where(y == 0, x, jnp.where(y == ny - 1, nx + x, edge))
    z = nz * ring // WIDE
    key_ref[...] = jnp.where(edge < 0, -1, lax.div(depth, z) * ring + edge)
    low_ref[...] = lax.rem(depth, z)
    face = jnp.where(x == 0, y, jnp.where(x == nx - 1, ny + y, -1))
    z = nz * 2 * ny // WIDE
    xkey_ref[...] = jnp.where(face < 0, -1, lax.div(depth, z) * (2 * ny) + face)
    xlow_ref[...] = lax.rem(depth, z)
    copies[1].wait()
    gather([v_ref[k].reshape(nx * ny, nz) for k in range(comps)], table_ref, row_ref, depth_ref, s_ref)
    for copy in copies[2:]:
        copy.wait()
    member = member_ref[...]
    owner = lax.div(lax.div(member, held), count_y)
    slot_ref[...] = (owner - lax.axis_index("gx") + 1) * held + lax.rem(member, held)
    own_ref[...] = jnp.zeros_like(own_ref)
    own_ref[0:3, 0:held] = mv_ref[...]
    own_ref[3:4, 0:held] = mass_ref[...]


def old_kernel(old_ref, row_ref, depth_ref, inertia_ref, s_ref, acc_ref, table_ref):
    comps, nx, ny, nz = old_ref.shape
    gather([old_ref[k].reshape(nx * ny, nz) for k in range(comps)], table_ref, row_ref, depth_ref, acc_ref)
    for c in range(comps):
        acc_ref[c] = inertia_ref[...] * (s_ref[c] - acc_ref[c])


def first_kernel(held, count_x, v_ref, s_ref, acc_ref, slot_ref, drag_ref, key_ref, low_ref, own_ref, even_ref,
                 odd_ref, force_ref, mtable_ref, spill_ref, ye_ref, yo_ref, col_ref, field_ref):
    low, high = beside(even_ref[...], odd_ref[...], lax.axis_index("gx"), count_x)
    table = low + pltpu.roll(own_ref[...], held, axis=1) + pltpu.roll(high, 2 * held, axis=1)
    mtable_ref[...] = table
    forces([s_ref[c] for c in range(3)], [acc_ref[c] for c in range(3)], slot_ref[...], drag_ref[...], table,
           force_ref)
    edges(v_ref, force_ref, key_ref, low_ref, col_ref, field_ref, spill_ref, (ye_ref, yo_ref))


def deposit_kernel(force_ref, row_ref, depth_ref, after_ref, out_ref, col_ref, acc_ref):
    comps, rows, nz = out_ref.shape
    for j in range(row_ref.shape[0] // 2):
        hot = hot_rows(wide_row(row_ref, j), rows)
        columns(col_ref, force_ref, wide_row(depth_ref, j), nz, j, 3)
        part = lax.dot_general(hot, col_ref[...], NT, preferred_element_type=f32)
        acc_ref[...] = part if j == 0 else acc_ref[...] + part
    for c in range(comps):
        out_ref[c] = -(acc_ref[:, c * nz : (c + 1) * nz] + acc_ref[:, (3 + c) * nz : (4 + c) * nz])


def turn_kernel(count_y, spill_ref, even_ref, odd_ref, total_ref, after_ref, xe_ref, xo_ref):
    comps, ny, nz = spill_ref.shape[1:]
    low, high = beside(even_ref[comps], odd_ref[comps], lax.axis_index("gy"), count_y)
    even = lax.axis_index("gx") % 2 == 0
    ids = lax.broadcasted_iota(i32, (ny, nz), 0)
    for c in range(comps):
        sides = []
        for side in range(2):
            at = 3 * side + c
            face = spill_ref[side, c]
            face = face + jnp.where(ids == 0, low[at : at + 1], 0.0)
            face = face + jnp.where(ids == ny - 1, high[at : at + 1], 0.0)
            sides.append(face)
        xe_ref[c] = jnp.where(even, sides[1], sides[0])
        xo_ref[c] = jnp.where(even, sides[0], sides[1])
    for ref in (xe_ref, xo_ref):
        ref[comps, 0:8, :] = total_ref[...]
        ref[comps, 8:16, :] = jnp.zeros_like(total_ref)


def own_update(c, v_ref, load_ref, l_ref, low, high):
    nx, ny, nz = v_ref.shape[1:]
    v = v_ref[c]
    w = smooth(smooth(smooth(load_ref[c].reshape(nx, ny, nz), 2), 1), 0)
    beside_all = both(v, 0) + both(v, 1) + both(v, 2)
    l_ref[c] = v + viscous * (beside_all - 6.0 * v) + w
    add_y(c, low, high, l_ref)


def middle_kernel(count_y, v_ref, load_ref, even_ref, odd_ref, row_ref, depth_ref, after_ref, l_ref, s_ref,
                  table_ref):
    comps, nx, ny, nz = v_ref.shape
    low, high = beside(even_ref[...], odd_ref[...], lax.axis_index("gy"), count_y)
    for c in range(comps):
        own_update(c, v_ref, load_ref, l_ref, low, high)
    gather([l_ref[k].reshape(nx * ny, nz) for k in range(comps)], table_ref, row_ref, depth_ref, s_ref)


def sum_totals(held, count_x, total, low1, high1, even2, odd2):
    own_x = lax.axis_index("gx")
    even = own_x // 2 % 2 == 0
    low2 = jnp.where(own_x > 1, jnp.where(even, odd2, even2), 0.0)
    high2 = jnp.where(own_x < count_x - 2, jnp.where(even, even2, odd2), 0.0)
    lane = lax.broadcasted_iota(i32, (8, LANES), 1)
    total = total + pltpu.roll(low1, LANES - held, axis=1) + pltpu.roll(high1, held, axis=1)
    total = total + jnp.where(lane < held, pltpu.roll(low2, LANES - 2 * held, axis=1), 0.0)
    return total + jnp.where(lane // held == 2, pltpu.roll(high2, 2 * held, axis=1), 0.0)


def second_kernel(held, count_x, l_ref, sp_ref, xe_ref, xo_ref, s_ref, inertia_ref, slot_ref, drag_ref, key_ref,
                  low_ref, xkey_ref, xlow_ref, old_table_ref, old_total_ref, te_ref, to_ref,
                  v_ref, force_ref, mtable_ref, spill_ref, ye_ref, yo_ref,
                  col_ref, field_ref, face_ref, sample_ref):
    comps, nx, ny, nz = l_ref.shape
    low, high = beside(xe_ref[...], xo_ref[...], lax.axis_index("gx"), count_x)
    total = sum_totals(held, count_x, old_total_ref[...], low[comps, 0:8], high[comps, 0:8], te_ref[...], to_ref[...])
    old = old_table_ref[...]
    row = lax.broadcasted_iota(i32, (8, LANES), 0)
    lane = lax.broadcasted_iota(i32, (8, LANES), 1)
    table = jnp.where((row < 3) & (lane < 3 * held), old + old[3:4] * total, old)
    mtable_ref[...] = table
    z = nz * 2 * ny // WIDE
    for c in range(comps):
        turned = jnp.concatenate([low[c], high[c]], axis=0).T
        wide = jnp.concatenate([turned[h * z : (h + 1) * z] for h in range(nz // z)], axis=1)
        face_ref[0, c * z : (c + 1) * z, :], face_ref[1, c * z : (c + 1) * z, :] = split(wide)
    for j in range(xkey_ref.shape[0] // 2):
        hot = hot_rows(wide_row(xkey_ref, j), WIDE)
        product = jnp.dot(face_ref[0], hot, preferred_element_type=f32)
        product = product + jnp.dot(face_ref[1], hot, preferred_element_type=f32)
        for k, found in enumerate(pick(product, wide_row(xlow_ref, j), comps)):
            store_row(sample_ref, k, j, found)
    v_ref[...] = l_ref[...]
    for c in range(comps):
        v_ref[c, 0] += low[c]
        v_ref[c, nx - 1] += high[c]
    samples = [sp_ref[c] + sample_ref[c] for c in range(comps)]
    acc = [inertia_ref[...] * (samples[c] - s_ref[c]) for c in range(comps)]
    forces(samples, acc, slot_ref[...], drag_ref[...], table, force_ref)
    edges(v_ref, force_ref, key_ref, low_ref, col_ref, field_ref, spill_ref, (ye_ref, yo_ref))


def finish_kernel(count_y, v_ref, load_ref, even_ref, odd_ref, after_ref, out_hbm, face_ref, l_ref, sem):
    comps, nx = v_ref.shape[:2]
    low, high = beside(even_ref[...], odd_ref[...], lax.axis_index("gy"), count_y)
    for c in range(comps):
        own_update(c, v_ref, load_ref, l_ref, low, high)
        pltpu.make_async_copy(l_ref.at[c], out_hbm.at[c], sem.at[c]).start()
        face_ref[c, 0] = l_ref[c, 0]
        face_ref[c, 1] = l_ref[c, nx - 1]
    for c in range(comps):
        pltpu.make_async_copy(l_ref.at[c], out_hbm.at[c], sem.at[c]).wait()


def last_kernel(held, count_x, face_ref, xe_ref, xo_ref, mtable_ref, total_ref, old_hbm, m_hbm, v_hbm, new_ref, m_ref, sem):
    comps, nx = v_hbm.shape[:2]
    low, high = beside(xe_ref[...], xo_ref[...], lax.axis_index("gx"), count_x)
    copies = []
    for side, part in enumerate((low, high)):
        for c in range(comps):
            new_ref[side, c] = face_ref[c, side] + part[c]
        copies.append(pltpu.make_async_copy(new_ref.at[side], v_hbm.at[:, side * (nx - 1)], sem.at[side]))
        copies[-1].start()
    total = total_ref[...] + pltpu.roll(low[comps, 0:8], LANES - held, axis=1)
    total = total + pltpu.roll(high[comps, 0:8], held, axis=1)
    table = mtable_ref[...]
    table = table + table[3:4] * total
    m_ref[...] = pltpu.roll(table, LANES - held, axis=1)[0:3, :held]
    copies.append(pltpu.make_async_copy(m_ref, m_hbm, sem.at[2]))
    copies[-1].start()
    for copy in copies:
        copy.wait()


def pairs(axis, stride, odd):
    count_x, count_y = lax.axis_size("gx"), lax.axis_size("gy")
    found = []
    for x in range(count_x):
        for y in range(count_y):
            at, count = (x, count_x) if axis == "gx" else (y, count_y)
            to = ((at + stride) ^ stride) - stride if odd else at ^ stride
            if axis == "gy":
                target = (x, to % count)
            else:
                target = (to, y) if 0 <= to < count else (x, y ^ 1)
            found.append((x * count_y + y, target[0] * count_y + target[1]))
    return found


def exchange(even_msg, odd_msg, axis, stride=1):
    both_axes = ("gx", "gy")
    return (
        lax.ppermute(even_msg, both_axes, pairs(axis, stride, False)),
        lax.ppermute(odd_msg, both_axes, pairs(axis, stride, True)),
    )


def per_device(velocity, velocity_old, station_cell, station_member, drag_coef, inertia_coef, member_velocity,
               member_inv_mass):
    count_x, count_y = lax.axis_size("gx"), lax.axis_size("gy")
    held = member_velocity.shape[1]
    grid = velocity.shape
    comps, nx, ny, nz = grid
    rows = nx * ny
    lines = (station_cell.shape[0] // LANES, LANES)
    ints = jax.ShapeDtypeStruct(lines, i32)
    one = real(*lines)
    three = real(3, *lines)
    tile = real(8, LANES)
    face = real(comps + 1, max(nx, ny), nz)
    spill = real(2, comps, ny, nz)
    product = 12 * nz * rows * lines[0] * LANES
    table = pltpu.VMEM((2, comps * nz, rows), bf16)

    (v, old, drag, inertia, slot, row, depth, key, low, xkey, xlow, own, s) = call(
        "start", functools.partial(start_kernel, held, count_y),
        (velocity, velocity_old, station_cell.reshape(lines), station_member.reshape(lines),
         drag_coef.reshape(lines), inertia_coef.reshape(lines), member_velocity, member_inv_mass.reshape(1, held)),
        [real(*grid)] * 2 + [one] * 2 + [ints] * 7 + [tile, three],
        [pltpu.VMEM(lines, i32), pltpu.VMEM(lines, i32), pltpu.VMEM((3, held), f32), pltpu.VMEM((1, held), f32),
         table, pltpu.SemaphoreType.DMA((8,))],
        in_hbm=range(8), flops=product,
    )
    own_even, own_odd = exchange(own, own, "gx")
    (acc,) = call("old_samples", old_kernel, (old, row, depth, inertia, s), [three], [table], flops=product)
    work = [pltpu.VMEM((WIDE, WIDE), bf16), pltpu.VMEM((WIDE, WIDE), f32)]
    edge_parts = [three, tile, spill, face, face]
    force, mtable, spills, y_even, y_odd = call(
        "first_forces", functools.partial(first_kernel, held, count_x),
        (v, s, acc, slot, drag, key, low, own, own_even, own_odd), edge_parts, work, flops=product // 2,
    )

    def turn(force, spills, y_even, y_odd):
        (total,) = call("totals", totals_kernel, (force, slot, y_even), [tile])
        y_even, y_odd = exchange(y_even, y_odd, "gy")
        (load,) = call(
            "deposit", deposit_kernel, (force, row, depth, total), [real(comps, rows, nz)],
            [pltpu.VMEM((6 * nz, WIDE), bf16), pltpu.VMEM((rows, 6 * nz), f32)], flops=product,
        )
        x_even, x_odd = call(
            "turn", functools.partial(turn_kernel, count_y), (spills, y_even, y_odd, total, load), [face, face]
        )
        return total, load, y_even, y_odd, x_even, x_odd

    total, load, y_even, y_odd, x_even, x_odd = turn(force, spills, y_even, y_odd)
    second_even, second_odd = exchange(total, total, "gx", 2)
    local, samples = call(
        "middle", functools.partial(middle_kernel, count_y), (v, load, y_even, y_odd, row, depth, x_even),
        [real(*grid), three], [table], flops=product,
    )
    x_even, x_odd = exchange(x_even, x_odd, "gx")
    z = nz * 2 * ny // WIDE
    v, force, mtable, spills, y_even, y_odd = call(
        "second_forces", functools.partial(second_kernel, held, count_x),
        (local, samples, x_even, x_odd, s, inertia, slot, drag, key, low, xkey, xlow, mtable, total,
         second_even, second_odd),
        [real(*grid)] + edge_parts, work + [pltpu.VMEM((2, comps * z, WIDE), bf16), pltpu.VMEM((3,) + lines, f32)],
        flops=product // 2,
    )
    total, load, y_even, y_odd, x_even, x_odd = turn(force, spills, y_even, y_odd)
    out, faces = call(
        "finish", functools.partial(finish_kernel, count_y), (v, load, y_even, y_odd, x_even),
        [real(*grid), real(comps, 2, ny, nz)], [pltpu.VMEM(grid, f32), pltpu.SemaphoreType.DMA((comps,))],
        out_hbm=(0,),
    )
    x_even, x_odd = exchange(x_even, x_odd, "gx")
    members, out = call(
        "last", functools.partial(last_kernel, held, count_x), (faces, x_even, x_odd, mtable, total, out),
        [real(3, held), real(*grid)], [pltpu.VMEM((2, comps, ny, nz), f32), pltpu.VMEM((3, held), f32), pltpu.SemaphoreType.DMA((3,))],
        in_hbm=(5,), out_hbm=(0, 1), aliases={5: 1},
    )
    return out, members


def solution(mesh):
    return jax.shard_map(
        per_device,
        mesh=mesh,
        in_specs=(
            P(None, "gx", "gy", None),
            P(None, "gx", "gy", None),
            P(("gx", "gy")),
            P(("gx", "gy"), None),
            P(("gx", "gy")),
            P(("gx", "gy")),
            P(None, ("gx", "gy")),
            P(("gx", "gy")),
        ),
        out_specs=(P(None, "gx", "gy", None), P(None, ("gx", "gy"))),
        check_vma=False,
    )
```

time: 659 us -> 36.6 us (0.06)
  the two profiles are of different devices: /device:TPU:0 before, /device:TPU:8 now
where the time goes in v2:
time: 36.6 us; the launch traced here: 36.4 us
  Pallas kernels  17.3 us (47%)
  starting transfers between devices  9.57 us (26%)
  waiting for transfers between devices  8.72 us (24%)
  between operations  0.76 us (2%)
    pallas_call x13, Pallas kernels, call(): pl.pallas_call(body, name=name, out_shape=outs, in_specs=[HBM if k in in_...  17.3 us
    ppermute x6, waiting for transfers between devices, exchange(): lax.ppermute(odd_msg, both_axes, pairs(axis, stride, True))  7.01 us
    ppermute x6, starting transfers between devices, exchange(): lax.ppermute(odd_msg, both_axes, pairs(axis, stride, True))  5.74 us
    ppermute x6, starting transfers between devices, exchange(): lax.ppermute(even_msg, both_axes, pairs(axis, stride, False))  3.84 us
    ppermute x6, waiting for transfers between devices, exchange(): lax.ppermute(even_msg, both_axes, pairs(axis, stride, False))  1.71 us
  transfers between devices with their start and end apart: 12, of which 7 were waited for; matrix products, arithmetic and copies ran while one was open for 0% of the time, Pallas kernels for 29%

profile of v2, /device:TPU:8, one launch (start us, length us, event | category | flops | bytes accessed | tf_op | source)
XLA Modules:
  0.0 36.4 jit_solution(6582843727179760119)
XLA Ops:
  0.6 3.1 %start.1 = (f32[3,16,16,128]{3,2,1,0:T(8,128)S(1)}, f32[3,16,16,128]{3,2,1,0:T(8,128)S(1)}, f32[32,128]{1,0:T(8,128)S(1)}, f32[32,128]{1,0:T(8,128)S(1)}, s32[32...) custom-call(f32[3,16,16,128]{3,2,1,0:T(8,128)} %v_any.1, ...), custom_call_target="tpu_custom_call" | custom-call | flops 1610612736 | bytes 262144 | tf_op jit(solution)/shard_map/start/pallas_call | solution.py:28
  3.8 1.6 %collective-permute-start = (f32[8,128]{1,0:T(8,128)S(1)}, f32[8,128]{1,0:T(8,128)S(1)}, u32[]{:S(2)}, u32[]{:S(2)}) collective-permute-start(f32[8,128]{1,0:T(8,128)S(1)} %get-tuple-element.46.own_ref), channel_id=1, source_target_pairs={{0,4},{1,5},{2,6},{3,7},{4,0},{5,1},{6,2},{7,3},{8,12},{9,13},{10,... | collective-permute-start | bytes 12296 | tf_op jit(solution)/shard_map/ppermute | solution.py:388
  5.3 0.0 collective-permute-start.1
  5.3 2.0 %old_samples.1.acc_ref = f32[3,32,128]{2,1,0:T(8,128)S(1)} custom-call(f32[3,16,16,128]{3,2,1,0:T(8,128)S(1)} %get-tuple-element.38.old_ref, s32[32,128]{1,0:T(8,128)S(1)} %get-tuple-element.39.row_ref, s32[32,128]{1,0:T(8,128)S(1)} %get-tuple-element.40.depth_ref, f32[32,128]{1,0:T(8,128)S(1)} %get-tuple-element.41.inertia_ref, ...), custom_call_target="tpu_custom_call" | custom-call | flops 1610612736 | bytes 262144 | tf_op jit(solution)/shard_map/old_samples/pallas_call | solution.py:28
  7.3 0.1 collective-permute-done.even_ref
  7.4 2.4 %collective-permute-done.1.odd_ref = f32[8,128]{1,0:T(8,128)S(1)} collective-permute-done((f32[8,128]{1,0:T(8,128)S(1)}, f32[8,128]{1,0:T(8,128)S(1)}, u32[]{:S(2)}, u32[]{:S(2)}) %collective-permute-start.1) | collective-permute-done | bytes 4128 | tf_op jit(solution)/shard_map/ppermute | solution.py:389
  9.8 1.1 %first_forces.1 = (f32[3,32,128]{2,1,0:T(8,128)S(1)}, f32[8,128]{1,0:T(8,128)S(1)}, f32[2,3,16,128]{3,2,1,0:T(8,128)S(1)}, f32[4,16,128]{2,1,0:T(8,128)S(1)}, f32[4,16,128]{2,1,0:T(8,128)S(1)}) custom-call(f32[3,16,16,128]{3,2,1,0:T(8,128)S(1)} %get-tuple-element.36.v_ref, f32[3,32,128]{2,1,0:T(8,128)S(1)} %get-tuple-element.37.s_ref, ...), custom_call_target="tpu_custom_call" | custom-call | flops 805306368 | bytes 262144 | tf_op jit(solution)/shard_map/first_forces/pallas_call | solution.py:28
  10.9 0.1 collective-permute-start.2
  11.0 0.4 %totals.2.after_ref.total_ref.old_total_ref = f32[8,128]{1,0:T(8,128)S(1)} custom-call(f32[3,32,128]{2,1,0:T(8,128)S(1)} %get-tuple-element.47.force_ref, s32[32,128]{1,0:T(8,128)S(1)} %get-tuple-element.42.slot_ref, f32[4,16,128]{2,1,0:T(8,128)S(1)} %get-tuple-element.48.after_ref), custom_call_target="tpu_custom_call" | custom-call | bytes 262144 | tf_op jit(solution)/shard_map/totals/pallas_call | solution.py:28
  11.4 1.6 %collective-permute-start.3 = (f32[4,16,128]{2,1,0:T(8,128)S(1)}, f32[4,16,128]{2,1,0:T(8,128)S(1)}, u32[]{:S(2)}, u32[]{:S(2)}) collective-permute-start(f32[4,16,128]{2,1,0:T(8,128)S(1)} %get-tuple-element.49), channel_id=1, source_target_pairs={{0,3},{1,2},{2,1},{3,0},{4,7},{5,6},{6,5},{7,4},{8,11},{9,10},{10,... | collective-permute-start | bytes 98312 | tf_op jit(solution)/shard_map/ppermute | solution.py:389
  13.0 1.9 %deposit.2.after_ref.load_ref = f32[3,256,128]{2,1,0:T(8,128)S(1)} custom-call(f32[3,32,128]{2,1,0:T(8,128)S(1)} %get-tuple-element.47.force_ref, s32[32,128]{1,0:T(8,128)S(1)} %get-tuple-element.39.row_ref, s32[32,128]{1,0:T(8,128)S(1)} %get-tuple-element.40.depth_ref, f32[8,128]{1,0:T(8,128)S(1)} %totals.2.after_ref.total_ref.old_total_ref), custom_call_target="tpu_custom_call" | custom-call | flops 1610612736 | bytes 262144 | tf_op jit(solution)/shard_map/deposit/pallas_call | solution.py:28
  14.9 0.1 collective-permute-start.6
  15.0 3.1 %collective-permute-start.7 = (f32[8,128]{1,0:T(8,128)S(1)}, f32[8,128]{1,0:T(8,128)S(1)}, u32[]{:S(2)}, u32[]{:S(2)}) collective-permute-start(f32[8,128]{1,0:T(8,128)S(1)} %totals.2.after_ref.total_ref.old_total_ref), channel_id=1, source_target_pairs={{0,1},{1,0},{2,3},{3,2},{4,5},{5,4},{6,7},{7,6},{8,16},{9,17},{10,... | collective-permute-start | bytes 12296 | tf_op jit(solution)/shard_map/ppermute | solution.py:389
  18.1 0.0 collective-permute-done.2.even_ref
  18.1 0.0 collective-permute-done.3.odd_ref
  18.2 0.1 collective-permute-start.4
  18.2 0.3 collective-permute-start.5
  18.6 2.6 %middle.1 = (f32[3,16,16,128]{3,2,1,0:T(8,128)S(1)}, f32[3,32,128]{2,1,0:T(8,128)S(1)}) custom-call(f32[3,16,16,128]{3,2,1,0:T(8,128)S(1)} %get-tuple-element.36.v_ref, f32[3,256,128]{2,1,0:T(8,128)S(1)} %deposit.2.after_ref.load_ref, f32[4,16,128]{2,1,0:T(8,128)S(1)} %collective-permute-done.2.even_ref, f32[4,16,128]{2,1,0:T(8,128)S(1)} %collective-permute-done.3.odd_ref, ...), custom_call_target="tpu_custom_call" | custom-call | flops 1610612736 | bytes 262144 | tf_op jit(solution)/shard_map/middle/pallas_call | solution.py:28
  21.2 0.0 collective-permute-done.6.te_ref
  21.2 0.0 collective-permute-done.7.to_ref
  21.2 0.9 %collective-permute-done.4.xe_ref = f32[4,16,128]{2,1,0:T(8,128)S(1)} collective-permute-done((f32[4,16,128]{2,1,0:T(8,128)S(1)}, f32[4,16,128]{2,1,0:T(8,128)S(1)}, u32[]{:S(2)}, u32[]{:S(2)}) %collective-permute-start.4) | collective-permute-done | bytes 32800 | tf_op jit(solution)/shard_map/ppermute | solution.py:388
  22.1 1.0 %collective-permute-done.5.xo_ref = f32[4,16,128]{2,1,0:T(8,128)S(1)} collective-permute-done((f32[4,16,128]{2,1,0:T(8,128)S(1)}, f32[4,16,128]{2,1,0:T(8,128)S(1)}, u32[]{:S(2)}, u32[]{:S(2)}) %collective-permute-start.5) | collective-permute-done | bytes 32800 | tf_op jit(solution)/shard_map/ppermute | solution.py:389
  23.1 1.9 %second_forces.1 = (f32[3,16,16,128]{3,2,1,0:T(8,128)S(1)}, f32[3,32,128]{2,1,0:T(8,128)S(1)}, f32[8,128]{1,0:T(8,128)S(1)}, f32[2,3,16,128]{3,2,1,0:T(8,128)S(1...) custom-call(f32[3,16,16,128]{3,2,1,0:T(8,128)S(1)} %get-tuple-element.52.l_ref, ...), custom_call_target="tpu_custom_call" | custom-call | flops 805306368 | bytes 262144 | tf_op jit(solution)/shard_map/second_forces/pallas_call | solution.py:28
  25.0 0.1 collective-permute-start.8
  25.1 0.4 %totals.3.after_ref.total_ref = f32[8,128]{1,0:T(8,128)S(1)} custom-call(f32[3,32,128]{2,1,0:T(8,128)S(1)} %get-tuple-element.59.force_ref, s32[32,128]{1,0:T(8,128)S(1)} %get-tuple-element.42.slot_ref, f32[4,16,128]{2,1,0:T(8,128)S(1)} %get-tuple-element.60.after_ref), custom_call_target="tpu_custom_call" | custom-call | bytes 262144 | tf_op jit(solution)/shard_map/totals/pallas_call | solution.py:28
  25.5 0.6 %collective-permute-start.9 = (f32[4,16,128]{2,1,0:T(8,128)S(1)}, f32[4,16,128]{2,1,0:T(8,128)S(1)}, u32[]{:S(2)}, u32[]{:S(2)}) collective-permute-start(f32[4,16,128]{2,1,0:T(8,128)S(1)} %get-tuple-element.61), channel_id=1, source_target_pairs={{0,3},{1,2},{2,1},{3,0},{4,7},{5,6},{6,5},{7,4},{8,11},{9,10},{10,... | collective-permute-start | bytes 98312 | tf_op jit(solution)/shard_map/ppermute | solution.py:389
  26.1 1.8 %deposit.3.after_ref.load_ref = f32[3,256,128]{2,1,0:T(8,128)S(1)} custom-call(f32[3,32,128]{2,1,0:T(8,128)S(1)} %get-tuple-element.59.force_ref, s32[32,128]{1,0:T(8,128)S(1)} %get-tuple-element.39.row_ref, s32[32,128]{1,0:T(8,128)S(1)} %get-tuple-element.40.depth_ref, f32[8,128]{1,0:T(8,128)S(1)} %totals.3.after_ref.total_ref), custom_call_target="tpu_custom_call" | custom-call | flops 1610612736 | bytes 262144 | tf_op jit(solution)/shard_map/deposit/pallas_call | solution.py:28
  27.9 0.0 collective-permute-done.8.even_ref
  27.9 0.9 %collective-permute-done.9.odd_ref = f32[4,16,128]{2,1,0:T(8,128)S(1)} collective-permute-done((f32[4,16,128]{2,1,0:T(8,128)S(1)}, f32[4,16,128]{2,1,0:T(8,128)S(1)}, u32[]{:S(2)}, u32[]{:S(2)}) %collective-permute-start.9) | collective-permute-done | bytes 32800 | tf_op jit(solution)/shard_map/ppermute | solution.py:389
  28.8 2.0 %collective-permute-start.10 = (f32[4,16,128]{2,1,0:T(8,128)S(1)}, f32[4,16,128]{2,1,0:T(8,128)S(1)}, u32[]{:S(2)}, u32[]{:S(2)}) collective-permute-start(f32[4,16,128]{2,1,0:T(8,128)S(1)} %get-tuple-element.63.after_ref), channel_id=1, source_target_pairs={{0,4},{1,5},{2,6},{3,7},{4,0},{5,1},{6,2},{7,3},{8,12},{9,13},{10,... | collective-permute-start | bytes 98312 | tf_op jit(solution)/shard_map/ppermute | solution.py:388
  30.8 0.0 collective-permute-start.11
  30.8 1.4 %finish.1 = (f32[3,16,16,128]{3,2,1,0:T(8,128)}, f32[3,2,16,128]{3,2,1,0:T(8,128)S(1)}) custom-call(f32[3,16,16,128]{3,2,1,0:T(8,128)S(1)} %get-tuple-element.58.v_ref, f32[3,256,128]{2,1,0:T(8,128)S(1)} %deposit.3.after_ref.load_ref, f32[4,16,128]{2,1,0:T(8,128)S(1)} %collective-permute-done.8.even_ref, f32[4,16,128]{2,1,0:T(8,128)S(1)} %collective-permute-done.9.odd_ref, ...), custom_call_target="tpu_custom_call" | custom-call | bytes 262144 | tf_op jit(solution)/shard_map/finish/pallas_call | solution.py:28
  32.2 0.7 %collective-permute-done.10.xe_ref = f32[4,16,128]{2,1,0:T(8,128)S(1)} collective-permute-done((f32[4,16,128]{2,1,0:T(8,128)S(1)}, f32[4,16,128]{2,1,0:T(8,128)S(1)}, u32[]{:S(2)}, u32[]{:S(2)}) %collective-permute-start.10) | collective-permute-done | bytes 32800 | tf_op jit(solution)/shard_map/ppermute | solution.py:388
  32.9 2.8 %collective-permute-done.11.xo_ref = f32[4,16,128]{2,1,0:T(8,128)S(1)} collective-permute-done((f32[4,16,128]{2,1,0:T(8,128)S(1)}, f32[4,16,128]{2,1,0:T(8,128)S(1)}, u32[]{:S(2)}, u32[]{:S(2)}) %collective-permute-start.11) | collective-permute-done | bytes 32800 | tf_op jit(solution)/shard_map/ppermute | solution.py:389
  35.6 0.7 %last.1 = (f32[3,16]{1,0:T(4,128)}, f32[3,16,16,128]{3,2,1,0:T(8,128)}) custom-call(f32[3,2,16,128]{3,2,1,0:T(8,128)S(1)} %get-tuple-element.64.face_ref, f32[4,16,128]{2,1,0:T(8,128)S(1)} %collective-permute-done.10.xe_ref, f32[4,16,128]{2,1,0:T(8,128)S(1)} %collective-permute-done.11.xo_ref, ...), custom_call_target="tpu_custom_call", output_to_operand_aliasing={{1}: (5, {})} | custom-call | bytes 262144 | tf_op jit(solution)/shard_map/last/pallas_call | solution.py:28
  (2 shorter events, 0.0 us)
Async XLA Ops:
  3.8 3.7 %collective-permute-start = (f32[8,128]{1,0:T(8,128)S(1)}, f32[8,128]{1,0:T(8,128)S(1)}, u32[]{:S(2)}, u32[]{:S(2)}) collective-permute-start(f32[8,128]{1,0:T(8,128)S(1)} %get-tuple-element.46.own_ref), channel_id=1, source_target_pairs={{0,4},{1,5},{2,6},{3,7},{4,0},{5,1},{6,2},{7,3},{8,12},{9,13},{10,... | collective-permute-start | bytes 12296 | tf_op jit(solution)/shard_map/ppermute | solution.py:388
  5.3 4.5 %collective-permute-start.1 = (f32[8,128]{1,0:T(8,128)S(1)}, f32[8,128]{1,0:T(8,128)S(1)}, u32[]{:S(2)}, u32[]{:S(2)}) collective-permute-start(f32[8,128]{1,0:T(8,128)S(1)} %get-tuple-element.46.own_ref), channel_id=1, source_target_pairs={{0,1},{1,0},{2,3},{3,2},{4,8},{5,9},{6,10},{7,11},{8,4},{9,5},{10,... | collective-permute-start | bytes 12296 | tf_op jit(solution)/shard_map/ppermute | solution.py:389
  10.9 7.2 %collective-permute-start.2 = (f32[4,16,128]{2,1,0:T(8,128)S(1)}, f32[4,16,128]{2,1,0:T(8,128)S(1)}, u32[]{:S(2)}, u32[]{:S(2)}) collective-permute-start(f32[4,16,128]{2,1,0:T(8,128)S(1)} %get-tuple-element.48.after_ref), channel_id=1, source_target_pairs={{0,1},{1,0},{2,3},{3,2},{4,5},{5,4},{6,7},{7,6},{8,9},{9,8},{10,11... | collective-permute-start | bytes 98312 | tf_op jit(solution)/shard_map/ppermute | solution.py:388
  11.4 6.7 %collective-permute-start.3 = (f32[4,16,128]{2,1,0:T(8,128)S(1)}, f32[4,16,128]{2,1,0:T(8,128)S(1)}, u32[]{:S(2)}, u32[]{:S(2)}) collective-permute-start(f32[4,16,128]{2,1,0:T(8,128)S(1)} %get-tuple-element.49), channel_id=1, source_target_pairs={{0,3},{1,2},{2,1},{3,0},{4,7},{5,6},{6,5},{7,4},{8,11},{9,10},{10,... | collective-permute-start | bytes 98312 | tf_op jit(solution)/shard_map/ppermute | solution.py:389
  14.9 6.3 %collective-permute-start.6 = (f32[8,128]{1,0:T(8,128)S(1)}, f32[8,128]{1,0:T(8,128)S(1)}, u32[]{:S(2)}, u32[]{:S(2)}) collective-permute-start(f32[8,128]{1,0:T(8,128)S(1)} %totals.2.after_ref.total_ref.old_total_ref), channel_id=1, source_target_pairs={{0,8},{1,9},{2,10},{3,11},{4,12},{5,13},{6,14},{7,15},{8,0},{9,1},... | collective-permute-start | bytes 12296 | tf_op jit(solution)/shard_map/ppermute | solution.py:388
  15.0 6.2 %collective-permute-start.7 = (f32[8,128]{1,0:T(8,128)S(1)}, f32[8,128]{1,0:T(8,128)S(1)}, u32[]{:S(2)}, u32[]{:S(2)}) collective-permute-start(f32[8,128]{1,0:T(8,128)S(1)} %totals.2.after_ref.total_ref.old_total_ref), channel_id=1, source_target_pairs={{0,1},{1,0},{2,3},{3,2},{4,5},{5,4},{6,7},{7,6},{8,16},{9,17},{10,... | collective-permute-start | bytes 12296 | tf_op jit(solution)/shard_map/ppermute | solution.py:389
  18.2 4.0 %collective-permute-start.4 = (f32[4,16,128]{2,1,0:T(8,128)S(1)}, f32[4,16,128]{2,1,0:T(8,128)S(1)}, u32[]{:S(2)}, u32[]{:S(2)}) collective-permute-start(f32[4,16,128]{2,1,0:T(8,128)S(1)} %get-tuple-element.51.after_ref), channel_id=1, source_target_pairs={{0,4},{1,5},{2,6},{3,7},{4,0},{5,1},{6,2},{7,3},{8,12},{9,13},{10,... | collective-permute-start | bytes 98312 | tf_op jit(solution)/shard_map/ppermute | solution.py:388
  18.2 4.9 %collective-permute-start.5 = (f32[4,16,128]{2,1,0:T(8,128)S(1)}, f32[4,16,128]{2,1,0:T(8,128)S(1)}, u32[]{:S(2)}, u32[]{:S(2)}) collective-permute-start(f32[4,16,128]{2,1,0:T(8,128)S(1)} %get-tuple-element.54), channel_id=1, source_target_pairs={{0,1},{1,0},{2,3},{3,2},{4,8},{5,9},{6,10},{7,11},{8,4},{9,5},{10,... | collective-permute-start | bytes 98312 | tf_op jit(solution)/shard_map/ppermute | solution.py:389
  25.0 2.9 %collective-permute-start.8 = (f32[4,16,128]{2,1,0:T(8,128)S(1)}, f32[4,16,128]{2,1,0:T(8,128)S(1)}, u32[]{:S(2)}, u32[]{:S(2)}) collective-permute-start(f32[4,16,128]{2,1,0:T(8,128)S(1)} %get-tuple-element.60.after_ref), channel_id=1, source_target_pairs={{0,1},{1,0},{2,3},{3,2},{4,5},{5,4},{6,7},{7,6},{8,9},{9,8},{10,11... | collective-permute-start | bytes 98312 | tf_op jit(solution)/shard_map/ppermute | solution.py:388
  25.5 3.4 %collective-permute-start.9 = (f32[4,16,128]{2,1,0:T(8,128)S(1)}, f32[4,16,128]{2,1,0:T(8,128)S(1)}, u32[]{:S(2)}, u32[]{:S(2)}) collective-permute-start(f32[4,16,128]{2,1,0:T(8,128)S(1)} %get-tuple-element.61), channel_id=1, source_target_pairs={{0,3},{1,2},{2,1},{3,0},{4,7},{5,6},{6,5},{7,4},{8,11},{9,10},{10,... | collective-permute-start | bytes 98312 | tf_op jit(solution)/shard_map/ppermute | solution.py:389
  28.8 4.0 %collective-permute-start.10 = (f32[4,16,128]{2,1,0:T(8,128)S(1)}, f32[4,16,128]{2,1,0:T(8,128)S(1)}, u32[]{:S(2)}, u32[]{:S(2)}) collective-permute-start(f32[4,16,128]{2,1,0:T(8,128)S(1)} %get-tuple-element.63.after_ref), channel_id=1, source_target_pairs={{0,4},{1,5},{2,6},{3,7},{4,0},{5,1},{6,2},{7,3},{8,12},{9,13},{10,... | collective-permute-start | bytes 98312 | tf_op jit(solution)/shard_map/ppermute | solution.py:388
  30.8 4.8 %collective-permute-start.11 = (f32[4,16,128]{2,1,0:T(8,128)S(1)}, f32[4,16,128]{2,1,0:T(8,128)S(1)}, u32[]{:S(2)}, u32[]{:S(2)}) collective-permute-start(f32[4,16,128]{2,1,0:T(8,128)S(1)} %get-tuple-element.65), channel_id=1, source_target_pairs={{0,1},{1,0},{2,3},{3,2},{4,8},{5,9},{6,10},{7,11},{8,4},{9,5},{10,... | collective-permute-start | bytes 98312 | tf_op jit(solution)/shard_map/ppermute | solution.py:389

commit v3 on v2

--- a/solution.py
+++ b/solution.py
@@ -124,18 +124,28 @@
     ref[c, :, ny - 1, :] += face_high[c]
 
 
-def edges(v_ref, force_ref, key_ref, low_ref, col_ref, acc_ref, spill_ref, y_refs):
+def edges(v_ref, force_ref, key_ref, low_ref, slot_ref, col_ref, acc_ref, spill_ref, y_refs, total_ref):
     comps, nx, ny, nz = v_ref.shape
     ring = 2 * (nx + ny)
     parts = WIDE // ring
     z = nz // parts
-    col_ref[...] = jnp.zeros_like(col_ref)
+    slots = acc_ref.shape[0] - WIDE
+    free = 3 * z
+    for p in range(2):
+        col_ref[p * LANES + free : (p + 1) * LANES, :] = jnp.zeros((LANES - free, WIDE), bf16)
     for j in range(key_ref.shape[0] // 2):
-        hot = hot_rows(wide_row(key_ref, j), WIDE)
-        columns(col_ref, force_ref, wide_row(low_ref, j), z, j, 4)
+        hot = jnp.concatenate([hot_rows(wide_row(key_ref, j), WIDE), hot_rows(wide_row(slot_ref, j), slots)], axis=0)
+        columns(col_ref, force_ref, wide_row(low_ref, j), z, j, LANES // z)
+        pieces = [split(wide_row(force_ref.at[c], j)) for c in range(3)]
+        for p in range(2):
+            rows = [piece[p].astype(f32) for piece in pieces] + [jnp.zeros((13, WIDE), f32)]
+            col_ref[p * LANES + free : p * LANES + free + 16, :] = jnp.concatenate(rows, axis=0).astype(bf16)
         part = lax.dot_general(hot, col_ref[...], NT, preferred_element_type=f32)
         acc_ref[...] = part if j == 0 else acc_ref[...] + part
-    found = -(acc_ref[:, :LANES] + acc_ref[:, LANES:])
+    found = acc_ref[:, :LANES] + acc_ref[:, LANES:]
+    sums = jnp.concatenate([found[WIDE:], jnp.zeros((LANES - slots, LANES), f32)], axis=0)
+    total_ref[...] = sums.T[free : free + 8]
+    found = -found[:WIDE]
     lane = lax.broadcasted_iota(i32, (ring, LANES), 1) // z
     yid = lax.broadcasted_iota(i32, (ny, nz), 0)
     even = lax.axis_index("gy") % 2 == 0
@@ -175,24 +185,11 @@
         force_ref[c] = speed * relative[c] + acc[c]
 
 
-def totals_kernel(force_ref, slot_ref, after_ref, total_ref):
-    total = jnp.zeros((8, LANES), f32)
-    for j in range(slot_ref.shape[0] // 2):
-        rows = [wide_row(force_ref.at[c], j) for c in range(3)]
-        tops = [r.astype(bf16).astype(f32) for r in rows]
-        rest = [r - t for r, t in zip(rows, tops)]
-        stack = jnp.concatenate(tops + rest + [jnp.zeros((2, WIDE), f32)], axis=0).astype(bf16)
-        total = total + lax.dot_general(
-            stack, hot_rows(wide_row(slot_ref, j), LANES), NT, preferred_element_type=f32
-        )
-    total_ref[...] = total + pltpu.roll(total, 5, axis=0)
-
-
-def start_kernel(held, count_y, v_any, old_any, cell_any, member_any, drag_any, inertia_any, mv_any, mass_any,
-                 v_ref, old_ref, drag_ref, inertia_ref, slot_ref, row_ref, depth_ref, key_ref, low_ref, xkey_ref,
-                 xlow_ref, own_ref, s_ref, cell_ref, member_ref, mv_ref, mass_ref, table_ref, sem):
-    pairs = [(cell_any, cell_ref), (v_any, v_ref), (member_any, member_ref), (mv_any, mv_ref), (mass_any, mass_ref),
-             (drag_any, drag_ref), (inertia_any, inertia_ref), (old_any, old_ref)]
+def load_kernel(held, count_y, v_any, old_any, cell_any, member_any, drag_any, inertia_any, mv_any, mass_any,
+                v_ref, old_ref, drag_ref, inertia_ref, slot_ref, row_ref, depth_ref, key_ref, low_ref, xkey_ref,
+                xlow_ref, own_ref, cell_ref, member_ref, mv_ref, mass_ref, sem):
+    pairs = [(cell_any, cell_ref), (member_any, member_ref), (mv_any, mv_ref), (mass_any, mass_ref),
+             (drag_any, drag_ref), (inertia_any, inertia_ref), (v_any, v_ref), (old_any, old_ref)]
     copies = [pltpu.make_async_copy(a, b, sem.at[k]) for k, (a, b) in enumerate(pairs)]
     for copy in copies:
         copy.start()
@@ -214,46 +211,58 @@
     xkey_ref[...] = jnp.where(face < 0, -1, lax.div(depth, z) * (2 * ny) + face)
     xlow_ref[...] = lax.rem(depth, z)
     copies[1].wait()
-    gather([v_ref[k].reshape(nx * ny, nz) for k in range(comps)], table_ref, row_ref, depth_ref, s_ref)
-    for copy in copies[2:]:
-        copy.wait()
     member = member_ref[...]
     owner = lax.div(lax.div(member, held), count_y)
     slot_ref[...] = (owner - lax.axis_index("gx") + 1) * held + lax.rem(member, held)
+    for copy in copies[2:]:
+        copy.wait()
     own_ref[...] = jnp.zeros_like(own_ref)
     own_ref[0:3, 0:held] = mv_ref[...]
     own_ref[3:4, 0:held] = mass_ref[...]
 
 
-def old_kernel(old_ref, row_ref, depth_ref, inertia_ref, s_ref, acc_ref, table_ref):
-    comps, nx, ny, nz = old_ref.shape
-    gather([old_ref[k].reshape(nx * ny, nz) for k in range(comps)], table_ref, row_ref, depth_ref, acc_ref)
-    for c in range(comps):
-        acc_ref[c] = inertia_ref[...] * (s_ref[c] - acc_ref[c])
-
-
-def first_kernel(held, count_x, v_ref, s_ref, acc_ref, slot_ref, drag_ref, key_ref, low_ref, own_ref, even_ref,
-                 odd_ref, force_ref, mtable_ref, spill_ref, ye_ref, yo_ref, col_ref, field_ref):
+def sample_kernel(v_ref, old_ref, row_ref, depth_ref, inertia_ref, s_ref, acc_ref, table_ref, six_ref):
+    comps, nx, ny, nz = v_ref.shape
+    fields = [ref[k].reshape(nx * ny, nz) for ref in (v_ref, old_ref) for k in range(comps)]
+    gather(fields, table_ref, row_ref, depth_ref, six_ref)
+    for c in range(comps):
+        s_ref[c] = six_ref[c]
+        acc_ref[c] = inertia_ref[...] * (six_ref[c] - six_ref[comps + c])
+
+
+def first_kernel(held, count_x, v_ref, s_ref, acc_ref, slot_ref, drag_ref, key_ref, low_ref, own_ref, odd_ref,
+                 even_ref, force_ref, mtable_ref, spill_ref, ye_ref, yo_ref, total_ref, col_ref, field_ref):
     low, high = beside(even_ref[...], odd_ref[...], lax.axis_index("gx"), count_x)
     table = low + pltpu.roll(own_ref[...], held, axis=1) + pltpu.roll(high, 2 * held, axis=1)
     mtable_ref[...] = table
     forces([s_ref[c] for c in range(3)], [acc_ref[c] for c in range(3)], slot_ref[...], drag_ref[...], table,
            force_ref)
-    edges(v_ref, force_ref, key_ref, low_ref, col_ref, field_ref, spill_ref, (ye_ref, yo_ref))
-
-
-def deposit_kernel(force_ref, row_ref, depth_ref, after_ref, out_ref, col_ref, acc_ref):
-    comps, rows, nz = out_ref.shape
+    edges(v_ref, force_ref, key_ref, low_ref, slot_ref, col_ref, field_ref, spill_ref, (ye_ref, yo_ref), total_ref)
+
+
+def deposit(comps, force_ref, row_ref, depth_ref, col_ref, acc_ref, out_ref):
+    rows, nz = out_ref.shape[1:]
+    count = len(comps)
     for j in range(row_ref.shape[0] // 2):
         hot = hot_rows(wide_row(row_ref, j), rows)
-        columns(col_ref, force_ref, wide_row(depth_ref, j), nz, j, 3)
+        hit = hot_rows(wide_row(depth_ref, j), nz) > 0
+        for k, c in enumerate(comps):
+            for p, piece in enumerate(split(wide_row(force_ref.at[c], j))):
+                wide = jnp.broadcast_to(piece, hit.shape)
+                at = (p * count + k) * nz
+                col_ref[at : at + nz, :] = jnp.where(hit, wide, jnp.zeros_like(wide))
         part = lax.dot_general(hot, col_ref[...], NT, preferred_element_type=f32)
         acc_ref[...] = part if j == 0 else acc_ref[...] + part
-    for c in range(comps):
-        out_ref[c] = -(acc_ref[:, c * nz : (c + 1) * nz] + acc_ref[:, (3 + c) * nz : (4 + c) * nz])
-
-
-def turn_kernel(count_y, spill_ref, even_ref, odd_ref, total_ref, after_ref, xe_ref, xo_ref):
+    for k in range(count):
+        out_ref[k] = -(acc_ref[:, k * nz : (k + 1) * nz] + acc_ref[:, (count + k) * nz : (count + k + 1) * nz])
+
+
+def deposit_kernel(comps, force_ref, row_ref, depth_ref, total_ref, out_ref, same_ref, col_ref, acc_ref):
+    same_ref[...] = total_ref[...]
+    deposit(comps, force_ref, row_ref, depth_ref, col_ref, acc_ref, out_ref)
+
+
+def turn_kernel(count_y, spill_ref, odd_ref, even_ref, total_ref, after_ref, xe_ref, xo_ref):
     comps, ny, nz = spill_ref.shape[1:]
     low, high = beside(even_ref[comps], odd_ref[comps], lax.axis_index("gy"), count_y)
     even = lax.axis_index("gx") % 2 == 0
@@ -273,21 +282,21 @@
         ref[comps, 8:16, :] = jnp.zeros_like(total_ref)
 
 
-def own_update(c, v_ref, load_ref, l_ref, low, high):
+def own_update(c, v_ref, load, l_ref, low, high):
     nx, ny, nz = v_ref.shape[1:]
     v = v_ref[c]
-    w = smooth(smooth(smooth(load_ref[c].reshape(nx, ny, nz), 2), 1), 0)
+    w = smooth(smooth(smooth(load.reshape(nx, ny, nz), 2), 1), 0)
     beside_all = both(v, 0) + both(v, 1) + both(v, 2)
     l_ref[c] = v + viscous * (beside_all - 6.0 * v) + w
     add_y(c, low, high, l_ref)
 
 
-def middle_kernel(count_y, v_ref, load_ref, even_ref, odd_ref, row_ref, depth_ref, after_ref, l_ref, s_ref,
+def middle_kernel(count_y, v_ref, load_ref, odd_ref, even_ref, row_ref, depth_ref, after_ref, l_ref, s_ref,
                   table_ref):
     comps, nx, ny, nz = v_ref.shape
     low, high = beside(even_ref[...], odd_ref[...], lax.axis_index("gy"), count_y)
     for c in range(comps):
-        own_update(c, v_ref, load_ref, l_ref, low, high)
+        own_update(c, v_ref, load_ref[c], l_ref, low, high)
     gather([l_ref[k].reshape(nx * ny, nz) for k in range(comps)], table_ref, row_ref, depth_ref, s_ref)
 
 
@@ -302,9 +311,9 @@
     return total + jnp.where(lane // held == 2, pltpu.roll(high2, 2 * held, axis=1), 0.0)
 
 
-def second_kernel(held, count_x, l_ref, sp_ref, xe_ref, xo_ref, s_ref, inertia_ref, slot_ref, drag_ref, key_ref,
+def second_kernel(held, count_x, l_ref, sp_ref, xo_ref, xe_ref, s_ref, inertia_ref, slot_ref, drag_ref, key_ref,
                   low_ref, xkey_ref, xlow_ref, old_table_ref, old_total_ref, te_ref, to_ref,
-                  v_ref, force_ref, mtable_ref, spill_ref, ye_ref, yo_ref,
+                  v_ref, force_ref, mtable_ref, spill_ref, ye_ref, yo_ref, total_ref,
                   col_ref, field_ref, face_ref, sample_ref):
     comps, nx, ny, nz = l_ref.shape
     low, high = beside(xe_ref[...], xo_ref[...], lax.axis_index("gx"), count_x)
@@ -332,14 +341,18 @@
     samples = [sp_ref[c] + sample_ref[c] for c in range(comps)]
     acc = [inertia_ref[...] * (samples[c] - s_ref[c]) for c in range(comps)]
     forces(samples, acc, slot_ref[...], drag_ref[...], table, force_ref)
-    edges(v_ref, force_ref, key_ref, low_ref, col_ref, field_ref, spill_ref, (ye_ref, yo_ref))
-
-
-def finish_kernel(count_y, v_ref, load_ref, even_ref, odd_ref, after_ref, out_hbm, face_ref, l_ref, sem):
+    edges(v_ref, force_ref, key_ref, low_ref, slot_ref, col_ref, field_ref, spill_ref, (ye_ref, yo_ref), total_ref)
+
+
+def finish_kernel(count_y, early, v_ref, load_ref, odd_ref, even_ref, force_ref, row_ref, depth_ref, after_ref,
+                  out_hbm, face_ref, l_ref, rest_ref, col_ref, acc_ref, sem):
     comps, nx = v_ref.shape[:2]
     low, high = beside(even_ref[...], odd_ref[...], lax.axis_index("gy"), count_y)
-    for c in range(comps):
-        own_update(c, v_ref, load_ref, l_ref, low, high)
+    if early < comps:
+        deposit(range(early, comps), force_ref, row_ref, depth_ref, col_ref, acc_ref, rest_ref)
+    for c in range(comps):
+        load = load_ref[c] if c < early else rest_ref[c - early]
+        own_update(c, v_ref, load, l_ref, low, high)
         pltpu.make_async_copy(l_ref.at[c], out_hbm.at[c], sem.at[c]).start()
         face_ref[c, 0] = l_ref[c, 0]
         face_ref[c, 1] = l_ref[c, nx - 1]
@@ -347,7 +360,7 @@
         pltpu.make_async_copy(l_ref.at[c], out_hbm.at[c], sem.at[c]).wait()
 
 
-def last_kernel(held, count_x, face_ref, xe_ref, xo_ref, mtable_ref, total_ref, old_hbm, m_hbm, v_hbm, new_ref, m_ref, sem):
+def last_kernel(held, count_x, face_ref, xo_ref, xe_ref, mtable_ref, total_ref, old_hbm, m_hbm, v_hbm, new_ref, m_ref, sem):
     comps, nx = v_hbm.shape[:2]
     low, high = beside(xe_ref[...], xo_ref[...], lax.axis_index("gx"), count_x)
     copies = []
@@ -384,10 +397,9 @@
 
 def exchange(even_msg, odd_msg, axis, stride=1):
     both_axes = ("gx", "gy")
-    return (
-        lax.ppermute(even_msg, both_axes, pairs(axis, stride, False)),
-        lax.ppermute(odd_msg, both_axes, pairs(axis, stride, True)),
-    )
+    came_odd = lax.ppermute(odd_msg, both_axes, pairs(axis, stride, True))
+    came_even = lax.ppermute(even_msg, both_axes, pairs(axis, stride, False))
+    return came_even, came_odd
 
 
 def per_device(velocity, velocity_old, station_cell, station_member, drag_coef, inertia_coef, member_velocity,
@@ -407,61 +419,76 @@
     product = 12 * nz * rows * lines[0] * LANES
     table = pltpu.VMEM((2, comps * nz, rows), bf16)
 
-    (v, old, drag, inertia, slot, row, depth, key, low, xkey, xlow, own, s) = call(
-        "start", functools.partial(start_kernel, held, count_y),
+    (v, old, drag, inertia, slot, row, depth, key, low, xkey, xlow, own) = call(
+        "load", functools.partial(load_kernel, held, count_y),
         (velocity, velocity_old, station_cell.reshape(lines), station_member.reshape(lines),
          drag_coef.reshape(lines), inertia_coef.reshape(lines), member_velocity, member_inv_mass.reshape(1, held)),
-        [real(*grid)] * 2 + [one] * 2 + [ints] * 7 + [tile, three],
+        [real(*grid)] * 2 + [one] * 2 + [ints] * 7 + [tile],
         [pltpu.VMEM(lines, i32), pltpu.VMEM(lines, i32), pltpu.VMEM((3, held), f32), pltpu.VMEM((1, held), f32),
-         table, pltpu.SemaphoreType.DMA((8,))],
-        in_hbm=range(8), flops=product,
+         pltpu.SemaphoreType.DMA((8,))],
+        in_hbm=range(8),
     )
     own_even, own_odd = exchange(own, own, "gx")
-    (acc,) = call("old_samples", old_kernel, (old, row, depth, inertia, s), [three], [table], flops=product)
-    work = [pltpu.VMEM((WIDE, WIDE), bf16), pltpu.VMEM((WIDE, WIDE), f32)]
-    edge_parts = [three, tile, spill, face, face]
-    force, mtable, spills, y_even, y_odd = call(
+    s, acc = call(
+        "samples", sample_kernel, (v, old, row, depth, inertia), [three, three],
+        [pltpu.VMEM((2, 2 * comps * nz, rows), bf16), pltpu.VMEM((6,) + lines, f32)], flops=2 * product,
+    )
+    slots = -(-3 * held // 16) * 16
+    work = [pltpu.VMEM((WIDE, WIDE), bf16), pltpu.VMEM((WIDE + slots, WIDE), f32)]
+    edge_parts = [three, tile, spill, face, face, tile]
+    force, mtable, spills, y_even, y_odd, total = call(
         "first_forces", functools.partial(first_kernel, held, count_x),
-        (v, s, acc, slot, drag, key, low, own, own_even, own_odd), edge_parts, work, flops=product // 2,
-    )
-
-    def turn(force, spills, y_even, y_odd):
-        (total,) = call("totals", totals_kernel, (force, slot, y_even), [tile])
-        y_even, y_odd = exchange(y_even, y_odd, "gy")
-        (load,) = call(
-            "deposit", deposit_kernel, (force, row, depth, total), [real(comps, rows, nz)],
-            [pltpu.VMEM((6 * nz, WIDE), bf16), pltpu.VMEM((rows, 6 * nz), f32)], flops=product,
+        (v, s, acc, slot, drag, key, low, own, own_odd, own_even), edge_parts, work, flops=product // 2,
+    )
+
+    def dep_scratch(count):
+        return [pltpu.VMEM((2 * count * nz, WIDE), bf16), pltpu.VMEM((rows, 2 * count * nz), f32)]
+
+    def spread(force, count, after):
+        return call(
+            "deposit", functools.partial(deposit_kernel, range(count)), (force, row, depth, after),
+            [real(count, rows, nz), tile], dep_scratch(count), flops=product * count // comps,
         )
-        x_even, x_odd = call(
-            "turn", functools.partial(turn_kernel, count_y), (spills, y_even, y_odd, total, load), [face, face]
+
+    def turn(spills, y_even, y_odd, total, after):
+        return call(
+            "turn", functools.partial(turn_kernel, count_y), (spills, y_odd, y_even, total, after), [face, face]
         )
-        return total, load, y_even, y_odd, x_even, x_odd
-
-    total, load, y_even, y_odd, x_even, x_odd = turn(force, spills, y_even, y_odd)
+
+    y_even, y_odd = exchange(y_even, y_odd, "gy")
+    load, total = spread(force, comps, total)
     second_even, second_odd = exchange(total, total, "gx", 2)
+    x_even, x_odd = turn(spills, y_even, y_odd, total, load)
     local, samples = call(
-        "middle", functools.partial(middle_kernel, count_y), (v, load, y_even, y_odd, row, depth, x_even),
+        "middle", functools.partial(middle_kernel, count_y), (v, load, y_odd, y_even, row, depth, x_even),
         [real(*grid), three], [table], flops=product,
     )
     x_even, x_odd = exchange(x_even, x_odd, "gx")
     z = nz * 2 * ny // WIDE
-    v, force, mtable, spills, y_even, y_odd = call(
+    v, force, mtable, spills, y_even, y_odd, total = call(
         "second_forces", functools.partial(second_kernel, held, count_x),
-        (local, samples, x_even, x_odd, s, inertia, slot, drag, key, low, xkey, xlow, mtable, total,
+        (local, samples, x_odd, x_even, s, inertia, slot, drag, key, low, xkey, xlow, mtable, total,
          second_even, second_odd),
         [real(*grid)] + edge_parts, work + [pltpu.VMEM((2, comps * z, WIDE), bf16), pltpu.VMEM((3,) + lines, f32)],
         flops=product // 2,
     )
-    total, load, y_even, y_odd, x_even, x_odd = turn(force, spills, y_even, y_odd)
+    y_even, y_odd = exchange(y_even, y_odd, "gy")
+    load, total = spread(force, 2, total)
+    x_even, x_odd = turn(spills, y_even, y_odd, total, load)
+    late = max(comps - 2, 1)
     out, faces = call(
-        "finish", functools.partial(finish_kernel, count_y), (v, load, y_even, y_odd, x_even),
-        [real(*grid), real(comps, 2, ny, nz)], [pltpu.VMEM(grid, f32), pltpu.SemaphoreType.DMA((comps,))],
-        out_hbm=(0,),
+        "finish", functools.partial(finish_kernel, count_y, 2),
+        (v, load, y_odd, y_even, force, row, depth, x_even),
+        [real(*grid), real(comps, 2, ny, nz)],
+        [pltpu.VMEM(grid, f32), pltpu.VMEM((late, rows, nz), f32)] + dep_scratch(late)
+        + [pltpu.SemaphoreType.DMA((comps,))],
+        out_hbm=(0,), flops=product // 3,
     )
     x_even, x_odd = exchange(x_even, x_odd, "gx")
     members, out = call(
-        "last", functools.partial(last_kernel, held, count_x), (faces, x_even, x_odd, mtable, total, out),
-        [real(3, held), real(*grid)], [pltpu.VMEM((2, comps, ny, nz), f32), pltpu.VMEM((3, held), f32), pltpu.SemaphoreType.DMA((3,))],
+        "last", functools.partial(last_kernel, held, count_x), (faces, x_odd, x_even, mtable, total, out),
+        [real(3, held), real(*grid)],
+        [pltpu.VMEM((2, comps, ny, nz), f32), pltpu.VMEM((3, held), f32), pltpu.SemaphoreType.DMA((3,))],
         in_hbm=(5,), out_hbm=(0, 1), aliases={5: 1},
     )
     return out, members

time: 36.6 us -> 33.3 us (0.910)
  the two profiles are of different devices: /device:TPU:8 before, /device:TPU:0 now
where the time goes in v3:
time: 33.3 us; the launch traced here: 33 us
  Pallas kernels  16.7 us (50%)
  starting transfers between devices  14.1 us (42%)
  waiting for transfers between devices  1.45 us (4%)
  between operations  0.79 us (2%)
    pallas_call x11, Pallas kernels, call(): pl.pallas_call(body, name=name, out_shape=outs, in_specs=[HBM if k in in_...  16.7 us
    ppermute x6, starting transfers between devices, exchange(): came_even = lax.ppermute(even_msg, both_axes, pairs(axis, stride, False))  12.4 us
    ppermute x6, starting transfers between devices, exchange(): came_odd = lax.ppermute(odd_msg, both_axes, pairs(axis, stride, True))  1.69 us
    ppermute x6, waiting for transfers between devices, exchange(): came_odd = lax.ppermute(odd_msg, both_axes, pairs(axis, stride, True))  1.44 us
  transfers between devices with their start and end apart: 12, of which 1 were waited for; matrix products, arithmetic and copies ran while one was open for 0% of the time, Pallas kernels for 34%

profile of v3, /device:TPU:0, one launch (start us, length us, event | category | flops | bytes accessed | tf_op | source)
XLA Modules:
  0.0 33.0 jit_solution(14473524875141921403)
XLA Ops:
  0.6 1.3 %load.1 = (f32[3,16,16,128]{3,2,1,0:T(8,128)S(1)}, f32[3,16,16,128]{3,2,1,0:T(8,128)S(1)}, f32[32,128]{1,0:T(8,128)S(1)}, f32[32,128]{1,0:T(8,128)S(1)}, s32[32,...) custom-call(f32[3,16,16,128]{3,2,1,0:T(8,128)} %v_any.1, ...), custom_call_target="tpu_custom_call" | custom-call | bytes 262144 | tf_op jit(solution)/shard_map/load/pallas_call | solution.py:28
  1.9 0.5 %collective-permute-start = (f32[8,128]{1,0:T(8,128)S(1)}, f32[8,128]{1,0:T(8,128)S(1)}, u32[]{:S(2)}, u32[]{:S(2)}) collective-permute-start(f32[8,128]{1,0:T(8,128)S(1)} %get-tuple-element.54.own_ref), channel_id=1, source_target_pairs={{0,1},{1,0},{2,3},{3,2},{4,8},{5,9},{6,10},{7,11},{8,4},{9,5},{10,... | collective-permute-start | bytes 12296 | tf_op jit(solution)/shard_map/ppermute | solution.py:400
  2.5 4.0 %collective-permute-start.1 = (f32[8,128]{1,0:T(8,128)S(1)}, f32[8,128]{1,0:T(8,128)S(1)}, u32[]{:S(2)}, u32[]{:S(2)}) collective-permute-start(f32[8,128]{1,0:T(8,128)S(1)} %get-tuple-element.54.own_ref), channel_id=1, source_target_pairs={{0,4},{1,5},{2,6},{3,7},{4,0},{5,1},{6,2},{7,3},{8,12},{9,13},{10,... | collective-permute-start | bytes 12296 | tf_op jit(solution)/shard_map/ppermute | solution.py:401
  6.5 3.7 %samples.1 = (f32[3,32,128]{2,1,0:T(8,128)S(1)}, f32[3,32,128]{2,1,0:T(8,128)S(1)}) custom-call(f32[3,16,16,128]{3,2,1,0:T(8,128)S(1)} %get-tuple-element.43.v_ref, f32[3,16,16,128]{3,2,1,0:T(8,128)S(1)} %get-tuple-element.44.old_ref, s32[32,128]{1,0:T(8,128)S(1)} %get-tuple-element.45.row_ref, s32[32,128]{1,0:T(8,128)S(1)} %get-tuple-element.46.depth_ref, ...), custom_call_target="tpu_custom_call" | custom-call | flops 3221225472 | bytes 262144 | tf_op jit(solution)/shard_map/samples/pallas_call | solution.py:28
  10.2 0.0 collective-permute-done.odd_ref
  10.2 0.0 collective-permute-done.1.even_ref
  10.2 1.2 %first_forces.1 = (f32[3,32,128]{2,1,0:T(8,128)S(1)}, f32[8,128]{1,0:T(8,128)S(1)}, f32[2,3,16,128]{3,2,1,0:T(8,128)S(1)}, f32[4,16,128]{2,1,0:T(8,128)S(1)}, f3...) custom-call(f32[3,16,16,128]{3,2,1,0:T(8,128)S(1)} %get-tuple-element.43.v_ref, f32[3,32,128]{2,1,0:T(8,128)S(1)} %get-tuple-element.48.s_ref, ...), custom_call_target="tpu_custom_call" | custom-call | flops 805306368 | bytes 262144 | tf_op jit(solution)/shard_map/first_forces/pallas_call | solution.py:28
  11.4 0.5 %collective-permute-start.2 = (f32[4,16,128]{2,1,0:T(8,128)S(1)}, f32[4,16,128]{2,1,0:T(8,128)S(1)}, u32[]{:S(2)}, u32[]{:S(2)}) collective-permute-start(f32[4,16,128]{2,1,0:T(8,128)S(1)} %get-tuple-element.58), channel_id=1, source_target_pairs={{0,3},{1,2},{2,1},{3,0},{4,7},{5,6},{6,5},{7,4},{8,11},{9,10},{10,... | collective-permute-start | bytes 98312 | tf_op jit(solution)/shard_map/ppermute | solution.py:400
  11.9 1.2 %collective-permute-start.3 = (f32[4,16,128]{2,1,0:T(8,128)S(1)}, f32[4,16,128]{2,1,0:T(8,128)S(1)}, u32[]{:S(2)}, u32[]{:S(2)}) collective-permute-start(f32[4,16,128]{2,1,0:T(8,128)S(1)} %get-tuple-element.59), channel_id=1, source_target_pairs={{0,1},{1,0},{2,3},{3,2},{4,5},{5,4},{6,7},{7,6},{8,9},{9,8},{10,11... | collective-permute-start | bytes 98312 | tf_op jit(solution)/shard_map/ppermute | solution.py:401
  13.1 1.8 %deposit.2 = (f32[3,256,128]{2,1,0:T(8,128)S(1)}, f32[8,128]{1,0:T(8,128)S(1)}) custom-call(f32[3,32,128]{2,1,0:T(8,128)S(1)} %get-tuple-element.55.force_ref, s32[32,128]{1,0:T(8,128)S(1)} %get-tuple-element.45.row_ref, s32[32,128]{1,0:T(8,128)S(1)} %get-tuple-element.46.depth_ref, f32[8,128]{1,0:T(8,128)S(1)} %get-tuple-element.56.total_ref), custom_call_target="tpu_custom_call" | custom-call | flops 1610612736 | bytes 262144 | tf_op jit(solution)/shard_map/deposit/pallas_call | solution.py:28
  15.0 1.7 %collective-permute-start.6 = (f32[8,128]{1,0:T(8,128)S(1)}, f32[8,128]{1,0:T(8,128)S(1)}, u32[]{:S(2)}, u32[]{:S(2)}) collective-permute-start(f32[8,128]{1,0:T(8,128)S(1)} %get-tuple-element.61.total_ref.old_total_ref), channel_id=1, source_target_pairs={{0,8},{1,9},{2,10},{3,11},{4,12},{5,13},{6,14},{7,15},{8,0},{9,1},... | collective-permute-start | bytes 12296 | tf_op jit(solution)/shard_map/ppermute | solution.py:401
  16.6 0.0 collective-permute-start.7
  16.6 0.0 collective-permute-done.2.odd_ref
  16.6 0.0 collective-permute-done.3.even_ref
  16.7 0.6 %collective-permute-start.4 = (f32[4,16,128]{2,1,0:T(8,128)S(1)}, f32[4,16,128]{2,1,0:T(8,128)S(1)}, u32[]{:S(2)}, u32[]{:S(2)}) collective-permute-start(f32[4,16,128]{2,1,0:T(8,128)S(1)} %get-tuple-element.65), channel_id=1, source_target_pairs={{0,1},{1,0},{2,3},{3,2},{4,8},{5,9},{6,10},{7,11},{8,4},{9,5},{10,... | collective-permute-start | bytes 98312 | tf_op jit(solution)/shard_map/ppermute | solution.py:400
  17.2 2.6 %collective-permute-start.5 = (f32[4,16,128]{2,1,0:T(8,128)S(1)}, f32[4,16,128]{2,1,0:T(8,128)S(1)}, u32[]{:S(2)}, u32[]{:S(2)}) collective-permute-start(f32[4,16,128]{2,1,0:T(8,128)S(1)} %get-tuple-element.62.after_ref), channel_id=1, source_target_pairs={{0,4},{1,5},{2,6},{3,7},{4,0},{5,1},{6,2},{7,3},{8,12},{9,13},{10,... | collective-permute-start | bytes 98312 | tf_op jit(solution)/shard_map/ppermute | solution.py:401
  19.9 2.6 %middle.1 = (f32[3,16,16,128]{3,2,1,0:T(8,128)S(1)}, f32[3,32,128]{2,1,0:T(8,128)S(1)}) custom-call(f32[3,16,16,128]{3,2,1,0:T(8,128)S(1)} %get-tuple-element.43.v_ref, f32[3,256,128]{2,1,0:T(8,128)S(1)} %get-tuple-element.57.after_ref.load_ref, f32[4,16,128]{2,1,0:T(8,128)S(1)} %collective-permute-done.2.odd_ref, ...), custom_call_target="tpu_custom_call" | custom-call | flops 1610612736 | bytes 262144 | tf_op jit(solution)/shard_map/middle/pallas_call | solution.py:28
  22.5 0.0 collective-permute-done.6.te_ref
  22.5 0.0 collective-permute-done.7.to_ref
  22.5 0.0 collective-permute-done.4.xo_ref
  22.5 0.0 collective-permute-done.5.xe_ref
  22.6 2.0 %second_forces.1 = (f32[3,16,16,128]{3,2,1,0:T(8,128)S(1)}, f32[3,32,128]{2,1,0:T(8,128)S(1)}, f32[8,128]{1,0:T(8,128)S(1)}, f32[2,3,16,128]{3,2,1,0:T(8,128)S(1...) custom-call(f32[3,16,16,128]{3,2,1,0:T(8,128)S(1)} %get-tuple-element.63.l_ref, ...), custom_call_target="tpu_custom_call" | custom-call | flops 805306368 | bytes 262144 | tf_op jit(solution)/shard_map/second_forces/pallas_call | solution.py:28
  24.6 0.1 collective-permute-start.8
  24.6 0.6 %collective-permute-start.9 = (f32[4,16,128]{2,1,0:T(8,128)S(1)}, f32[4,16,128]{2,1,0:T(8,128)S(1)}, u32[]{:S(2)}, u32[]{:S(2)}) collective-permute-start(f32[4,16,128]{2,1,0:T(8,128)S(1)} %get-tuple-element.74), channel_id=1, source_target_pairs={{0,1},{1,0},{2,3},{3,2},{4,5},{5,4},{6,7},{7,6},{8,9},{9,8},{10,11... | collective-permute-start | bytes 98312 | tf_op jit(solution)/shard_map/ppermute | solution.py:401
  25.2 1.3 %deposit.3 = (f32[2,256,128]{2,1,0:T(8,128)S(1)}, f32[8,128]{1,0:T(8,128)S(1)}) custom-call(f32[3,32,128]{2,1,0:T(8,128)S(1)} %get-tuple-element.70.force_ref, s32[32,128]{1,0:T(8,128)S(1)} %get-tuple-element.45.row_ref, s32[32,128]{1,0:T(8,128)S(1)} %get-tuple-element.46.depth_ref, f32[8,128]{1,0:T(8,128)S(1)} %get-tuple-element.71.total_ref), custom_call_target="tpu_custom_call" | custom-call | flops 1073741824 | bytes 262144 | tf_op jit(solution)/shard_map/deposit/pallas_call | solution.py:28
  26.5 1.4 %collective-permute-done.8.odd_ref = f32[4,16,128]{2,1,0:T(8,128)S(1)} collective-permute-done((f32[4,16,128]{2,1,0:T(8,128)S(1)}, f32[4,16,128]{2,1,0:T(8,128)S(1)}, u32[]{:S(2)}, u32[]{:S(2)}) %collective-permute-start.8) | collective-permute-done | bytes 32800 | tf_op jit(solution)/shard_map/ppermute | solution.py:400
  28.0 0.0 collective-permute-done.9.even_ref
  28.0 0.1 collective-permute-start.10
  28.1 2.3 %collective-permute-start.11 = (f32[4,16,128]{2,1,0:T(8,128)S(1)}, f32[4,16,128]{2,1,0:T(8,128)S(1)}, u32[]{:S(2)}, u32[]{:S(2)}) collective-permute-start(f32[4,16,128]{2,1,0:T(8,128)S(1)} %get-tuple-element.77.after_ref), channel_id=1, source_target_pairs={{0,4},{1,5},{2,6},{3,7},{4,0},{5,1},{6,2},{7,3},{8,12},{9,13},{10,... | collective-permute-start | bytes 98312 | tf_op jit(solution)/shard_map/ppermute | solution.py:401
  30.3 1.9 %finish.1 = (f32[3,16,16,128]{3,2,1,0:T(8,128)}, f32[3,2,16,128]{3,2,1,0:T(8,128)S(1)}) custom-call(f32[3,16,16,128]{3,2,1,0:T(8,128)S(1)} %get-tuple-element.69.v_ref, f32[2,256,128]{2,1,0:T(8,128)S(1)} %get-tuple-element.72.after_ref.load_ref, f32[4,16,128]{2,1,0:T(8,128)S(1)} %collective-permute-done.8.odd_ref, ...), custom_call_target="tpu_custom_call" | custom-call | flops 536870912 | bytes 262144 | tf_op jit(solution)/shard_map/finish/pallas_call | solution.py:28
  32.2 0.0 collective-permute-done.10.xo_ref
  32.2 0.0 collective-permute-done.11.xe_ref
  32.3 0.8 %last.1 = (f32[3,16]{1,0:T(4,128)}, f32[3,16,16,128]{3,2,1,0:T(8,128)}) custom-call(f32[3,2,16,128]{3,2,1,0:T(8,128)S(1)} %get-tuple-element.78.face_ref, f32[4,16,128]{2,1,0:T(8,128)S(1)} %collective-permute-done.10.xo_ref, f32[4,16,128]{2,1,0:T(8,128)S(1)} %collective-permute-done.11.xe_ref, ...), custom_call_target="tpu_custom_call", output_to_operand_aliasing={{1}: (5, {})} | custom-call | bytes 262144 | tf_op jit(solution)/shard_map/last/pallas_call | solution.py:28
  (2 shorter events, 0.0 us)
Async XLA Ops:
  1.9 8.2 %collective-permute-start = (f32[8,128]{1,0:T(8,128)S(1)}, f32[8,128]{1,0:T(8,128)S(1)}, u32[]{:S(2)}, u32[]{:S(2)}) collective-permute-start(f32[8,128]{1,0:T(8,128)S(1)} %get-tuple-element.54.own_ref), channel_id=1, source_target_pairs={{0,1},{1,0},{2,3},{3,2},{4,8},{5,9},{6,10},{7,11},{8,4},{9,5},{10,... | collective-permute-start | bytes 12296 | tf_op jit(solution)/shard_map/ppermute | solution.py:400
  2.5 7.7 %collective-permute-start.1 = (f32[8,128]{1,0:T(8,128)S(1)}, f32[8,128]{1,0:T(8,128)S(1)}, u32[]{:S(2)}, u32[]{:S(2)}) collective-permute-start(f32[8,128]{1,0:T(8,128)S(1)} %get-tuple-element.54.own_ref), channel_id=1, source_target_pairs={{0,4},{1,5},{2,6},{3,7},{4,0},{5,1},{6,2},{7,3},{8,12},{9,13},{10,... | collective-permute-start | bytes 12296 | tf_op jit(solution)/shard_map/ppermute | solution.py:401
  11.4 5.2 %collective-permute-start.2 = (f32[4,16,128]{2,1,0:T(8,128)S(1)}, f32[4,16,128]{2,1,0:T(8,128)S(1)}, u32[]{:S(2)}, u32[]{:S(2)}) collective-permute-start(f32[4,16,128]{2,1,0:T(8,128)S(1)} %get-tuple-element.58), channel_id=1, source_target_pairs={{0,3},{1,2},{2,1},{3,0},{4,7},{5,6},{6,5},{7,4},{8,11},{9,10},{10,... | collective-permute-start | bytes 98312 | tf_op jit(solution)/shard_map/ppermute | solution.py:400
  11.9 4.8 %collective-permute-start.3 = (f32[4,16,128]{2,1,0:T(8,128)S(1)}, f32[4,16,128]{2,1,0:T(8,128)S(1)}, u32[]{:S(2)}, u32[]{:S(2)}) collective-permute-start(f32[4,16,128]{2,1,0:T(8,128)S(1)} %get-tuple-element.59), channel_id=1, source_target_pairs={{0,1},{1,0},{2,3},{3,2},{4,5},{5,4},{6,7},{7,6},{8,9},{9,8},{10,11... | collective-permute-start | bytes 98312 | tf_op jit(solution)/shard_map/ppermute | solution.py:401
  15.0 7.5 %collective-permute-start.6 = (f32[8,128]{1,0:T(8,128)S(1)}, f32[8,128]{1,0:T(8,128)S(1)}, u32[]{:S(2)}, u32[]{:S(2)}) collective-permute-start(f32[8,128]{1,0:T(8,128)S(1)} %get-tuple-element.61.total_ref.old_total_ref), channel_id=1, source_target_pairs={{0,8},{1,9},{2,10},{3,11},{4,12},{5,13},{6,14},{7,15},{8,0},{9,1},... | collective-permute-start | bytes 12296 | tf_op jit(solution)/shard_map/ppermute | solution.py:401
  16.6 5.9 %collective-permute-start.7 = (f32[8,128]{1,0:T(8,128)S(1)}, f32[8,128]{1,0:T(8,128)S(1)}, u32[]{:S(2)}, u32[]{:S(2)}) collective-permute-start(f32[8,128]{1,0:T(8,128)S(1)} %get-tuple-element.61.total_ref.old_total_ref), channel_id=1, source_target_pairs={{0,1},{1,0},{2,3},{3,2},{4,5},{5,4},{6,7},{7,6},{8,16},{9,17},{10,... | collective-permute-start | bytes 12296 | tf_op jit(solution)/shard_map/ppermute | solution.py:400
  16.7 5.9 %collective-permute-start.4 = (f32[4,16,128]{2,1,0:T(8,128)S(1)}, f32[4,16,128]{2,1,0:T(8,128)S(1)}, u32[]{:S(2)}, u32[]{:S(2)}) collective-permute-start(f32[4,16,128]{2,1,0:T(8,128)S(1)} %get-tuple-element.65), channel_id=1, source_target_pairs={{0,1},{1,0},{2,3},{3,2},{4,8},{5,9},{6,10},{7,11},{8,4},{9,5},{10,... | collective-permute-start | bytes 98312 | tf_op jit(solution)/shard_map/ppermute | solution.py:400
  17.2 5.3 %collective-permute-start.5 = (f32[4,16,128]{2,1,0:T(8,128)S(1)}, f32[4,16,128]{2,1,0:T(8,128)S(1)}, u32[]{:S(2)}, u32[]{:S(2)}) collective-permute-start(f32[4,16,128]{2,1,0:T(8,128)S(1)} %get-tuple-element.62.after_ref), channel_id=1, source_target_pairs={{0,4},{1,5},{2,6},{3,7},{4,0},{5,1},{6,2},{7,3},{8,12},{9,13},{10,... | collective-permute-start | bytes 98312 | tf_op jit(solution)/shard_map/ppermute | solution.py:401
  24.6 3.4 %collective-permute-start.8 = (f32[4,16,128]{2,1,0:T(8,128)S(1)}, f32[4,16,128]{2,1,0:T(8,128)S(1)}, u32[]{:S(2)}, u32[]{:S(2)}) collective-permute-start(f32[4,16,128]{2,1,0:T(8,128)S(1)} %get-tuple-element.73), channel_id=1, source_target_pairs={{0,3},{1,2},{2,1},{3,0},{4,7},{5,6},{6,5},{7,4},{8,11},{9,10},{10,... | collective-permute-start | bytes 98312 | tf_op jit(solution)/shard_map/ppermute | solution.py:400
  24.6 3.3 %collective-permute-start.9 = (f32[4,16,128]{2,1,0:T(8,128)S(1)}, f32[4,16,128]{2,1,0:T(8,128)S(1)}, u32[]{:S(2)}, u32[]{:S(2)}) collective-permute-start(f32[4,16,128]{2,1,0:T(8,128)S(1)} %get-tuple-element.74), channel_id=1, source_target_pairs={{0,1},{1,0},{2,3},{3,2},{4,5},{5,4},{6,7},{7,6},{8,9},{9,8},{10,11... | collective-permute-start | bytes 98312 | tf_op jit(solution)/shard_map/ppermute | solution.py:401
  28.0 4.2 %collective-permute-start.10 = (f32[4,16,128]{2,1,0:T(8,128)S(1)}, f32[4,16,128]{2,1,0:T(8,128)S(1)}, u32[]{:S(2)}, u32[]{:S(2)}) collective-permute-start(f32[4,16,128]{2,1,0:T(8,128)S(1)} %get-tuple-element.79), channel_id=1, source_target_pairs={{0,1},{1,0},{2,3},{3,2},{4,8},{5,9},{6,10},{7,11},{8,4},{9,5},{10,... | collective-permute-start | bytes 98312 | tf_op jit(solution)/shard_map/ppermute | solution.py:400
  28.1 4.2 %collective-permute-start.11 = (f32[4,16,128]{2,1,0:T(8,128)S(1)}, f32[4,16,128]{2,1,0:T(8,128)S(1)}, u32[]{:S(2)}, u32[]{:S(2)}) collective-permute-start(f32[4,16,128]{2,1,0:T(8,128)S(1)} %get-tuple-element.77.after_ref), channel_id=1, source_target_pairs={{0,4},{1,5},{2,6},{3,7},{4,0},{5,1},{6,2},{7,3},{8,12},{9,13},{10,... | collective-permute-start | bytes 98312 | tf_op jit(solution)/shard_map/ppermute | solution.py:401

commit v4 on v3

--- a/solution.py
+++ b/solution.py
@@ -7,7 +7,6 @@
 from jax.experimental.pallas import tpu as pltpu
 from jax.sharding import PartitionSpec as P
 
-STEPS = 2
 LANES = 128
 WIDE = 256
 
@@ -189,7 +188,9 @@
                 v_ref, old_ref, drag_ref, inertia_ref, slot_ref, row_ref, depth_ref, key_ref, low_ref, xkey_ref,
                 xlow_ref, own_ref, cell_ref, member_ref, mv_ref, mass_ref, sem):
     pairs = [(cell_any, cell_ref), (member_any, member_ref), (mv_any, mv_ref), (mass_any, mass_ref),
-             (drag_any, drag_ref), (inertia_any, inertia_ref), (v_any, v_ref), (old_any, old_ref)]
+             (drag_any, drag_ref), (inertia_any, inertia_ref)]
+    for a, b in ((v_any, v_ref), (old_any, old_ref)):
+        pairs += [(a.at[c], b.at[c]) for c in range(b.shape[0])]
     copies = [pltpu.make_async_copy(a, b, sem.at[k]) for k, (a, b) in enumerate(pairs)]
     for copy in copies:
         copy.start()
@@ -230,14 +231,32 @@
         acc_ref[c] = inertia_ref[...] * (six_ref[c] - six_ref[comps + c])
 
 
-def first_kernel(held, count_x, v_ref, s_ref, acc_ref, slot_ref, drag_ref, key_ref, low_ref, own_ref, odd_ref,
-                 even_ref, force_ref, mtable_ref, spill_ref, ye_ref, yo_ref, total_ref, col_ref, field_ref):
+def first_kernel(held, count_x, v_ref, s_ref, acc_ref, slot_ref, drag_ref, key_ref, low_ref, own_ref, even_ref,
+                 odd_ref, force_ref, mtable_ref, spill_ref, ye_ref, yo_ref, total_ref, col_ref, field_ref):
     low, high = beside(even_ref[...], odd_ref[...], lax.axis_index("gx"), count_x)
     table = low + pltpu.roll(own_ref[...], held, axis=1) + pltpu.roll(high, 2 * held, axis=1)
     mtable_ref[...] = table
     forces([s_ref[c] for c in range(3)], [acc_ref[c] for c in range(3)], slot_ref[...], drag_ref[...], table,
            force_ref)
     edges(v_ref, force_ref, key_ref, low_ref, slot_ref, col_ref, field_ref, spill_ref, (ye_ref, yo_ref), total_ref)
+    comps = v_ref.shape[0]
+    for ref in (ye_ref, yo_ref):
+        ref[comps, 8:16, :] = total_ref[...]
+
+
+def pair_kernel(total_ref, came_ref, after_ref, out_ref):
+    comps = came_ref.shape[0] - 1
+    even = lax.axis_index("gy") % 2 == 0
+    own, other = total_ref[...], came_ref[comps, 8:16, :]
+    out_ref[0:8, :] = jnp.where(even, own, other)
+    out_ref[8:16, :] = jnp.where(even, other, own)
+
+
+def share_kernel(came_ref, after_ref, keep_ref, give_ref):
+    even = lax.axis_index("gy") % 2 == 0
+    first, second = came_ref[0:8, :], came_ref[8:16, :]
+    keep_ref[...] = jnp.where(even, first, second)
+    give_ref[...] = jnp.where(even, second, first)
 
 
 def deposit(comps, force_ref, row_ref, depth_ref, col_ref, acc_ref, out_ref):
@@ -300,11 +319,11 @@
     gather([l_ref[k].reshape(nx * ny, nz) for k in range(comps)], table_ref, row_ref, depth_ref, s_ref)
 
 
-def sum_totals(held, count_x, total, low1, high1, even2, odd2):
+def sum_totals(held, count_x, total, low1, high1, kept, shared):
     own_x = lax.axis_index("gx")
-    even = own_x // 2 % 2 == 0
-    low2 = jnp.where(own_x > 1, jnp.where(even, odd2, even2), 0.0)
-    high2 = jnp.where(own_x < count_x - 2, jnp.where(even, even2, odd2), 0.0)
+    even = lax.axis_index("gy") % 2 == 0
+    low2 = jnp.where(own_x > 1, jnp.where(even, kept, shared), 0.0)
+    high2 = jnp.where(own_x < count_x - 2, jnp.where(even, shared, kept), 0.0)
     lane = lax.broadcasted_iota(i32, (8, LANES), 1)
     total = total + pltpu.roll(low1, LANES - held, axis=1) + pltpu.roll(high1, held, axis=1)
     total = total + jnp.where(lane < held, pltpu.roll(low2, LANES - 2 * held, axis=1), 0.0)
@@ -327,17 +346,17 @@
     for c in range(comps):
         turned = jnp.concatenate([low[c], high[c]], axis=0).T
         wide = jnp.concatenate([turned[h * z : (h + 1) * z] for h in range(nz // z)], axis=1)
-        face_ref[0, c * z : (c + 1) * z, :], face_ref[1, c * z : (c + 1) * z, :] = split(wide)
+        at = comps * z + c * z
+        face_ref[c * z : (c + 1) * z, :], face_ref[at : at + z, :] = split(wide)
     for j in range(xkey_ref.shape[0] // 2):
         hot = hot_rows(wide_row(xkey_ref, j), WIDE)
-        product = jnp.dot(face_ref[0], hot, preferred_element_type=f32)
-        product = product + jnp.dot(face_ref[1], hot, preferred_element_type=f32)
+        product = jnp.dot(face_ref[...], hot, preferred_element_type=f32)
+        product = product[: comps * z] + product[comps * z :]
         for k, found in enumerate(pick(product, wide_row(xlow_ref, j), comps)):
             store_row(sample_ref, k, j, found)
-    v_ref[...] = l_ref[...]
-    for c in range(comps):
-        v_ref[c, 0] += low[c]
-        v_ref[c, nx - 1] += high[c]
+    for c in range(comps):
+        v_ref[c, 0] = l_ref[c, 0] + low[c]
+        v_ref[c, nx - 1] = l_ref[c, nx - 1] + high[c]
     samples = [sp_ref[c] + sample_ref[c] for c in range(comps)]
     acc = [inertia_ref[...] * (samples[c] - s_ref[c]) for c in range(comps)]
     forces(samples, acc, slot_ref[...], drag_ref[...], table, force_ref)
@@ -380,13 +399,13 @@
         copy.wait()
 
 
-def pairs(axis, stride, odd):
+def near_pairs(axis, odd):
     count_x, count_y = lax.axis_size("gx"), lax.axis_size("gy")
     found = []
     for x in range(count_x):
         for y in range(count_y):
             at, count = (x, count_x) if axis == "gx" else (y, count_y)
-            to = ((at + stride) ^ stride) - stride if odd else at ^ stride
+            to = ((at + 1) ^ 1) - 1 if odd else at ^ 1
             if axis == "gy":
                 target = (x, to % count)
             else:
@@ -395,10 +414,21 @@
     return found
 
 
-def exchange(even_msg, odd_msg, axis, stride=1):
+def cross_pairs():
+    count_x, count_y = lax.axis_size("gx"), lax.axis_size("gy")
+    found = []
+    for x in range(count_x):
+        for y in range(count_y):
+            to = x - 2 if y % 2 == 0 else x + 2
+            target = (to, y ^ 1) if 0 <= to < count_x else (x ^ 1, y)
+            found.append((x * count_y + y, target[0] * count_y + target[1]))
+    return found
+
+
+def exchange(even_msg, odd_msg, axis):
     both_axes = ("gx", "gy")
-    came_odd = lax.ppermute(odd_msg, both_axes, pairs(axis, stride, True))
-    came_even = lax.ppermute(even_msg, both_axes, pairs(axis, stride, False))
+    came_odd = lax.ppermute(odd_msg, both_axes, near_pairs(axis, True))
+    came_even = lax.ppermute(even_msg, both_axes, near_pairs(axis, False))
     return came_even, came_odd
 
 
@@ -425,7 +455,7 @@
          drag_coef.reshape(lines), inertia_coef.reshape(lines), member_velocity, member_inv_mass.reshape(1, held)),
         [real(*grid)] * 2 + [one] * 2 + [ints] * 7 + [tile],
         [pltpu.VMEM(lines, i32), pltpu.VMEM(lines, i32), pltpu.VMEM((3, held), f32), pltpu.VMEM((1, held), f32),
-         pltpu.SemaphoreType.DMA((8,))],
+         pltpu.SemaphoreType.DMA((6 + 2 * comps,))],
         in_hbm=range(8),
     )
     own_even, own_odd = exchange(own, own, "gx")
@@ -438,7 +468,7 @@
     edge_parts = [three, tile, spill, face, face, tile]
     force, mtable, spills, y_even, y_odd, total = call(
         "first_forces", functools.partial(first_kernel, held, count_x),
-        (v, s, acc, slot, drag, key, low, own, own_odd, own_even), edge_parts, work, flops=product // 2,
+        (v, s, acc, slot, drag, key, low, own, own_even, own_odd), edge_parts, work, flops=product // 2,
     )
 
     def dep_scratch(count):
@@ -457,10 +487,13 @@
 
     y_even, y_odd = exchange(y_even, y_odd, "gy")
     load, total = spread(force, comps, total)
-    second_even, second_odd = exchange(total, total, "gx", 2)
+    (sums,) = call("pair", pair_kernel, (total, y_even, load), [real(16, LANES)])
+    sums = lax.ppermute(sums, ("gx", "gy"), cross_pairs())
     x_even, x_odd = turn(spills, y_even, y_odd, total, load)
+    kept, given = call("share", share_kernel, (sums, x_even), [tile, tile])
+    shared = lax.ppermute(given, ("gx", "gy"), near_pairs("gy", False))
     local, samples = call(
-        "middle", functools.partial(middle_kernel, count_y), (v, load, y_odd, y_even, row, depth, x_even),
+        "middle", functools.partial(middle_kernel, count_y), (v, load, y_odd, y_even, row, depth, kept),
         [real(*grid), three], [table], flops=product,
     )
     x_even, x_odd = exchange(x_even, x_odd, "gx")
@@ -468,9 +501,9 @@
     v, force, mtable, spills, y_even, y_odd, total = call(
         "second_forces", functools.partial(second_kernel, held, count_x),
         (local, samples, x_odd, x_even, s, inertia, slot, drag, key, low, xkey, xlow, mtable, total,
-         second_even, second_odd),
-        [real(*grid)] + edge_parts, work + [pltpu.VMEM((2, comps * z, WIDE), bf16), pltpu.VMEM((3,) + lines, f32)],
-        flops=product // 2,
+         kept, shared),
+        [real(*grid)] + edge_parts, work + [pltpu.VMEM((2 * comps * z, WIDE), bf16), pltpu.VMEM((3,) + lines, f32)],
+        flops=product // 2, aliases={0: 0},
     )
     y_even, y_odd = exchange(y_even, y_odd, "gy")
     load, total = spread(force, 2, total)

time: 33.3 us -> 32.6 us (0.979)
  starting transfers between devices: 14.1 us -> 12.7 us
  waiting for transfers between devices: 1.45 us -> 2.33 us
    ppermute x12, starting transfers between devices: 14.1 us -> 12.7 us  [the longest x5 8.79 us: exchange(): came_even = lax.ppermute(even_msg, both_axes, near_pairs(axis, False))]
    ppermute x12, waiting for transfers between devices: 1.45 us -> 2.33 us  [the longest x5 1.59 us: exchange(): came_odd = lax.ppermute(odd_msg, both_axes, near_pairs(axis, True))]
    pallas_call x11 -> x13, Pallas kernels: 16.7 us -> 16.5 us  [call(): pl.pallas_call(body, name=name, out_shape=outs, in_specs=[HBM if k in in_...]
  transfers between devices with their start and end apart: 12 -> 12, of which waited for: 1 -> 3; matrix products, arithmetic and copies ran while one was open for 0% -> 0% of each run, Pallas kernels for 34% -> 35%
where the time goes in v4:
time: 32.6 us; the launch traced here: 32.3 us
  Pallas kernels  16.5 us (51%)
  starting transfers between devices  12.7 us (39%)
  waiting for transfers between devices  2.33 us (7%)
  between operations  0.79 us (2%)
    pallas_call x13, Pallas kernels, call(): pl.pallas_call(body, name=name, out_shape=outs, in_specs=[HBM if k in in_...  16.5 us
    ppermute x5, starting transfers between devices, exchange(): came_even = lax.ppermute(even_msg, both_axes, near_pairs(axis, False))  8.79 us
    ppermute x5, starting transfers between devices, exchange(): came_odd = lax.ppermute(odd_msg, both_axes, near_pairs(axis, True))  3.21 us
    ppermute x5, waiting for transfers between devices, exchange(): came_odd = lax.ppermute(odd_msg, both_axes, near_pairs(axis, True))  1.59 us
  transfers between devices with their start and end apart: 12, of which 3 were waited for; matrix products, arithmetic and copies ran while one was open for 0% of the time, Pallas kernels for 35%

profile of v4, /device:TPU:0, one launch (start us, length us, event | category | flops | bytes accessed | tf_op | source)
XLA Modules:
  0.0 32.3 jit_solution(9405959453640170518)
XLA Ops:
  0.6 1.4 %load.1 = (f32[3,16,16,128]{3,2,1,0:T(8,128)S(1)}, f32[3,16,16,128]{3,2,1,0:T(8,128)S(1)}, f32[32,128]{1,0:T(8,128)S(1)}, f32[32,128]{1,0:T(8,128)S(1)}, s32[32,...) custom-call(f32[3,16,16,128]{3,2,1,0:T(8,128)} %v_any.1, ...), custom_call_target="tpu_custom_call" | custom-call | bytes 262144 | tf_op jit(solution)/shard_map/load/pallas_call | solution.py:27
  2.0 0.5 %collective-permute-start.1 = (f32[8,128]{1,0:T(8,128)S(1)}, f32[8,128]{1,0:T(8,128)S(1)}, u32[]{:S(2)}, u32[]{:S(2)}) collective-permute-start(f32[8,128]{1,0:T(8,128)S(1)} %get-tuple-element.56.own_ref), channel_id=1, source_target_pairs={{0,1},{1,0},{2,3},{3,2},{4,8},{5,9},{6,10},{7,11},{8,4},{9,5},{10,... | collective-permute-start | bytes 12296 | tf_op jit(solution)/shard_map/ppermute | solution.py:430
  2.6 4.0 %collective-permute-start = (f32[8,128]{1,0:T(8,128)S(1)}, f32[8,128]{1,0:T(8,128)S(1)}, u32[]{:S(2)}, u32[]{:S(2)}) collective-permute-start(f32[8,128]{1,0:T(8,128)S(1)} %get-tuple-element.56.own_ref), channel_id=1, source_target_pairs={{0,4},{1,5},{2,6},{3,7},{4,0},{5,1},{6,2},{7,3},{8,12},{9,13},{10,... | collective-permute-start | bytes 12296 | tf_op jit(solution)/shard_map/ppermute | solution.py:431
  6.6 3.7 %samples.1 = (f32[3,32,128]{2,1,0:T(8,128)S(1)}, f32[3,32,128]{2,1,0:T(8,128)S(1)}) custom-call(f32[3,16,16,128]{3,2,1,0:T(8,128)S(1)} %get-tuple-element.45.v_ref, f32[3,16,16,128]{3,2,1,0:T(8,128)S(1)} %get-tuple-element.46.old_ref, s32[32,128]{1,0:T(8,128)S(1)} %get-tuple-element.47.row_ref, s32[32,128]{1,0:T(8,128)S(1)} %get-tuple-element.48.depth_ref, ...), custom_call_target="tpu_custom_call" | custom-call | flops 3221225472 | bytes 262144 | tf_op jit(solution)/shard_map/samples/pallas_call | solution.py:27
  10.3 0.0 collective-permute-done.1.odd_ref
  10.3 0.0 collective-permute-done.even_ref
  10.3 1.2 %first_forces.1 = (f32[3,32,128]{2,1,0:T(8,128)S(1)}, f32[8,128]{1,0:T(8,128)S(1)}, f32[2,3,16,128]{3,2,1,0:T(8,128)S(1)}, f32[4,16,128]{2,1,0:T(8,128)S(1)}, f3...) custom-call(f32[3,16,16,128]{3,2,1,0:T(8,128)S(1)} %get-tuple-element.45.v_ref, f32[3,32,128]{2,1,0:T(8,128)S(1)} %get-tuple-element.50.s_ref, ...), custom_call_target="tpu_custom_call" | custom-call | flops 805306368 | bytes 262144 | tf_op jit(solution)/shard_map/first_forces/pallas_call | solution.py:27
  11.5 0.5 %collective-permute-start.2 = (f32[4,16,128]{2,1,0:T(8,128)S(1)}, f32[4,16,128]{2,1,0:T(8,128)S(1)}, u32[]{:S(2)}, u32[]{:S(2)}) collective-permute-start(f32[4,16,128]{2,1,0:T(8,128)S(1)} %get-tuple-element.60), channel_id=1, source_target_pairs={{0,3},{1,2},{2,1},{3,0},{4,7},{5,6},{6,5},{7,4},{8,11},{9,10},{10,... | collective-permute-start | bytes 98312 | tf_op jit(solution)/shard_map/ppermute | solution.py:430
  12.0 1.2 %collective-permute-start.3 = (f32[4,16,128]{2,1,0:T(8,128)S(1)}, f32[4,16,128]{2,1,0:T(8,128)S(1)}, u32[]{:S(2)}, u32[]{:S(2)}) collective-permute-start(f32[4,16,128]{2,1,0:T(8,128)S(1)} %get-tuple-element.61), channel_id=1, source_target_pairs={{0,1},{1,0},{2,3},{3,2},{4,5},{5,4},{6,7},{7,6},{8,9},{9,8},{10,11... | collective-permute-start | bytes 98312 | tf_op jit(solution)/shard_map/ppermute | solution.py:431
  13.2 1.9 %deposit.2 = (f32[3,256,128]{2,1,0:T(8,128)S(1)}, f32[8,128]{1,0:T(8,128)S(1)}) custom-call(f32[3,32,128]{2,1,0:T(8,128)S(1)} %get-tuple-element.57.force_ref, s32[32,128]{1,0:T(8,128)S(1)} %get-tuple-element.47.row_ref, s32[32,128]{1,0:T(8,128)S(1)} %get-tuple-element.48.depth_ref, f32[8,128]{1,0:T(8,128)S(1)} %get-tuple-element.58.total_ref), custom_call_target="tpu_custom_call" | custom-call | flops 1610612736 | bytes 262144 | tf_op jit(solution)/shard_map/deposit/pallas_call | solution.py:27
  15.1 0.0 collective-permute-done.3.came_ref.even_ref
  15.1 0.1 collective-permute-start.4
  15.2 0.0 collective-permute-done.2.odd_ref
  15.3 1.7 %collective-permute-start.5 = (f32[4,16,128]{2,1,0:T(8,128)S(1)}, f32[4,16,128]{2,1,0:T(8,128)S(1)}, u32[]{:S(2)}, u32[]{:S(2)}) collective-permute-start(f32[4,16,128]{2,1,0:T(8,128)S(1)} %get-tuple-element.68), channel_id=1, source_target_pairs={{0,1},{1,0},{2,3},{3,2},{4,8},{5,9},{6,10},{7,11},{8,4},{9,5},{10,... | collective-permute-start | bytes 98312 | tf_op jit(solution)/shard_map/ppermute | solution.py:430
  17.0 1.4 %collective-permute-start.6 = (f32[4,16,128]{2,1,0:T(8,128)S(1)}, f32[4,16,128]{2,1,0:T(8,128)S(1)}, u32[]{:S(2)}, u32[]{:S(2)}) collective-permute-start(f32[4,16,128]{2,1,0:T(8,128)S(1)} %get-tuple-element.64.after_ref), channel_id=1, source_target_pairs={{0,4},{1,5},{2,6},{3,7},{4,0},{5,1},{6,2},{7,3},{8,12},{9,13},{10,... | collective-permute-start | bytes 98312 | tf_op jit(solution)/shard_map/ppermute | solution.py:431
  18.4 0.5 %collective-permute-done.4.came_ref = f32[16,128]{1,0:T(8,128)S(1)} collective-permute-done((f32[16,128]{1,0:T(8,128)S(1)}, f32[16,128]{1,0:T(8,128)S(1)}, u32[]{:S(2)}, u32[]{:S(2)}) %collective-permute-start.4) | collective-permute-done | bytes 8224 | tf_op jit(solution)/shard_map/ppermute | solution.py:491
  18.9 0.6 %collective-permute-start.7 = (f32[8,128]{1,0:T(8,128)S(1)}, f32[8,128]{1,0:T(8,128)S(1)}, u32[]{:S(2)}, u32[]{:S(2)}) collective-permute-start(f32[8,128]{1,0:T(8,128)S(1)} %get-tuple-element.72), channel_id=1, source_target_pairs={{0,1},{1,0},{2,3},{3,2},{4,5},{5,4},{6,7},{7,6},{8,9},{9,8},{10,11... | collective-permute-start | bytes 12296 | tf_op jit(solution)/shard_map/ppermute | solution.py:494
  19.5 2.6 %middle.1 = (f32[3,16,16,128]{3,2,1,0:T(8,128)S(1)}, f32[3,32,128]{2,1,0:T(8,128)S(1)}) custom-call(f32[3,16,16,128]{3,2,1,0:T(8,128)S(1)} %get-tuple-element.45.v_ref, f32[3,256,128]{2,1,0:T(8,128)S(1)} %get-tuple-element.59.after_ref.load_ref, f32[4,16,128]{2,1,0:T(8,128)S(1)} %collective-permute-done.2.odd_ref, ...), custom_call_target="tpu_custom_call" | custom-call | flops 1610612736 | bytes 262144 | tf_op jit(solution)/shard_map/middle/pallas_call | solution.py:27
  22.1 0.0 collective-permute-done.7.to_ref
  22.1 0.0 collective-permute-done.5.xo_ref
  22.1 0.0 collective-permute-done.6.xe_ref
  22.1 1.7 %second_forces.1 = (f32[3,16,16,128]{3,2,1,0:T(8,128)S(1)}, f32[3,32,128]{2,1,0:T(8,128)S(1)}, f32[8,128]{1,0:T(8,128)S(1)}, f32[2,3,16,128]{3,2,1,0:T(8,128)S(1...) custom-call(f32[3,16,16,128]{3,2,1,0:T(8,128)S(1)} %get-tuple-elemen, ...), custom_call_target="tpu_custom_call", output_to_operand_aliasing={{0}: (0, {})} | custom-call | flops 805306368 | bytes 262144 | tf_op jit(solution)/shard_map/second_forces/pallas_call | solution.py:27
  23.8 0.3 collective-permute-start.8
  24.2 0.4 %collective-permute-start.9 = (f32[4,16,128]{2,1,0:T(8,128)S(1)}, f32[4,16,128]{2,1,0:T(8,128)S(1)}, u32[]{:S(2)}, u32[]{:S(2)}) collective-permute-start(f32[4,16,128]{2,1,0:T(8,128)S(1)} %get-tuple-element.78), channel_id=1, source_target_pairs={{0,1},{1,0},{2,3},{3,2},{4,5},{5,4},{6,7},{7,6},{8,9},{9,8},{10,11... | collective-permute-start | bytes 98312 | tf_op jit(solution)/shard_map/ppermute | solution.py:431
  24.5 1.3 %deposit.3 = (f32[2,256,128]{2,1,0:T(8,128)S(1)}, f32[8,128]{1,0:T(8,128)S(1)}) custom-call(f32[3,32,128]{2,1,0:T(8,128)S(1)} %get-tuple-element.74.force_ref, s32[32,128]{1,0:T(8,128)S(1)} %get-tuple-element.47.row_ref, s32[32,128]{1,0:T(8,128)S(1)} %get-tuple-element.48.depth_ref, f32[8,128]{1,0:T(8,128)S(1)} %get-tuple-element.75.total_ref), custom_call_target="tpu_custom_call" | custom-call | flops 1073741824 | bytes 262144 | tf_op jit(solution)/shard_map/deposit/pallas_call | solution.py:27
  25.8 1.6 %collective-permute-done.8.odd_ref = f32[4,16,128]{2,1,0:T(8,128)S(1)} collective-permute-done((f32[4,16,128]{2,1,0:T(8,128)S(1)}, f32[4,16,128]{2,1,0:T(8,128)S(1)}, u32[]{:S(2)}, u32[]{:S(2)}) %collective-permute-start.8) | collective-permute-done | bytes 32800 | tf_op jit(solution)/shard_map/ppermute | solution.py:430
  27.4 0.0 collective-permute-done.9.even_ref
  27.4 0.2 collective-permute-start.10
  27.6 1.8 %collective-permute-start.11 = (f32[4,16,128]{2,1,0:T(8,128)S(1)}, f32[4,16,128]{2,1,0:T(8,128)S(1)}, u32[]{:S(2)}, u32[]{:S(2)}) collective-permute-start(f32[4,16,128]{2,1,0:T(8,128)S(1)} %get-tuple-element.81.after_ref), channel_id=1, source_target_pairs={{0,4},{1,5},{2,6},{3,7},{4,0},{5,1},{6,2},{7,3},{8,12},{9,13},{10,... | collective-permute-start | bytes 98312 | tf_op jit(solution)/shard_map/ppermute | solution.py:431
  29.4 1.9 %finish.1 = (f32[3,16,16,128]{3,2,1,0:T(8,128)}, f32[3,2,16,128]{3,2,1,0:T(8,128)S(1)}) custom-call(f32[3,16,16,128]{3,2,1,0:T(8,128)S(1)} %get-tuple-element.73.v_ref, f32[2,256,128]{2,1,0:T(8,128)S(1)} %get-tuple-element.76.after_ref.load_ref, f32[4,16,128]{2,1,0:T(8,128)S(1)} %collective-permute-done.8.odd_ref, ...), custom_call_target="tpu_custom_call" | custom-call | flops 536870912 | bytes 262144 | tf_op jit(solution)/shard_map/finish/pallas_call | solution.py:27
  31.3 0.0 collective-permute-done.10.xo_ref
  31.3 0.2 collective-permute-done.11.xe_ref
  31.6 0.7 %last.1 = (f32[3,16]{1,0:T(4,128)}, f32[3,16,16,128]{3,2,1,0:T(8,128)}) custom-call(f32[3,2,16,128]{3,2,1,0:T(8,128)S(1)} %get-tuple-element.82.face_ref, f32[4,16,128]{2,1,0:T(8,128)S(1)} %collective-permute-done.10.xo_ref, f32[4,16,128]{2,1,0:T(8,128)S(1)} %collective-permute-done.11.xe_ref, ...), custom_call_target="tpu_custom_call", output_to_operand_aliasing={{1}: (5, {})} | custom-call | bytes 262144 | tf_op jit(solution)/shard_map/last/pallas_call | solution.py:27
  (4 shorter events, 0.1 us)
Async XLA Ops:
  2.0 8.2 %collective-permute-start.1 = (f32[8,128]{1,0:T(8,128)S(1)}, f32[8,128]{1,0:T(8,128)S(1)}, u32[]{:S(2)}, u32[]{:S(2)}) collective-permute-start(f32[8,128]{1,0:T(8,128)S(1)} %get-tuple-element.56.own_ref), channel_id=1, source_target_pairs={{0,1},{1,0},{2,3},{3,2},{4,8},{5,9},{6,10},{7,11},{8,4},{9,5},{10,... | collective-permute-start | bytes 12296 | tf_op jit(solution)/shard_map/ppermute | solution.py:430
  2.6 7.7 %collective-permute-start = (f32[8,128]{1,0:T(8,128)S(1)}, f32[8,128]{1,0:T(8,128)S(1)}, u32[]{:S(2)}, u32[]{:S(2)}) collective-permute-start(f32[8,128]{1,0:T(8,128)S(1)} %get-tuple-element.56.own_ref), channel_id=1, source_target_pairs={{0,4},{1,5},{2,6},{3,7},{4,0},{5,1},{6,2},{7,3},{8,12},{9,13},{10,... | collective-permute-start | bytes 12296 | tf_op jit(solution)/shard_map/ppermute | solution.py:431
  11.5 3.7 %collective-permute-start.2 = (f32[4,16,128]{2,1,0:T(8,128)S(1)}, f32[4,16,128]{2,1,0:T(8,128)S(1)}, u32[]{:S(2)}, u32[]{:S(2)}) collective-permute-start(f32[4,16,128]{2,1,0:T(8,128)S(1)} %get-tuple-element.60), channel_id=1, source_target_pairs={{0,3},{1,2},{2,1},{3,0},{4,7},{5,6},{6,5},{7,4},{8,11},{9,10},{10,... | collective-permute-start | bytes 98312 | tf_op jit(solution)/shard_map/ppermute | solution.py:430
  12.0 3.1 %collective-permute-start.3 = (f32[4,16,128]{2,1,0:T(8,128)S(1)}, f32[4,16,128]{2,1,0:T(8,128)S(1)}, u32[]{:S(2)}, u32[]{:S(2)}) collective-permute-start(f32[4,16,128]{2,1,0:T(8,128)S(1)} %get-tuple-element.61), channel_id=1, source_target_pairs={{0,1},{1,0},{2,3},{3,2},{4,5},{5,4},{6,7},{7,6},{8,9},{9,8},{10,11... | collective-permute-start | bytes 98312 | tf_op jit(solution)/shard_map/ppermute | solution.py:431
  15.1 3.7 %collective-permute-start.4 = (f32[16,128]{1,0:T(8,128)S(1)}, f32[16,128]{1,0:T(8,128)S(1)}, u32[]{:S(2)}, u32[]{:S(2)}) collective-permute-start(f32[16,128]{1,0:T(8,128)S(1)} %pair.1), channel_id=1, source_target_pairs={{0,4},{1,8},{2,6},{3,10},{4,0},{5,12},{6,2},{7,14},{8,1},{9,16},{1... | collective-permute-start | bytes 24584 | tf_op jit(solution)/shard_map/ppermute | solution.py:491
  15.3 6.9 %collective-permute-start.5 = (f32[4,16,128]{2,1,0:T(8,128)S(1)}, f32[4,16,128]{2,1,0:T(8,128)S(1)}, u32[]{:S(2)}, u32[]{:S(2)}) collective-permute-start(f32[4,16,128]{2,1,0:T(8,128)S(1)} %get-tuple-element.68), channel_id=1, source_target_pairs={{0,1},{1,0},{2,3},{3,2},{4,8},{5,9},{6,10},{7,11},{8,4},{9,5},{10,... | collective-permute-start | bytes 98312 | tf_op jit(solution)/shard_map/ppermute | solution.py:430
  17.0 5.2 %collective-permute-start.6 = (f32[4,16,128]{2,1,0:T(8,128)S(1)}, f32[4,16,128]{2,1,0:T(8,128)S(1)}, u32[]{:S(2)}, u32[]{:S(2)}) collective-permute-start(f32[4,16,128]{2,1,0:T(8,128)S(1)} %get-tuple-element.64.after_ref), channel_id=1, source_target_pairs={{0,4},{1,5},{2,6},{3,7},{4,0},{5,1},{6,2},{7,3},{8,12},{9,13},{10,... | collective-permute-start | bytes 98312 | tf_op jit(solution)/shard_map/ppermute | solution.py:431
  18.9 3.3 %collective-permute-start.7 = (f32[8,128]{1,0:T(8,128)S(1)}, f32[8,128]{1,0:T(8,128)S(1)}, u32[]{:S(2)}, u32[]{:S(2)}) collective-permute-start(f32[8,128]{1,0:T(8,128)S(1)} %get-tuple-element.72), channel_id=1, source_target_pairs={{0,1},{1,0},{2,3},{3,2},{4,5},{5,4},{6,7},{7,6},{8,9},{9,8},{10,11... | collective-permute-start | bytes 12296 | tf_op jit(solution)/shard_map/ppermute | solution.py:494
  23.8 3.6 %collective-permute-start.8 = (f32[4,16,128]{2,1,0:T(8,128)S(1)}, f32[4,16,128]{2,1,0:T(8,128)S(1)}, u32[]{:S(2)}, u32[]{:S(2)}) collective-permute-start(f32[4,16,128]{2,1,0:T(8,128)S(1)} %get-tuple-element.77), channel_id=1, source_target_pairs={{0,3},{1,2},{2,1},{3,0},{4,7},{5,6},{6,5},{7,4},{8,11},{9,10},{10,... | collective-permute-start | bytes 98312 | tf_op jit(solution)/shard_map/ppermute | solution.py:430
  24.2 3.2 %collective-permute-start.9 = (f32[4,16,128]{2,1,0:T(8,128)S(1)}, f32[4,16,128]{2,1,0:T(8,128)S(1)}, u32[]{:S(2)}, u32[]{:S(2)}) collective-permute-start(f32[4,16,128]{2,1,0:T(8,128)S(1)} %get-tuple-element.78), channel_id=1, source_target_pairs={{0,1},{1,0},{2,3},{3,2},{4,5},{5,4},{6,7},{7,6},{8,9},{9,8},{10,11... | collective-permute-start | bytes 98312 | tf_op jit(solution)/shard_map/ppermute | solution.py:431
  27.4 3.9 %collective-permute-start.10 = (f32[4,16,128]{2,1,0:T(8,128)S(1)}, f32[4,16,128]{2,1,0:T(8,128)S(1)}, u32[]{:S(2)}, u32[]{:S(2)}) collective-permute-start(f32[4,16,128]{2,1,0:T(8,128)S(1)} %get-tuple-element.83), channel_id=1, source_target_pairs={{0,1},{1,0},{2,3},{3,2},{4,8},{5,9},{6,10},{7,11},{8,4},{9,5},{10,... | collective-permute-start | bytes 98312 | tf_op jit(solution)/shard_map/ppermute | solution.py:430
  27.6 3.9 %collective-permute-start.11 = (f32[4,16,128]{2,1,0:T(8,128)S(1)}, f32[4,16,128]{2,1,0:T(8,128)S(1)}, u32[]{:S(2)}, u32[]{:S(2)}) collective-permute-start(f32[4,16,128]{2,1,0:T(8,128)S(1)} %get-tuple-element.81.after_ref), channel_id=1, source_target_pairs={{0,4},{1,5},{2,6},{3,7},{4,0},{5,1},{6,2},{7,3},{8,12},{9,13},{10,... | collective-permute-start | bytes 98312 | tf_op jit(solution)/shard_map/ppermute | solution.py:431

commit v5 on v4

--- a/solution.py
+++ b/solution.py
@@ -9,6 +9,7 @@
 
 LANES = 128
 WIDE = 256
+FACE_ROWS = 32
 
 viscous = 0.125
 softening = 0.01
@@ -76,10 +77,12 @@
         table_ref[0, k * z : (k + 1) * z, :], table_ref[1, k * z : (k + 1) * z, :] = split(field.T)
     for j in range(row_ref.shape[0] // 2):
         hot = hot_rows(wide_row(row_ref, j), rows)
-        product = jnp.dot(table_ref[0], hot, preferred_element_type=f32)
-        product = product + jnp.dot(table_ref[1], hot, preferred_element_type=f32)
-        for k, row in enumerate(pick(product, wide_row(depth_ref, j), count)):
-            store_row(out_ref, k, j, row)
+        hit = lax.broadcasted_iota(i32, (z, WIDE), 0) == wide_row(depth_ref, j)
+        for k in range(count):
+            part = slice(k * z, (k + 1) * z)
+            product = jnp.dot(table_ref[0, part], hot, preferred_element_type=f32)
+            product = product + jnp.dot(table_ref[1, part], hot, preferred_element_type=f32)
+            store_row(out_ref, k, j, jnp.sum(jnp.where(hit, product, 0.0), axis=0, keepdims=True))
 
 
 def columns(ref, force_ref, depth_row, z, j, groups):
@@ -147,7 +150,6 @@
     found = -found[:WIDE]
     lane = lax.broadcasted_iota(i32, (ring, LANES), 1) // z
     yid = lax.broadcasted_iota(i32, (ny, nz), 0)
-    even = lax.axis_index("gy") % 2 == 0
     for c in range(comps):
         w = jnp.zeros((ring, nz), f32)
         for h in range(parts):
@@ -162,15 +164,67 @@
             face = jnp.where(yid == 0, y_ends[0][x : x + 1], face)
             face = jnp.where(yid == ny - 1, y_ends[1][x : x + 1], face)
             spill_ref[side, c] = 0.25 * smooth(face, 0) + viscous * v_ref[c, x]
-        low, high = [
-            (smooth(0.25 * w_y, 0) + viscous * v_ref[c, :, y, :], 0.0625 * w_y[0:1], 0.0625 * w_y[nx - 1 : nx])
-            for y, w_y in zip((0, ny - 1), y_ends)
-        ]
-        for ref, flip in zip(y_refs, (even, jnp.logical_not(even))):
-            ref[c] = jnp.where(flip, high[0], low[0])
-            for side in range(2):
-                at = 3 * side + c
-                ref[comps, at : at + 1, :] = jnp.where(flip, high[1 + side], low[1 + side])
+        y_messages(v_ref, c, y_ends, y_refs)
+
+
+def faces_of(key_ref, low_ref, slot_ref, force_ref, col_ref, acc_ref, nz):
+    parts = LANES // FACE_ROWS
+    z = nz // parts
+    free = 3 * z
+    slots = acc_ref.shape[0] - LANES
+    for p in range(2):
+        col_ref[p * LANES + free : (p + 1) * LANES, :] = jnp.zeros((LANES - free, WIDE), bf16)
+    for j in range(key_ref.shape[0] // 2):
+        hot = hot_rows(wide_row(key_ref, j), LANES)
+        columns(col_ref, force_ref, wide_row(low_ref, j), z, j, LANES // z)
+        if slot_ref is not None:
+            hot = jnp.concatenate([hot, hot_rows(wide_row(slot_ref, j), slots)], axis=0)
+            pieces = [split(wide_row(force_ref.at[c], j)) for c in range(3)]
+            for p in range(2):
+                rows = [piece[p].astype(f32) for piece in pieces] + [jnp.zeros((13, WIDE), f32)]
+                col_ref[p * LANES + free : p * LANES + free + 16, :] = jnp.concatenate(rows, axis=0).astype(bf16)
+        part = lax.dot_general(hot, col_ref[...], NT, preferred_element_type=f32)
+        acc_ref[...] = part if j == 0 else acc_ref[...] + part
+    found = acc_ref[:, :LANES] + acc_ref[:, LANES:]
+    total = None
+    if slot_ref is not None:
+        sums = jnp.concatenate([found[LANES:], jnp.zeros((LANES - slots, LANES), f32)], axis=0)
+        total = sums.T[free : free + 8]
+    lane = lax.broadcasted_iota(i32, (FACE_ROWS, LANES), 1) // z
+    fields = []
+    for c in range(3):
+        w = jnp.zeros((FACE_ROWS, nz), f32)
+        for h in range(parts):
+            block = -found[h * FACE_ROWS : (h + 1) * FACE_ROWS]
+            by = (h - c) * z % LANES
+            block = pltpu.roll(block, by, axis=1) if by else block
+            w = jnp.where(lane == h, block, w)
+        fields.append(smooth(w, 1))
+    return fields, total
+
+
+def y_messages(v_ref, c, y_ends, y_refs):
+    comps, nx, ny, nz = v_ref.shape
+    even = lax.axis_index("gy") % 2 == 0
+    low, high = [
+        (smooth(0.25 * w_y, 0) + viscous * v_ref[c, :, y, :], 0.0625 * w_y[0:1], 0.0625 * w_y[nx - 1 : nx])
+        for y, w_y in zip((0, ny - 1), y_ends)
+    ]
+    for ref, flip in zip(y_refs, (even, jnp.logical_not(even))):
+        ref[c] = jnp.where(flip, high[0], low[0])
+        for side in range(2):
+            at = 3 * side + c
+            ref[comps, at : at + 1, :] = jnp.where(flip, high[1 + side], low[1 + side])
+
+
+def spill_kernel(v_ref, force_ref, key_ref, low_ref, slot_ref, spill_ref, total_ref, col_ref, acc_ref):
+    comps, nx, ny, nz = v_ref.shape
+    fields, total = faces_of(key_ref, low_ref, slot_ref, force_ref, col_ref, acc_ref, nz)
+    total_ref[...] = total
+    for c in range(comps):
+        for side, x in ((0, 0), (1, nx - 1)):
+            face = fields[c][side * ny : (side + 1) * ny]
+            spill_ref[side, c] = 0.25 * smooth(face, 0) + viscous * v_ref[c, x]
 
 
 def forces(samples, acc, slot, drag, table, force_ref):
@@ -186,11 +240,9 @@
 
 def load_kernel(held, count_y, v_any, old_any, cell_any, member_any, drag_any, inertia_any, mv_any, mass_any,
                 v_ref, old_ref, drag_ref, inertia_ref, slot_ref, row_ref, depth_ref, key_ref, low_ref, xkey_ref,
-                xlow_ref, own_ref, cell_ref, member_ref, mv_ref, mass_ref, sem):
+                xface_ref, yface_ref, xlow_ref, own_ref, cell_ref, member_ref, mv_ref, mass_ref, sem):
     pairs = [(cell_any, cell_ref), (member_any, member_ref), (mv_any, mv_ref), (mass_any, mass_ref),
-             (drag_any, drag_ref), (inertia_any, inertia_ref)]
-    for a, b in ((v_any, v_ref), (old_any, old_ref)):
-        pairs += [(a.at[c], b.at[c]) for c in range(b.shape[0])]
+             (drag_any, drag_ref), (inertia_any, inertia_ref), (v_any, v_ref), (old_any, old_ref)]
     copies = [pltpu.make_async_copy(a, b, sem.at[k]) for k, (a, b) in enumerate(pairs)]
     for copy in copies:
         copy.start()
@@ -207,7 +259,11 @@
     z = nz * ring // WIDE
     key_ref[...] = jnp.where(edge < 0, -1, lax.div(depth, z) * ring + edge)
     low_ref[...] = lax.rem(depth, z)
+    part = lax.div(depth, nz // (LANES // FACE_ROWS)) * FACE_ROWS
+    face = jnp.where(y == 0, x, jnp.where(y == ny - 1, nx + x, -1))
+    yface_ref[...] = jnp.where(face < 0, -1, part + face)
     face = jnp.where(x == 0, y, jnp.where(x == nx - 1, ny + y, -1))
+    xface_ref[...] = jnp.where(face < 0, -1, part + face)
     z = nz * 2 * ny // WIDE
     xkey_ref[...] = jnp.where(face < 0, -1, lax.div(depth, z) * (2 * ny) + face)
     xlow_ref[...] = lax.rem(depth, z)
@@ -330,13 +386,12 @@
     return total + jnp.where(lane // held == 2, pltpu.roll(high2, 2 * held, axis=1), 0.0)
 
 
-def second_kernel(held, count_x, l_ref, sp_ref, xo_ref, xe_ref, s_ref, inertia_ref, slot_ref, drag_ref, key_ref,
-                  low_ref, xkey_ref, xlow_ref, old_table_ref, old_total_ref, te_ref, to_ref,
-                  v_ref, force_ref, mtable_ref, spill_ref, ye_ref, yo_ref, total_ref,
-                  col_ref, field_ref, face_ref, sample_ref):
+def second_kernel(held, count_x, l_ref, sp_ref, xo_ref, xe_ref, s_ref, inertia_ref, slot_ref, drag_ref, xkey_ref,
+                  xlow_ref, yface_ref, low_ref, old_table_ref, old_total_ref, kept_ref, shared_ref,
+                  v_ref, force_ref, mtable_ref, ye_ref, yo_ref, col_ref, acc_ref, face_ref, sample_ref):
     comps, nx, ny, nz = l_ref.shape
     low, high = beside(xe_ref[...], xo_ref[...], lax.axis_index("gx"), count_x)
-    total = sum_totals(held, count_x, old_total_ref[...], low[comps, 0:8], high[comps, 0:8], te_ref[...], to_ref[...])
+    total = sum_totals(held, count_x, old_total_ref[...], low[comps, 0:8], high[comps, 0:8], kept_ref[...], shared_ref[...])
     old = old_table_ref[...]
     row = lax.broadcasted_iota(i32, (8, LANES), 0)
     lane = lax.broadcasted_iota(i32, (8, LANES), 1)
@@ -360,7 +415,9 @@
     samples = [sp_ref[c] + sample_ref[c] for c in range(comps)]
     acc = [inertia_ref[...] * (samples[c] - s_ref[c]) for c in range(comps)]
     forces(samples, acc, slot_ref[...], drag_ref[...], table, force_ref)
-    edges(v_ref, force_ref, key_ref, low_ref, slot_ref, col_ref, field_ref, spill_ref, (ye_ref, yo_ref), total_ref)
+    fields, _ = faces_of(yface_ref, low_ref, None, force_ref, col_ref, acc_ref, nz)
+    for c in range(comps):
+        y_messages(v_ref, c, (fields[c][:nx], fields[c][nx:]), (ye_ref, yo_ref))
 
 
 def finish_kernel(count_y, early, v_ref, load_ref, odd_ref, even_ref, force_ref, row_ref, depth_ref, after_ref,
@@ -449,13 +506,13 @@
     product = 12 * nz * rows * lines[0] * LANES
     table = pltpu.VMEM((2, comps * nz, rows), bf16)
 
-    (v, old, drag, inertia, slot, row, depth, key, low, xkey, xlow, own) = call(
+    (v, old, drag, inertia, slot, row, depth, key, low, xkey, xface, yface, xlow, own) = call(
         "load", functools.partial(load_kernel, held, count_y),
         (velocity, velocity_old, station_cell.reshape(lines), station_member.reshape(lines),
          drag_coef.reshape(lines), inertia_coef.reshape(lines), member_velocity, member_inv_mass.reshape(1, held)),
-        [real(*grid)] * 2 + [one] * 2 + [ints] * 7 + [tile],
+        [real(*grid)] * 2 + [one] * 2 + [ints] * 9 + [tile],
         [pltpu.VMEM(lines, i32), pltpu.VMEM(lines, i32), pltpu.VMEM((3, held), f32), pltpu.VMEM((1, held), f32),
-         pltpu.SemaphoreType.DMA((6 + 2 * comps,))],
+         pltpu.SemaphoreType.DMA((8,))],
         in_hbm=range(8),
     )
     own_even, own_odd = exchange(own, own, "gx")
@@ -498,14 +555,20 @@
     )
     x_even, x_odd = exchange(x_even, x_odd, "gx")
     z = nz * 2 * ny // WIDE
-    v, force, mtable, spills, y_even, y_odd, total = call(
+    v, force, mtable, y_even, y_odd = call(
         "second_forces", functools.partial(second_kernel, held, count_x),
-        (local, samples, x_odd, x_even, s, inertia, slot, drag, key, low, xkey, xlow, mtable, total,
+        (local, samples, x_odd, x_even, s, inertia, slot, drag, xkey, xlow, yface, low, mtable, total,
          kept, shared),
-        [real(*grid)] + edge_parts, work + [pltpu.VMEM((2 * comps * z, WIDE), bf16), pltpu.VMEM((3,) + lines, f32)],
+        [real(*grid), three, tile, face, face],
+        [pltpu.VMEM((WIDE, WIDE), bf16), pltpu.VMEM((LANES, WIDE), f32),
+         pltpu.VMEM((2 * comps * z, WIDE), bf16), pltpu.VMEM((3,) + lines, f32)],
         flops=product // 2, aliases={0: 0},
     )
     y_even, y_odd = exchange(y_even, y_odd, "gy")
+    spills, total = call(
+        "spills", spill_kernel, (v, force, xface, low, slot), [spill, tile],
+        [pltpu.VMEM((WIDE, WIDE), bf16), pltpu.VMEM((LANES + slots, WIDE), f32)], flops=product // 4,
+    )
     load, total = spread(force, 2, total)
     x_even, x_odd = turn(spills, y_even, y_odd, total, load)
     late = max(comps - 2, 1)

time: 32.6 us -> 32.1 us (0.985)
  waiting for transfers between devices: 2.33 us -> 1.05 us
  Pallas kernels: 16.5 us -> 17.1 us
    ppermute x5, waiting for transfers between devices: 1.59 us -> 0.58 us  [exchange(): came_odd = lax.ppermute(odd_msg, both_axes, near_pairs(axis, True))]
    pallas_call x13 -> x14, Pallas kernels: 16.5 us -> 17.1 us  [call(): pl.pallas_call(body, name=name, out_shape=outs, in_specs=[HBM if k in in_...]
  transfers between devices with their start and end apart: 12 -> 12, of which waited for: 3 -> 2; matrix products, arithmetic and copies ran while one was open for 0% -> 0% of each run, Pallas kernels for 35% -> 38%
where the time goes in v5:
time: 32.1 us; the launch traced here: 31.9 us
  Pallas kernels  17.1 us (53%)
  starting transfers between devices  13 us (40%)
  waiting for transfers between devices  1.05 us (3%)
  between operations  0.8 us (2%)
    pallas_call x14, Pallas kernels, call(): pl.pallas_call(body, name=name, out_shape=outs, in_specs=[HBM if k in in_...  17.1 us
    ppermute x5, starting transfers between devices, exchange(): came_even = lax.ppermute(even_msg, both_axes, near_pairs(axis, False))  9.08 us
    ppermute x5, starting transfers between devices, exchange(): came_odd = lax.ppermute(odd_msg, both_axes, near_pairs(axis, True))  3.21 us
  transfers between devices with their start and end apart: 12, of which 2 were waited for; matrix products, arithmetic and copies ran while one was open for 0% of the time, Pallas kernels for 38%

profile of v5, /device:TPU:0, one launch (start us, length us, event | category | flops | bytes accessed | tf_op | source)
XLA Modules:
  0.0 31.9 jit_solution(5498744646514587201)
XLA Ops:
  0.6 1.3 %load.1 = (f32[3,16,16,128]{3,2,1,0:T(8,128)S(1)}, f32[3,16,16,128]{3,2,1,0:T(8,128)S(1)}, f32[32,128]{1,0:T(8,128)S(1)}, f32[32,128]{1,0:T(8,128)S(1)}, s32[32,...) custom-call(f32[3,16,16,128]{3,2,1,0:T(8,128)} %v_any.1, ...), custom_call_target="tpu_custom_call" | custom-call | bytes 262144 | tf_op jit(solution)/shard_map/load/pallas_call | solution.py:28
  1.9 0.5 %collective-permute-start.1 = (f32[8,128]{1,0:T(8,128)S(1)}, f32[8,128]{1,0:T(8,128)S(1)}, u32[]{:S(2)}, u32[]{:S(2)}) collective-permute-start(f32[8,128]{1,0:T(8,128)S(1)} %get-tuple-element.58.own_ref), channel_id=1, source_target_pairs={{0,1},{1,0},{2,3},{3,2},{4,8},{5,9},{6,10},{7,11},{8,4},{9,5},{10,... | collective-permute-start | bytes 12296 | tf_op jit(solution)/shard_map/ppermute | solution.py:487
  2.5 4.0 %collective-permute-start = (f32[8,128]{1,0:T(8,128)S(1)}, f32[8,128]{1,0:T(8,128)S(1)}, u32[]{:S(2)}, u32[]{:S(2)}) collective-permute-start(f32[8,128]{1,0:T(8,128)S(1)} %get-tuple-element.58.own_ref), channel_id=1, source_target_pairs={{0,4},{1,5},{2,6},{3,7},{4,0},{5,1},{6,2},{7,3},{8,12},{9,13},{10,... | collective-permute-start | bytes 12296 | tf_op jit(solution)/shard_map/ppermute | solution.py:488
  6.5 3.6 %samples.1 = (f32[3,32,128]{2,1,0:T(8,128)S(1)}, f32[3,32,128]{2,1,0:T(8,128)S(1)}) custom-call(f32[3,16,16,128]{3,2,1,0:T(8,128)S(1)} %get-tuple-element.47.v_ref, f32[3,16,16,128]{3,2,1,0:T(8,128)S(1)} %get-tuple-element.48.old_ref, s32[32,128]{1,0:T(8,128)S(1)} %get-tuple-element.49.row_ref, s32[32,128]{1,0:T(8,128)S(1)} %get-tuple-element.50.depth_ref, ...), custom_call_target="tpu_custom_call" | custom-call | flops 3221225472 | bytes 262144 | tf_op jit(solution)/shard_map/samples/pallas_call | solution.py:28
  10.1 0.0 collective-permute-done.1.odd_ref
  10.1 0.0 collective-permute-done.even_ref
  10.1 1.2 %first_forces.1 = (f32[3,32,128]{2,1,0:T(8,128)S(1)}, f32[8,128]{1,0:T(8,128)S(1)}, f32[2,3,16,128]{3,2,1,0:T(8,128)S(1)}, f32[4,16,128]{2,1,0:T(8,128)S(1)}, f3...) custom-call(f32[3,16,16,128]{3,2,1,0:T(8,128)S(1)} %get-tuple-element.47.v_ref, f32[3,32,128]{2,1,0:T(8,128)S(1)} %get-tuple-element.52.s_ref, ...), custom_call_target="tpu_custom_call" | custom-call | flops 805306368 | bytes 262144 | tf_op jit(solution)/shard_map/first_forces/pallas_call | solution.py:28
  11.4 0.5 %collective-permute-start.2 = (f32[4,16,128]{2,1,0:T(8,128)S(1)}, f32[4,16,128]{2,1,0:T(8,128)S(1)}, u32[]{:S(2)}, u32[]{:S(2)}) collective-permute-start(f32[4,16,128]{2,1,0:T(8,128)S(1)} %get-tuple-element.62), channel_id=1, source_target_pairs={{0,3},{1,2},{2,1},{3,0},{4,7},{5,6},{6,5},{7,4},{8,11},{9,10},{10,... | collective-permute-start | bytes 98312 | tf_op jit(solution)/shard_map/ppermute | solution.py:487
  11.8 1.2 %collective-permute-start.3 = (f32[4,16,128]{2,1,0:T(8,128)S(1)}, f32[4,16,128]{2,1,0:T(8,128)S(1)}, u32[]{:S(2)}, u32[]{:S(2)}) collective-permute-start(f32[4,16,128]{2,1,0:T(8,128)S(1)} %get-tuple-element.63), channel_id=1, source_target_pairs={{0,1},{1,0},{2,3},{3,2},{4,5},{5,4},{6,7},{7,6},{8,9},{9,8},{10,11... | collective-permute-start | bytes 98312 | tf_op jit(solution)/shard_map/ppermute | solution.py:488
  13.1 1.8 %deposit.2 = (f32[3,256,128]{2,1,0:T(8,128)S(1)}, f32[8,128]{1,0:T(8,128)S(1)}) custom-call(f32[3,32,128]{2,1,0:T(8,128)S(1)} %get-tuple-element.59.force_ref, s32[32,128]{1,0:T(8,128)S(1)} %get-tuple-element.49.row_ref, s32[32,128]{1,0:T(8,128)S(1)} %get-tuple-element.50.depth_ref, f32[8,128]{1,0:T(8,128)S(1)} %get-tuple-element.60.total_ref), custom_call_target="tpu_custom_call" | custom-call | flops 1610612736 | bytes 262144 | tf_op jit(solution)/shard_map/deposit/pallas_call | solution.py:28
  14.9 0.0 collective-permute-done.3.came_ref.even_ref
  15.0 0.1 collective-permute-start.4
  15.0 0.0 collective-permute-done.2.odd_ref
  15.1 1.7 %collective-permute-start.5 = (f32[4,16,128]{2,1,0:T(8,128)S(1)}, f32[4,16,128]{2,1,0:T(8,128)S(1)}, u32[]{:S(2)}, u32[]{:S(2)}) collective-permute-start(f32[4,16,128]{2,1,0:T(8,128)S(1)} %get-tuple-element.70), channel_id=1, source_target_pairs={{0,1},{1,0},{2,3},{3,2},{4,8},{5,9},{6,10},{7,11},{8,4},{9,5},{10,... | collective-permute-start | bytes 98312 | tf_op jit(solution)/shard_map/ppermute | solution.py:487
  16.8 1.4 %collective-permute-start.6 = (f32[4,16,128]{2,1,0:T(8,128)S(1)}, f32[4,16,128]{2,1,0:T(8,128)S(1)}, u32[]{:S(2)}, u32[]{:S(2)}) collective-permute-start(f32[4,16,128]{2,1,0:T(8,128)S(1)} %get-tuple-element.66.after_ref), channel_id=1, source_target_pairs={{0,4},{1,5},{2,6},{3,7},{4,0},{5,1},{6,2},{7,3},{8,12},{9,13},{10,... | collective-permute-start | bytes 98312 | tf_op jit(solution)/shard_map/ppermute | solution.py:488
  18.2 0.5 %collective-permute-done.4.came_ref = f32[16,128]{1,0:T(8,128)S(1)} collective-permute-done((f32[16,128]{1,0:T(8,128)S(1)}, f32[16,128]{1,0:T(8,128)S(1)}, u32[]{:S(2)}, u32[]{:S(2)}) %collective-permute-start.4) | collective-permute-done | bytes 8224 | tf_op jit(solution)/shard_map/ppermute | solution.py:548
  18.7 0.6 %collective-permute-start.7 = (f32[8,128]{1,0:T(8,128)S(1)}, f32[8,128]{1,0:T(8,128)S(1)}, u32[]{:S(2)}, u32[]{:S(2)}) collective-permute-start(f32[8,128]{1,0:T(8,128)S(1)} %get-tuple-element.75), channel_id=1, source_target_pairs={{0,1},{1,0},{2,3},{3,2},{4,5},{5,4},{6,7},{7,6},{8,9},{9,8},{10,11... | collective-permute-start | bytes 12296 | tf_op jit(solution)/shard_map/ppermute | solution.py:551
  19.3 2.5 %middle.1 = (f32[3,16,16,128]{3,2,1,0:T(8,128)S(1)}, f32[3,32,128]{2,1,0:T(8,128)S(1)}) custom-call(f32[3,16,16,128]{3,2,1,0:T(8,128)S(1)} %get-tuple-element.47.v_ref, f32[3,256,128]{2,1,0:T(8,128)S(1)} %get-tuple-element.61.after_ref.load_ref, f32[4,16,128]{2,1,0:T(8,128)S(1)} %collective-permute-done.2.odd_ref, ...), custom_call_target="tpu_custom_call" | custom-call | flops 1610612736 | bytes 262144 | tf_op jit(solution)/shard_map/middle/pallas_call | solution.py:28
  21.8 0.0 collective-permute-done.7.shared_ref
  21.8 0.0 collective-permute-done.5.xo_ref
  21.8 0.0 collective-permute-done.6.xe_ref
  21.9 1.5 %second_forces.1 = (f32[3,16,16,128]{3,2,1,0:T(8,128)S(1)}, f32[3,32,128]{2,1,0:T(8,128)S(1)}, f32[8,128]{1,0:T(8,128)S(1)}, f32[4,16,128]{2,1,0:T(8,128)S(1)}, f32[4,16,128]{2,1,0:T(8,128)S(1)}) custom-call(f32[3,16,16,128]{3,2,1,0:T(8,128)S(1)} %get-tuple-element.68.l_ref, ...), custom_call_target="tpu_custom_call", output_to_operand_aliasing={{0}: (0, {})} | custom-call | flops 805306368 | bytes 262144 | tf_op jit(solution)/shard_map/second_forces/pallas_call | solution.py:28
  23.4 0.3 collective-permute-start.8
  23.7 0.4 %collective-permute-start.9 = (f32[4,16,128]{2,1,0:T(8,128)S(1)}, f32[4,16,128]{2,1,0:T(8,128)S(1)}, u32[]{:S(2)}, u32[]{:S(2)}) collective-permute-start(f32[4,16,128]{2,1,0:T(8,128)S(1)} %get-tuple-element.82), channel_id=1, source_target_pairs={{0,1},{1,0},{2,3},{3,2},{4,5},{5,4},{6,7},{7,6},{8,9},{9,8},{10,11... | collective-permute-start | bytes 98312 | tf_op jit(solution)/shard_map/ppermute | solution.py:488
  24.1 1.0 %spills.1 = (f32[2,3,16,128]{3,2,1,0:T(8,128)S(1)}, f32[8,128]{1,0:T(8,128)S(1)}) custom-call(f32[3,16,16,128]{3,2,1,0:T(8,128)S(1)} %get-tuple-element.76.v_ref, f32[3,32,128]{2,1,0:T(8,128)S(1)} %get-tuple-element.77.force_ref, s32[32,128]{1,0:T(8,128)S(1)} %get-tuple-element.78.key_ref, s32[32,128]{1,0:T(8,128)S(1)} %get-tuple-element.57.low_ref, ...), custom_call_target="tpu_custom_call" | custom-call | flops 402653184 | bytes 262144 | tf_op jit(solution)/shard_map/spills/pallas_call | solution.py:28
  25.1 1.3 %deposit.3 = (f32[2,256,128]{2,1,0:T(8,128)S(1)}, f32[8,128]{1,0:T(8,128)S(1)}) custom-call(f32[3,32,128]{2,1,0:T(8,128)S(1)} %get-tuple-element.77.force_ref, s32[32,128]{1,0:T(8,128)S(1)} %get-tuple-element.49.row_ref, s32[32,128]{1,0:T(8,128)S(1)} %get-tuple-element.50.depth_ref, f32[8,128]{1,0:T(8,128)S(1)} %get-tuple-element.79.total_ref), custom_call_target="tpu_custom_call" | custom-call | flops 1073741824 | bytes 262144 | tf_op jit(solution)/shard_map/deposit/pallas_call | solution.py:28
  26.4 0.6 %collective-permute-done.8.odd_ref = f32[4,16,128]{2,1,0:T(8,128)S(1)} collective-permute-done((f32[4,16,128]{2,1,0:T(8,128)S(1)}, f32[4,16,128]{2,1,0:T(8,128)S(1)}, u32[]{:S(2)}, u32[]{:S(2)}) %collective-permute-start.8) | collective-permute-done | bytes 32800 | tf_op jit(solution)/shard_map/ppermute | solution.py:487
  26.9 0.0 collective-permute-done.9.even_ref
  27.0 0.2 collective-permute-start.10
  27.2 2.0 %collective-permute-start.11 = (f32[4,16,128]{2,1,0:T(8,128)S(1)}, f32[4,16,128]{2,1,0:T(8,128)S(1)}, u32[]{:S(2)}, u32[]{:S(2)}) collective-permute-start(f32[4,16,128]{2,1,0:T(8,128)S(1)} %get-tuple-element.85.after_ref), channel_id=1, source_target_pairs={{0,4},{1,5},{2,6},{3,7},{4,0},{5,1},{6,2},{7,3},{8,12},{9,13},{10,... | collective-permute-start | bytes 98312 | tf_op jit(solution)/shard_map/ppermute | solution.py:488
  29.2 1.9 %finish.1 = (f32[3,16,16,128]{3,2,1,0:T(8,128)}, f32[3,2,16,128]{3,2,1,0:T(8,128)S(1)}) custom-call(f32[3,16,16,128]{3,2,1,0:T(8,128)S(1)} %get-tuple-element.76.v_ref, f32[2,256,128]{2,1,0:T(8,128)S(1)} %get-tuple-element.80.after_ref.load_ref, f32[4,16,128]{2,1,0:T(8,128)S(1)} %collective-permute-done.8.odd_ref, ...), custom_call_target="tpu_custom_call" | custom-call | flops 536870912 | bytes 262144 | tf_op jit(solution)/shard_map/finish/pallas_call | solution.py:28
  31.1 0.0 collective-permute-done.10.xo_ref
  31.1 0.0 collective-permute-done.11.xe_ref
  31.1 0.8 %last.1 = (f32[3,16]{1,0:T(4,128)}, f32[3,16,16,128]{3,2,1,0:T(8,128)}) custom-call(f32[3,2,16,128]{3,2,1,0:T(8,128)S(1)} %get-tuple-element.86.face_ref, f32[4,16,128]{2,1,0:T(8,128)S(1)} %collective-permute-done.10.xo_ref, f32[4,16,128]{2,1,0:T(8,128)S(1)} %collective-permute-done.11.xe_ref, ...), custom_call_target="tpu_custom_call", output_to_operand_aliasing={{1}: (5, {})} | custom-call | bytes 262144 | tf_op jit(solution)/shard_map/last/pallas_call | solution.py:28
  (4 shorter events, 0.1 us)
Async XLA Ops:
  1.9 8.2 %collective-permute-start.1 = (f32[8,128]{1,0:T(8,128)S(1)}, f32[8,128]{1,0:T(8,128)S(1)}, u32[]{:S(2)}, u32[]{:S(2)}) collective-permute-start(f32[8,128]{1,0:T(8,128)S(1)} %get-tuple-element.58.own_ref), channel_id=1, source_target_pairs={{0,1},{1,0},{2,3},{3,2},{4,8},{5,9},{6,10},{7,11},{8,4},{9,5},{10,... | collective-permute-start | bytes 12296 | tf_op jit(solution)/shard_map/ppermute | solution.py:487
  2.5 7.7 %collective-permute-start = (f32[8,128]{1,0:T(8,128)S(1)}, f32[8,128]{1,0:T(8,128)S(1)}, u32[]{:S(2)}, u32[]{:S(2)}) collective-permute-start(f32[8,128]{1,0:T(8,128)S(1)} %get-tuple-element.58.own_ref), channel_id=1, source_target_pairs={{0,4},{1,5},{2,6},{3,7},{4,0},{5,1},{6,2},{7,3},{8,12},{9,13},{10,... | collective-permute-start | bytes 12296 | tf_op jit(solution)/shard_map/ppermute | solution.py:488
  11.4 3.7 %collective-permute-start.2 = (f32[4,16,128]{2,1,0:T(8,128)S(1)}, f32[4,16,128]{2,1,0:T(8,128)S(1)}, u32[]{:S(2)}, u32[]{:S(2)}) collective-permute-start(f32[4,16,128]{2,1,0:T(8,128)S(1)} %get-tuple-element.62), channel_id=1, source_target_pairs={{0,3},{1,2},{2,1},{3,0},{4,7},{5,6},{6,5},{7,4},{8,11},{9,10},{10,... | collective-permute-start | bytes 98312 | tf_op jit(solution)/shard_map/ppermute | solution.py:487
  11.8 3.1 %collective-permute-start.3 = (f32[4,16,128]{2,1,0:T(8,128)S(1)}, f32[4,16,128]{2,1,0:T(8,128)S(1)}, u32[]{:S(2)}, u32[]{:S(2)}) collective-permute-start(f32[4,16,128]{2,1,0:T(8,128)S(1)} %get-tuple-element.63), channel_id=1, source_target_pairs={{0,1},{1,0},{2,3},{3,2},{4,5},{5,4},{6,7},{7,6},{8,9},{9,8},{10,11... | collective-permute-start | bytes 98312 | tf_op jit(solution)/shard_map/ppermute | solution.py:488
  15.0 3.7 %collective-permute-start.4 = (f32[16,128]{1,0:T(8,128)S(1)}, f32[16,128]{1,0:T(8,128)S(1)}, u32[]{:S(2)}, u32[]{:S(2)}) collective-permute-start(f32[16,128]{1,0:T(8,128)S(1)} %pair.1), channel_id=1, source_target_pairs={{0,4},{1,8},{2,6},{3,10},{4,0},{5,12},{6,2},{7,14},{8,1},{9,16},{1... | collective-permute-start | bytes 24584 | tf_op jit(solution)/shard_map/ppermute | solution.py:548
  15.1 6.8 %collective-permute-start.5 = (f32[4,16,128]{2,1,0:T(8,128)S(1)}, f32[4,16,128]{2,1,0:T(8,128)S(1)}, u32[]{:S(2)}, u32[]{:S(2)}) collective-permute-start(f32[4,16,128]{2,1,0:T(8,128)S(1)} %get-tuple-element.70), channel_id=1, source_target_pairs={{0,1},{1,0},{2,3},{3,2},{4,8},{5,9},{6,10},{7,11},{8,4},{9,5},{10,... | collective-permute-start | bytes 98312 | tf_op jit(solution)/shard_map/ppermute | solution.py:487
  16.8 5.0 %collective-permute-start.6 = (f32[4,16,128]{2,1,0:T(8,128)S(1)}, f32[4,16,128]{2,1,0:T(8,128)S(1)}, u32[]{:S(2)}, u32[]{:S(2)}) collective-permute-start(f32[4,16,128]{2,1,0:T(8,128)S(1)} %get-tuple-element.66.after_ref), channel_id=1, source_target_pairs={{0,4},{1,5},{2,6},{3,7},{4,0},{5,1},{6,2},{7,3},{8,12},{9,13},{10,... | collective-permute-start | bytes 98312 | tf_op jit(solution)/shard_map/ppermute | solution.py:488
  18.7 3.1 %collective-permute-start.7 = (f32[8,128]{1,0:T(8,128)S(1)}, f32[8,128]{1,0:T(8,128)S(1)}, u32[]{:S(2)}, u32[]{:S(2)}) collective-permute-start(f32[8,128]{1,0:T(8,128)S(1)} %get-tuple-element.75), channel_id=1, source_target_pairs={{0,1},{1,0},{2,3},{3,2},{4,5},{5,4},{6,7},{7,6},{8,9},{9,8},{10,11... | collective-permute-start | bytes 12296 | tf_op jit(solution)/shard_map/ppermute | solution.py:551
  23.4 3.6 %collective-permute-start.8 = (f32[4,16,128]{2,1,0:T(8,128)S(1)}, f32[4,16,128]{2,1,0:T(8,128)S(1)}, u32[]{:S(2)}, u32[]{:S(2)}) collective-permute-start(f32[4,16,128]{2,1,0:T(8,128)S(1)} %get-tuple-element.81), channel_id=1, source_target_pairs={{0,3},{1,2},{2,1},{3,0},{4,7},{5,6},{6,5},{7,4},{8,11},{9,10},{10,... | collective-permute-start | bytes 98312 | tf_op jit(solution)/shard_map/ppermute | solution.py:487
  23.7 3.3 %collective-permute-start.9 = (f32[4,16,128]{2,1,0:T(8,128)S(1)}, f32[4,16,128]{2,1,0:T(8,128)S(1)}, u32[]{:S(2)}, u32[]{:S(2)}) collective-permute-start(f32[4,16,128]{2,1,0:T(8,128)S(1)} %get-tuple-element.82), channel_id=1, source_target_pairs={{0,1},{1,0},{2,3},{3,2},{4,5},{5,4},{6,7},{7,6},{8,9},{9,8},{10,11... | collective-permute-start | bytes 98312 | tf_op jit(solution)/shard_map/ppermute | solution.py:488
  27.0 4.1 %collective-permute-start.10 = (f32[4,16,128]{2,1,0:T(8,128)S(1)}, f32[4,16,128]{2,1,0:T(8,128)S(1)}, u32[]{:S(2)}, u32[]{:S(2)}) collective-permute-start(f32[4,16,128]{2,1,0:T(8,128)S(1)} %get-tuple-element.87), channel_id=1, source_target_pairs={{0,1},{1,0},{2,3},{3,2},{4,8},{5,9},{6,10},{7,11},{8,4},{9,5},{10,... | collective-permute-start | bytes 98312 | tf_op jit(solution)/shard_map/ppermute | solution.py:487
  27.2 4.0 %collective-permute-start.11 = (f32[4,16,128]{2,1,0:T(8,128)S(1)}, f32[4,16,128]{2,1,0:T(8,128)S(1)}, u32[]{:S(2)}, u32[]{:S(2)}) collective-permute-start(f32[4,16,128]{2,1,0:T(8,128)S(1)} %get-tuple-element.85.after_ref), channel_id=1, source_target_pairs={{0,4},{1,5},{2,6},{3,7},{4,0},{5,1},{6,2},{7,3},{8,12},{9,13},{10,... | collective-permute-start | bytes 98312 | tf_op jit(solution)/shard_map/ppermute | solution.py:488

commit v6 on v5

--- a/solution.py
+++ b/solution.py
@@ -241,9 +241,9 @@
 def load_kernel(held, count_y, v_any, old_any, cell_any, member_any, drag_any, inertia_any, mv_any, mass_any,
                 v_ref, old_ref, drag_ref, inertia_ref, slot_ref, row_ref, depth_ref, key_ref, low_ref, xkey_ref,
                 xface_ref, yface_ref, xlow_ref, own_ref, cell_ref, member_ref, mv_ref, mass_ref, sem):
-    pairs = [(cell_any, cell_ref), (member_any, member_ref), (mv_any, mv_ref), (mass_any, mass_ref),
+    loads = [(cell_any, cell_ref), (member_any, member_ref), (mv_any, mv_ref), (mass_any, mass_ref),
              (drag_any, drag_ref), (inertia_any, inertia_ref), (v_any, v_ref), (old_any, old_ref)]
-    copies = [pltpu.make_async_copy(a, b, sem.at[k]) for k, (a, b) in enumerate(pairs)]
+    copies = [pltpu.make_async_copy(a, b, sem.at[k]) for k, (a, b) in enumerate(loads)]
     for copy in copies:
         copy.start()
     comps, nx, ny, nz = v_ref.shape
@@ -411,6 +411,7 @@
             store_row(sample_ref, k, j, found)
     for c in range(comps):
         v_ref[c, 0] = l_ref[c, 0] + low[c]
+        v_ref[c, 1 : nx - 1] = l_ref[c, 1 : nx - 1]
         v_ref[c, nx - 1] = l_ref[c, nx - 1] + high[c]
     samples = [sp_ref[c] + sample_ref[c] for c in range(comps)]
     acc = [inertia_ref[...] * (samples[c] - s_ref[c]) for c in range(comps)]
@@ -562,7 +563,7 @@
         [real(*grid), three, tile, face, face],
         [pltpu.VMEM((WIDE, WIDE), bf16), pltpu.VMEM((LANES, WIDE), f32),
          pltpu.VMEM((2 * comps * z, WIDE), bf16), pltpu.VMEM((3,) + lines, f32)],
-        flops=product // 2, aliases={0: 0},
+        flops=product // 2,
     )
     y_even, y_odd = exchange(y_even, y_odd, "gy")
     spills, total = call(

time: 32.1 us -> 32.1 us (level)
  no operation moved by 1% of the time
where the time goes in v6:
time: 32.1 us; the launch traced here: 31.9 us
  Pallas kernels  17.1 us (53%)
  starting transfers between devices  13 us (40%)
  waiting for transfers between devices  1.04 us (3%)
  between operations  0.8 us (2%)
    pallas_call x14, Pallas kernels, call(): pl.pallas_call(body, name=name, out_shape=outs, in_specs=[HBM if k in in_...  17.1 us
    ppermute x5, starting transfers between devices, exchange(): came_even = lax.ppermute(even_msg, both_axes, near_pairs(axis, False))  9.08 us
    ppermute x5, starting transfers between devices, exchange(): came_odd = lax.ppermute(odd_msg, both_axes, near_pairs(axis, True))  3.21 us
  transfers between devices with their start and end apart: 12, of which 2 were waited for; matrix products, arithmetic and copies ran while one was open for 0% of the time, Pallas kernels for 38%

profile of v6, /device:TPU:0, one launch (start us, length us, event | category | flops | bytes accessed | tf_op | source)
XLA Modules:
  0.0 31.9 jit_solution(16080969152179659756)
XLA Ops:
  0.6 1.3 %load.1 = (f32[3,16,16,128]{3,2,1,0:T(8,128)S(1)}, f32[3,16,16,128]{3,2,1,0:T(8,128)S(1)}, f32[32,128]{1,0:T(8,128)S(1)}, f32[32,128]{1,0:T(8,128)S(1)}, s32[32,...) custom-call(f32[3,16,16,128]{3,2,1,0:T(8,128)} %v_any.1, ...), custom_call_target="tpu_custom_call" | custom-call | bytes 262144 | tf_op jit(solution)/shard_map/load/pallas_call | solution.py:28
  1.9 0.5 %collective-permute-start.1 = (f32[8,128]{1,0:T(8,128)S(1)}, f32[8,128]{1,0:T(8,128)S(1)}, u32[]{:S(2)}, u32[]{:S(2)}) collective-permute-start(f32[8,128]{1,0:T(8,128)S(1)} %get-tuple-element.58.own_ref), channel_id=1, source_target_pairs={{0,1},{1,0},{2,3},{3,2},{4,8},{5,9},{6,10},{7,11},{8,4},{9,5},{10,... | collective-permute-start | bytes 12296 | tf_op jit(solution)/shard_map/ppermute | solution.py:488
  2.5 4.0 %collective-permute-start = (f32[8,128]{1,0:T(8,128)S(1)}, f32[8,128]{1,0:T(8,128)S(1)}, u32[]{:S(2)}, u32[]{:S(2)}) collective-permute-start(f32[8,128]{1,0:T(8,128)S(1)} %get-tuple-element.58.own_ref), channel_id=1, source_target_pairs={{0,4},{1,5},{2,6},{3,7},{4,0},{5,1},{6,2},{7,3},{8,12},{9,13},{10,... | collective-permute-start | bytes 12296 | tf_op jit(solution)/shard_map/ppermute | solution.py:489
  6.5 3.6 %samples.1 = (f32[3,32,128]{2,1,0:T(8,128)S(1)}, f32[3,32,128]{2,1,0:T(8,128)S(1)}) custom-call(f32[3,16,16,128]{3,2,1,0:T(8,128)S(1)} %get-tuple-element.47.v_ref, f32[3,16,16,128]{3,2,1,0:T(8,128)S(1)} %get-tuple-element.48.old_ref, s32[32,128]{1,0:T(8,128)S(1)} %get-tuple-element.49.row_ref, s32[32,128]{1,0:T(8,128)S(1)} %get-tuple-element.50.depth_ref, ...), custom_call_target="tpu_custom_call" | custom-call | flops 3221225472 | bytes 262144 | tf_op jit(solution)/shard_map/samples/pallas_call | solution.py:28
  10.1 0.0 collective-permute-done.1.odd_ref
  10.1 0.0 collective-permute-done.even_ref
  10.1 1.2 %first_forces.1 = (f32[3,32,128]{2,1,0:T(8,128)S(1)}, f32[8,128]{1,0:T(8,128)S(1)}, f32[2,3,16,128]{3,2,1,0:T(8,128)S(1)}, f32[4,16,128]{2,1,0:T(8,128)S(1)}, f3...) custom-call(f32[3,16,16,128]{3,2,1,0:T(8,128)S(1)} %get-tuple-element.47.v_ref, f32[3,32,128]{2,1,0:T(8,128)S(1)} %get-tuple-element.52.s_ref, ...), custom_call_target="tpu_custom_call" | custom-call | flops 805306368 | bytes 262144 | tf_op jit(solution)/shard_map/first_forces/pallas_call | solution.py:28
  11.4 0.5 %collective-permute-start.2 = (f32[4,16,128]{2,1,0:T(8,128)S(1)}, f32[4,16,128]{2,1,0:T(8,128)S(1)}, u32[]{:S(2)}, u32[]{:S(2)}) collective-permute-start(f32[4,16,128]{2,1,0:T(8,128)S(1)} %get-tuple-element.62), channel_id=1, source_target_pairs={{0,3},{1,2},{2,1},{3,0},{4,7},{5,6},{6,5},{7,4},{8,11},{9,10},{10,... | collective-permute-start | bytes 98312 | tf_op jit(solution)/shard_map/ppermute | solution.py:488
  11.8 1.2 %collective-permute-start.3 = (f32[4,16,128]{2,1,0:T(8,128)S(1)}, f32[4,16,128]{2,1,0:T(8,128)S(1)}, u32[]{:S(2)}, u32[]{:S(2)}) collective-permute-start(f32[4,16,128]{2,1,0:T(8,128)S(1)} %get-tuple-element.63), channel_id=1, source_target_pairs={{0,1},{1,0},{2,3},{3,2},{4,5},{5,4},{6,7},{7,6},{8,9},{9,8},{10,11... | collective-permute-start | bytes 98312 | tf_op jit(solution)/shard_map/ppermute | solution.py:489
  13.1 1.8 %deposit.2 = (f32[3,256,128]{2,1,0:T(8,128)S(1)}, f32[8,128]{1,0:T(8,128)S(1)}) custom-call(f32[3,32,128]{2,1,0:T(8,128)S(1)} %get-tuple-element.59.force_ref, s32[32,128]{1,0:T(8,128)S(1)} %get-tuple-element.49.row_ref, s32[32,128]{1,0:T(8,128)S(1)} %get-tuple-element.50.depth_ref, f32[8,128]{1,0:T(8,128)S(1)} %get-tuple-element.60.total_ref), custom_call_target="tpu_custom_call" | custom-call | flops 1610612736 | bytes 262144 | tf_op jit(solution)/shard_map/deposit/pallas_call | solution.py:28
  14.9 0.0 collective-permute-done.3.came_ref.even_ref
  15.0 0.1 collective-permute-start.4
  15.0 0.0 collective-permute-done.2.odd_ref
  15.1 1.7 %collective-permute-start.5 = (f32[4,16,128]{2,1,0:T(8,128)S(1)}, f32[4,16,128]{2,1,0:T(8,128)S(1)}, u32[]{:S(2)}, u32[]{:S(2)}) collective-permute-start(f32[4,16,128]{2,1,0:T(8,128)S(1)} %get-tuple-element.70), channel_id=1, source_target_pairs={{0,1},{1,0},{2,3},{3,2},{4,8},{5,9},{6,10},{7,11},{8,4},{9,5},{10,... | collective-permute-start | bytes 98312 | tf_op jit(solution)/shard_map/ppermute | solution.py:488
  16.8 1.4 %collective-permute-start.6 = (f32[4,16,128]{2,1,0:T(8,128)S(1)}, f32[4,16,128]{2,1,0:T(8,128)S(1)}, u32[]{:S(2)}, u32[]{:S(2)}) collective-permute-start(f32[4,16,128]{2,1,0:T(8,128)S(1)} %get-tuple-element.66.after_ref), channel_id=1, source_target_pairs={{0,4},{1,5},{2,6},{3,7},{4,0},{5,1},{6,2},{7,3},{8,12},{9,13},{10,... | collective-permute-start | bytes 98312 | tf_op jit(solution)/shard_map/ppermute | solution.py:489
  18.2 0.5 %collective-permute-done.4.came_ref = f32[16,128]{1,0:T(8,128)S(1)} collective-permute-done((f32[16,128]{1,0:T(8,128)S(1)}, f32[16,128]{1,0:T(8,128)S(1)}, u32[]{:S(2)}, u32[]{:S(2)}) %collective-permute-start.4) | collective-permute-done | bytes 8224 | tf_op jit(solution)/shard_map/ppermute | solution.py:549
  18.7 0.6 %collective-permute-start.7 = (f32[8,128]{1,0:T(8,128)S(1)}, f32[8,128]{1,0:T(8,128)S(1)}, u32[]{:S(2)}, u32[]{:S(2)}) collective-permute-start(f32[8,128]{1,0:T(8,128)S(1)} %get-tuple-element.75), channel_id=1, source_target_pairs={{0,1},{1,0},{2,3},{3,2},{4,5},{5,4},{6,7},{7,6},{8,9},{9,8},{10,11... | collective-permute-start | bytes 12296 | tf_op jit(solution)/shard_map/ppermute | solution.py:552
  19.3 2.5 %middle.1 = (f32[3,16,16,128]{3,2,1,0:T(8,128)S(1)}, f32[3,32,128]{2,1,0:T(8,128)S(1)}) custom-call(f32[3,16,16,128]{3,2,1,0:T(8,128)S(1)} %get-tuple-element.47.v_ref, f32[3,256,128]{2,1,0:T(8,128)S(1)} %get-tuple-element.61.after_ref.load_ref, f32[4,16,128]{2,1,0:T(8,128)S(1)} %collective-permute-done.2.odd_ref, ...), custom_call_target="tpu_custom_call" | custom-call | flops 1610612736 | bytes 262144 | tf_op jit(solution)/shard_map/middle/pallas_call | solution.py:28
  21.8 0.0 collective-permute-done.7.shared_ref
  21.8 0.0 collective-permute-done.5.xo_ref
  21.8 0.0 collective-permute-done.6.xe_ref
  21.8 1.5 %second_forces.1 = (f32[3,16,16,128]{3,2,1,0:T(8,128)S(1)}, f32[3,32,128]{2,1,0:T(8,128)S(1)}, f32[8,128]{1,0:T(8,128)S(1)}, f32[4,16,128]{2,1,0:T(8,128)S(1)}, f32[4,16,128]{2,1,0:T(8,128)S(1)}) custom-call(f32[3,16,16,128]{3,2,1,0:T(8,128)S(1)} %get-tuple-element.68.l_ref, f32[3,32,128]{2,1,0:T(8,128)S(1)} %get-tuple-element.69.sp_ref, ...), custom_call_target="tpu_custom_call" | custom-call | flops 805306368 | bytes 262144 | tf_op jit(solution)/shard_map/second_forces/pallas_call | solution.py:28
  23.4 0.3 %collective-permute-start.8 = (f32[4,16,128]{2,1,0:T(8,128)S(1)}, f32[4,16,128]{2,1,0:T(8,128)S(1)}, u32[]{:S(2)}, u32[]{:S(2)}) collective-permute-start(f32[4,16,128]{2,1,0:T(8,128)S(1)} %get-tuple-element.81), channel_id=1, source_target_pairs={{0,3},{1,2},{2,1},{3,0},{4,7},{5,6},{6,5},{7,4},{8,11},{9,10},{10,... | collective-permute-start | bytes 98312 | tf_op jit(solution)/shard_map/ppermute | solution.py:488
  23.7 0.4 %collective-permute-start.9 = (f32[4,16,128]{2,1,0:T(8,128)S(1)}, f32[4,16,128]{2,1,0:T(8,128)S(1)}, u32[]{:S(2)}, u32[]{:S(2)}) collective-permute-start(f32[4,16,128]{2,1,0:T(8,128)S(1)} %get-tuple-element.82), channel_id=1, source_target_pairs={{0,1},{1,0},{2,3},{3,2},{4,5},{5,4},{6,7},{7,6},{8,9},{9,8},{10,11... | collective-permute-start | bytes 98312 | tf_op jit(solution)/shard_map/ppermute | solution.py:489
  24.1 1.0 %spills.1 = (f32[2,3,16,128]{3,2,1,0:T(8,128)S(1)}, f32[8,128]{1,0:T(8,128)S(1)}) custom-call(f32[3,16,16,128]{3,2,1,0:T(8,128)S(1)} %get-tuple-element.76.v_ref, f32[3,32,128]{2,1,0:T(8,128)S(1)} %get-tuple-element.77.force_ref, s32[32,128]{1,0:T(8,128)S(1)} %get-tuple-element.78.key_ref, s32[32,128]{1,0:T(8,128)S(1)} %get-tuple-element.57.low_ref, ...), custom_call_target="tpu_custom_call" | custom-call | flops 402653184 | bytes 262144 | tf_op jit(solution)/shard_map/spills/pallas_call | solution.py:28
  25.1 1.3 %deposit.3 = (f32[2,256,128]{2,1,0:T(8,128)S(1)}, f32[8,128]{1,0:T(8,128)S(1)}) custom-call(f32[3,32,128]{2,1,0:T(8,128)S(1)} %get-tuple-element.77.force_ref, s32[32,128]{1,0:T(8,128)S(1)} %get-tuple-element.49.row_ref, s32[32,128]{1,0:T(8,128)S(1)} %get-tuple-element.50.depth_ref, f32[8,128]{1,0:T(8,128)S(1)} %get-tuple-element.79.total_ref), custom_call_target="tpu_custom_call" | custom-call | flops 1073741824 | bytes 262144 | tf_op jit(solution)/shard_map/deposit/pallas_call | solution.py:28
  26.4 0.5 %collective-permute-done.8.odd_ref = f32[4,16,128]{2,1,0:T(8,128)S(1)} collective-permute-done((f32[4,16,128]{2,1,0:T(8,128)S(1)}, f32[4,16,128]{2,1,0:T(8,128)S(1)}, u32[]{:S(2)}, u32[]{:S(2)}) %collective-permute-start.8) | collective-permute-done | bytes 32800 | tf_op jit(solution)/shard_map/ppermute | solution.py:488
  26.9 0.0 collective-permute-done.9.even_ref
  27.0 0.2 collective-permute-start.10
  27.1 2.0 %collective-permute-start.11 = (f32[4,16,128]{2,1,0:T(8,128)S(1)}, f32[4,16,128]{2,1,0:T(8,128)S(1)}, u32[]{:S(2)}, u32[]{:S(2)}) collective-permute-start(f32[4,16,128]{2,1,0:T(8,128)S(1)} %get-tuple-element.85.after_ref), channel_id=1, source_target_pairs={{0,4},{1,5},{2,6},{3,7},{4,0},{5,1},{6,2},{7,3},{8,12},{9,13},{10,... | collective-permute-start | bytes 98312 | tf_op jit(solution)/shard_map/ppermute | solution.py:489
  29.2 1.9 %finish.1 = (f32[3,16,16,128]{3,2,1,0:T(8,128)}, f32[3,2,16,128]{3,2,1,0:T(8,128)S(1)}) custom-call(f32[3,16,16,128]{3,2,1,0:T(8,128)S(1)} %get-tuple-element.76.v_ref, f32[2,256,128]{2,1,0:T(8,128)S(1)} %get-tuple-element.80.after_ref.load_ref, f32[4,16,128]{2,1,0:T(8,128)S(1)} %collective-permute-done.8.odd_ref, ...), custom_call_target="tpu_custom_call" | custom-call | flops 536870912 | bytes 262144 | tf_op jit(solution)/shard_map/finish/pallas_call | solution.py:28
  31.1 0.0 collective-permute-done.10.xo_ref
  31.1 0.0 collective-permute-done.11.xe_ref
  31.1 0.8 %last.1 = (f32[3,16]{1,0:T(4,128)}, f32[3,16,16,128]{3,2,1,0:T(8,128)}) custom-call(f32[3,2,16,128]{3,2,1,0:T(8,128)S(1)} %get-tuple-element.86.face_ref, f32[4,16,128]{2,1,0:T(8,128)S(1)} %collective-permute-done.10.xo_ref, f32[4,16,128]{2,1,0:T(8,128)S(1)} %collective-permute-done.11.xe_ref, ...), custom_call_target="tpu_custom_call", output_to_operand_aliasing={{1}: (5, {})} | custom-call | bytes 262144 | tf_op jit(solution)/shard_map/last/pallas_call | solution.py:28
  (4 shorter events, 0.1 us)
Async XLA Ops:
  1.9 8.2 %collective-permute-start.1 = (f32[8,128]{1,0:T(8,128)S(1)}, f32[8,128]{1,0:T(8,128)S(1)}, u32[]{:S(2)}, u32[]{:S(2)}) collective-permute-start(f32[8,128]{1,0:T(8,128)S(1)} %get-tuple-element.58.own_ref), channel_id=1, source_target_pairs={{0,1},{1,0},{2,3},{3,2},{4,8},{5,9},{6,10},{7,11},{8,4},{9,5},{10,... | collective-permute-start | bytes 12296 | tf_op jit(solution)/shard_map/ppermute | solution.py:488
  2.5 7.7 %collective-permute-start = (f32[8,128]{1,0:T(8,128)S(1)}, f32[8,128]{1,0:T(8,128)S(1)}, u32[]{:S(2)}, u32[]{:S(2)}) collective-permute-start(f32[8,128]{1,0:T(8,128)S(1)} %get-tuple-element.58.own_ref), channel_id=1, source_target_pairs={{0,4},{1,5},{2,6},{3,7},{4,0},{5,1},{6,2},{7,3},{8,12},{9,13},{10,... | collective-permute-start | bytes 12296 | tf_op jit(solution)/shard_map/ppermute | solution.py:489
  11.4 3.7 %collective-permute-start.2 = (f32[4,16,128]{2,1,0:T(8,128)S(1)}, f32[4,16,128]{2,1,0:T(8,128)S(1)}, u32[]{:S(2)}, u32[]{:S(2)}) collective-permute-start(f32[4,16,128]{2,1,0:T(8,128)S(1)} %get-tuple-element.62), channel_id=1, source_target_pairs={{0,3},{1,2},{2,1},{3,0},{4,7},{5,6},{6,5},{7,4},{8,11},{9,10},{10,... | collective-permute-start | bytes 98312 | tf_op jit(solution)/shard_map/ppermute | solution.py:488
  11.8 3.1 %collective-permute-start.3 = (f32[4,16,128]{2,1,0:T(8,128)S(1)}, f32[4,16,128]{2,1,0:T(8,128)S(1)}, u32[]{:S(2)}, u32[]{:S(2)}) collective-permute-start(f32[4,16,128]{2,1,0:T(8,128)S(1)} %get-tuple-element.63), channel_id=1, source_target_pairs={{0,1},{1,0},{2,3},{3,2},{4,5},{5,4},{6,7},{7,6},{8,9},{9,8},{10,11... | collective-permute-start | bytes 98312 | tf_op jit(solution)/shard_map/ppermute | solution.py:489
  15.0 3.7 %collective-permute-start.4 = (f32[16,128]{1,0:T(8,128)S(1)}, f32[16,128]{1,0:T(8,128)S(1)}, u32[]{:S(2)}, u32[]{:S(2)}) collective-permute-start(f32[16,128]{1,0:T(8,128)S(1)} %pair.1), channel_id=1, source_target_pairs={{0,4},{1,8},{2,6},{3,10},{4,0},{5,12},{6,2},{7,14},{8,1},{9,16},{1... | collective-permute-start | bytes 24584 | tf_op jit(solution)/shard_map/ppermute | solution.py:549
  15.1 6.7 %collective-permute-start.5 = (f32[4,16,128]{2,1,0:T(8,128)S(1)}, f32[4,16,128]{2,1,0:T(8,128)S(1)}, u32[]{:S(2)}, u32[]{:S(2)}) collective-permute-start(f32[4,16,128]{2,1,0:T(8,128)S(1)} %get-tuple-element.70), channel_id=1, source_target_pairs={{0,1},{1,0},{2,3},{3,2},{4,8},{5,9},{6,10},{7,11},{8,4},{9,5},{10,... | collective-permute-start | bytes 98312 | tf_op jit(solution)/shard_map/ppermute | solution.py:488
  16.8 5.0 %collective-permute-start.6 = (f32[4,16,128]{2,1,0:T(8,128)S(1)}, f32[4,16,128]{2,1,0:T(8,128)S(1)}, u32[]{:S(2)}, u32[]{:S(2)}) collective-permute-start(f32[4,16,128]{2,1,0:T(8,128)S(1)} %get-tuple-element.66.after_ref), channel_id=1, source_target_pairs={{0,4},{1,5},{2,6},{3,7},{4,0},{5,1},{6,2},{7,3},{8,12},{9,13},{10,... | collective-permute-start | bytes 98312 | tf_op jit(solution)/shard_map/ppermute | solution.py:489
  18.7 3.1 %collective-permute-start.7 = (f32[8,128]{1,0:T(8,128)S(1)}, f32[8,128]{1,0:T(8,128)S(1)}, u32[]{:S(2)}, u32[]{:S(2)}) collective-permute-start(f32[8,128]{1,0:T(8,128)S(1)} %get-tuple-element.75), channel_id=1, source_target_pairs={{0,1},{1,0},{2,3},{3,2},{4,5},{5,4},{6,7},{7,6},{8,9},{9,8},{10,11... | collective-permute-start | bytes 12296 | tf_op jit(solution)/shard_map/ppermute | solution.py:552
  23.4 3.6 %collective-permute-start.8 = (f32[4,16,128]{2,1,0:T(8,128)S(1)}, f32[4,16,128]{2,1,0:T(8,128)S(1)}, u32[]{:S(2)}, u32[]{:S(2)}) collective-permute-start(f32[4,16,128]{2,1,0:T(8,128)S(1)} %get-tuple-element.81), channel_id=1, source_target_pairs={{0,3},{1,2},{2,1},{3,0},{4,7},{5,6},{6,5},{7,4},{8,11},{9,10},{10,... | collective-permute-start | bytes 98312 | tf_op jit(solution)/shard_map/ppermute | solution.py:488
  23.7 3.2 %collective-permute-start.9 = (f32[4,16,128]{2,1,0:T(8,128)S(1)}, f32[4,16,128]{2,1,0:T(8,128)S(1)}, u32[]{:S(2)}, u32[]{:S(2)}) collective-permute-start(f32[4,16,128]{2,1,0:T(8,128)S(1)} %get-tuple-element.82), channel_id=1, source_target_pairs={{0,1},{1,0},{2,3},{3,2},{4,5},{5,4},{6,7},{7,6},{8,9},{9,8},{10,11... | collective-permute-start | bytes 98312 | tf_op jit(solution)/shard_map/ppermute | solution.py:489
  27.0 4.1 %collective-permute-start.10 = (f32[4,16,128]{2,1,0:T(8,128)S(1)}, f32[4,16,128]{2,1,0:T(8,128)S(1)}, u32[]{:S(2)}, u32[]{:S(2)}) collective-permute-start(f32[4,16,128]{2,1,0:T(8,128)S(1)} %get-tuple-element.87), channel_id=1, source_target_pairs={{0,1},{1,0},{2,3},{3,2},{4,8},{5,9},{6,10},{7,11},{8,4},{9,5},{10,... | collective-permute-start | bytes 98312 | tf_op jit(solution)/shard_map/ppermute | solution.py:488
  27.1 4.0 %collective-permute-start.11 = (f32[4,16,128]{2,1,0:T(8,128)S(1)}, f32[4,16,128]{2,1,0:T(8,128)S(1)}, u32[]{:S(2)}, u32[]{:S(2)}) collective-permute-start(f32[4,16,128]{2,1,0:T(8,128)S(1)} %get-tuple-element.85.after_ref), channel_id=1, source_target_pairs={{0,4},{1,5},{2,6},{3,7},{4,0},{5,1},{6,2},{7,3},{8,12},{9,13},{10,... | collective-permute-start | bytes 98312 | tf_op jit(solution)/shard_map/ppermute | solution.py:489

commit v7 on v6

--- a/solution.py
+++ b/solution.py
@@ -241,13 +241,13 @@
 def load_kernel(held, count_y, v_any, old_any, cell_any, member_any, drag_any, inertia_any, mv_any, mass_any,
                 v_ref, old_ref, drag_ref, inertia_ref, slot_ref, row_ref, depth_ref, key_ref, low_ref, xkey_ref,
                 xface_ref, yface_ref, xlow_ref, own_ref, cell_ref, member_ref, mv_ref, mass_ref, sem):
-    loads = [(cell_any, cell_ref), (member_any, member_ref), (mv_any, mv_ref), (mass_any, mass_ref),
-             (drag_any, drag_ref), (inertia_any, inertia_ref), (v_any, v_ref), (old_any, old_ref)]
+    loads = [(v_any, v_ref), (old_any, old_ref), (cell_any, cell_ref), (member_any, member_ref), (mv_any, mv_ref),
+             (mass_any, mass_ref), (drag_any, drag_ref), (inertia_any, inertia_ref)]
     copies = [pltpu.make_async_copy(a, b, sem.at[k]) for k, (a, b) in enumerate(loads)]
     for copy in copies:
         copy.start()
     comps, nx, ny, nz = v_ref.shape
-    copies[0].wait()
+    copies[2].wait()
     cell = cell_ref[...]
     row, depth = lax.div(cell, nz), lax.rem(cell, nz)
     row_ref[...] = row
@@ -267,11 +267,11 @@
     z = nz * 2 * ny // WIDE
     xkey_ref[...] = jnp.where(face < 0, -1, lax.div(depth, z) * (2 * ny) + face)
     xlow_ref[...] = lax.rem(depth, z)
-    copies[1].wait()
+    copies[3].wait()
     member = member_ref[...]
     owner = lax.div(lax.div(member, held), count_y)
     slot_ref[...] = (owner - lax.axis_index("gx") + 1) * held + lax.rem(member, held)
-    for copy in copies[2:]:
+    for copy in copies[4:] + copies[:2]:
         copy.wait()
     own_ref[...] = jnp.zeros_like(own_ref)
     own_ref[0:3, 0:held] = mv_ref[...]

time: 32.1 us -> 31.9 us (level)
  no operation moved by 1% of the time
where the time goes in v7:
time: 31.9 us; the launch traced here: 31.8 us
  Pallas kernels  16.9 us (53%)
  starting transfers between devices  13 us (41%)
  waiting for transfers between devices  1.03 us (3%)
  between operations  0.79 us (2%)
    pallas_call x14, Pallas kernels, call(): pl.pallas_call(body, name=name, out_shape=outs, in_specs=[HBM if k in in_...  16.9 us
    ppermute x5, starting transfers between devices, exchange(): came_even = lax.ppermute(even_msg, both_axes, near_pairs(axis, False))  9.1 us
    ppermute x5, starting transfers between devices, exchange(): came_odd = lax.ppermute(odd_msg, both_axes, near_pairs(axis, True))  3.21 us
  transfers between devices with their start and end apart: 12, of which 2 were waited for; matrix products, arithmetic and copies ran while one was open for 0% of the time, Pallas kernels for 38%

profile of v7, /device:TPU:0, one launch (start us, length us, event | category | flops | bytes accessed | tf_op | source)
XLA Modules:
  0.0 31.8 jit_solution(6309438602041375403)
XLA Ops:
  0.6 1.2 %load.1 = (f32[3,16,16,128]{3,2,1,0:T(8,128)S(1)}, f32[3,16,16,128]{3,2,1,0:T(8,128)S(1)}, f32[32,128]{1,0:T(8,128)S(1)}, f32[32,128]{1,0:T(8,128)S(1)}, s32[32,...) custom-call(f32[3,16,16,128]{3,2,1,0:T(8,128)} %v_any.1, ...), custom_call_target="tpu_custom_call" | custom-call | bytes 262144 | tf_op jit(solution)/shard_map/load/pallas_call | solution.py:28
  1.8 0.5 %collective-permute-start.1 = (f32[8,128]{1,0:T(8,128)S(1)}, f32[8,128]{1,0:T(8,128)S(1)}, u32[]{:S(2)}, u32[]{:S(2)}) collective-permute-start(f32[8,128]{1,0:T(8,128)S(1)} %get-tuple-element.58.own_ref), channel_id=1, source_target_pairs={{0,1},{1,0},{2,3},{3,2},{4,8},{5,9},{6,10},{7,11},{8,4},{9,5},{10,... | collective-permute-start | bytes 12296 | tf_op jit(solution)/shard_map/ppermute | solution.py:488
  2.4 4.0 %collective-permute-start = (f32[8,128]{1,0:T(8,128)S(1)}, f32[8,128]{1,0:T(8,128)S(1)}, u32[]{:S(2)}, u32[]{:S(2)}) collective-permute-start(f32[8,128]{1,0:T(8,128)S(1)} %get-tuple-element.58.own_ref), channel_id=1, source_target_pairs={{0,4},{1,5},{2,6},{3,7},{4,0},{5,1},{6,2},{7,3},{8,12},{9,13},{10,... | collective-permute-start | bytes 12296 | tf_op jit(solution)/shard_map/ppermute | solution.py:489
  6.4 3.6 %samples.1 = (f32[3,32,128]{2,1,0:T(8,128)S(1)}, f32[3,32,128]{2,1,0:T(8,128)S(1)}) custom-call(f32[3,16,16,128]{3,2,1,0:T(8,128)S(1)} %get-tuple-element.47.v_ref, f32[3,16,16,128]{3,2,1,0:T(8,128)S(1)} %get-tuple-element.48.old_ref, s32[32,128]{1,0:T(8,128)S(1)} %get-tuple-element.49.row_ref, s32[32,128]{1,0:T(8,128)S(1)} %get-tuple-element.50.depth_ref, ...), custom_call_target="tpu_custom_call" | custom-call | flops 3221225472 | bytes 262144 | tf_op jit(solution)/shard_map/samples/pallas_call | solution.py:28
  10.0 0.0 collective-permute-done.1.odd_ref
  10.0 0.0 collective-permute-done.even_ref
  10.0 1.2 %first_forces.1 = (f32[3,32,128]{2,1,0:T(8,128)S(1)}, f32[8,128]{1,0:T(8,128)S(1)}, f32[2,3,16,128]{3,2,1,0:T(8,128)S(1)}, f32[4,16,128]{2,1,0:T(8,128)S(1)}, f3...) custom-call(f32[3,16,16,128]{3,2,1,0:T(8,128)S(1)} %get-tuple-element.47.v_ref, f32[3,32,128]{2,1,0:T(8,128)S(1)} %get-tuple-element.52.s_ref, ...), custom_call_target="tpu_custom_call" | custom-call | flops 805306368 | bytes 262144 | tf_op jit(solution)/shard_map/first_forces/pallas_call | solution.py:28
  11.3 0.5 %collective-permute-start.2 = (f32[4,16,128]{2,1,0:T(8,128)S(1)}, f32[4,16,128]{2,1,0:T(8,128)S(1)}, u32[]{:S(2)}, u32[]{:S(2)}) collective-permute-start(f32[4,16,128]{2,1,0:T(8,128)S(1)} %get-tuple-element.62), channel_id=1, source_target_pairs={{0,3},{1,2},{2,1},{3,0},{4,7},{5,6},{6,5},{7,4},{8,11},{9,10},{10,... | collective-permute-start | bytes 98312 | tf_op jit(solution)/shard_map/ppermute | solution.py:488
  11.7 1.2 %collective-permute-start.3 = (f32[4,16,128]{2,1,0:T(8,128)S(1)}, f32[4,16,128]{2,1,0:T(8,128)S(1)}, u32[]{:S(2)}, u32[]{:S(2)}) collective-permute-start(f32[4,16,128]{2,1,0:T(8,128)S(1)} %get-tuple-element.63), channel_id=1, source_target_pairs={{0,1},{1,0},{2,3},{3,2},{4,5},{5,4},{6,7},{7,6},{8,9},{9,8},{10,11... | collective-permute-start | bytes 98312 | tf_op jit(solution)/shard_map/ppermute | solution.py:489
  13.0 1.8 %deposit.2 = (f32[3,256,128]{2,1,0:T(8,128)S(1)}, f32[8,128]{1,0:T(8,128)S(1)}) custom-call(f32[3,32,128]{2,1,0:T(8,128)S(1)} %get-tuple-element.59.force_ref, s32[32,128]{1,0:T(8,128)S(1)} %get-tuple-element.49.row_ref, s32[32,128]{1,0:T(8,128)S(1)} %get-tuple-element.50.depth_ref, f32[8,128]{1,0:T(8,128)S(1)} %get-tuple-element.60.total_ref), custom_call_target="tpu_custom_call" | custom-call | flops 1610612736 | bytes 262144 | tf_op jit(solution)/shard_map/deposit/pallas_call | solution.py:28
  14.8 0.0 collective-permute-done.3.came_ref.even_ref
  14.9 0.1 collective-permute-start.4
  14.9 0.0 collective-permute-done.2.odd_ref
  15.0 1.7 %collective-permute-start.5 = (f32[4,16,128]{2,1,0:T(8,128)S(1)}, f32[4,16,128]{2,1,0:T(8,128)S(1)}, u32[]{:S(2)}, u32[]{:S(2)}) collective-permute-start(f32[4,16,128]{2,1,0:T(8,128)S(1)} %get-tuple-element.70), channel_id=1, source_target_pairs={{0,1},{1,0},{2,3},{3,2},{4,8},{5,9},{6,10},{7,11},{8,4},{9,5},{10,... | collective-permute-start | bytes 98312 | tf_op jit(solution)/shard_map/ppermute | solution.py:488
  16.7 1.4 %collective-permute-start.6 = (f32[4,16,128]{2,1,0:T(8,128)S(1)}, f32[4,16,128]{2,1,0:T(8,128)S(1)}, u32[]{:S(2)}, u32[]{:S(2)}) collective-permute-start(f32[4,16,128]{2,1,0:T(8,128)S(1)} %get-tuple-element.66.after_ref), channel_id=1, source_target_pairs={{0,4},{1,5},{2,6},{3,7},{4,0},{5,1},{6,2},{7,3},{8,12},{9,13},{10,... | collective-permute-start | bytes 98312 | tf_op jit(solution)/shard_map/ppermute | solution.py:489
  18.1 0.5 %collective-permute-done.4.came_ref = f32[16,128]{1,0:T(8,128)S(1)} collective-permute-done((f32[16,128]{1,0:T(8,128)S(1)}, f32[16,128]{1,0:T(8,128)S(1)}, u32[]{:S(2)}, u32[]{:S(2)}) %collective-permute-start.4) | collective-permute-done | bytes 8224 | tf_op jit(solution)/shard_map/ppermute | solution.py:549
  18.6 0.6 %collective-permute-start.7 = (f32[8,128]{1,0:T(8,128)S(1)}, f32[8,128]{1,0:T(8,128)S(1)}, u32[]{:S(2)}, u32[]{:S(2)}) collective-permute-start(f32[8,128]{1,0:T(8,128)S(1)} %get-tuple-element.75), channel_id=1, source_target_pairs={{0,1},{1,0},{2,3},{3,2},{4,5},{5,4},{6,7},{7,6},{8,9},{9,8},{10,11... | collective-permute-start | bytes 12296 | tf_op jit(solution)/shard_map/ppermute | solution.py:552
  19.2 2.5 %middle.1 = (f32[3,16,16,128]{3,2,1,0:T(8,128)S(1)}, f32[3,32,128]{2,1,0:T(8,128)S(1)}) custom-call(f32[3,16,16,128]{3,2,1,0:T(8,128)S(1)} %get-tuple-element.47.v_ref, f32[3,256,128]{2,1,0:T(8,128)S(1)} %get-tuple-element.61.after_ref.load_ref, f32[4,16,128]{2,1,0:T(8,128)S(1)} %collective-permute-done.2.odd_ref, ...), custom_call_target="tpu_custom_call" | custom-call | flops 1610612736 | bytes 262144 | tf_op jit(solution)/shard_map/middle/pallas_call | solution.py:28
  21.7 0.0 collective-permute-done.7.shared_ref
  21.7 0.0 collective-permute-done.5.xo_ref
  21.7 0.0 collective-permute-done.6.xe_ref
  21.7 1.5 %second_forces.1 = (f32[3,16,16,128]{3,2,1,0:T(8,128)S(1)}, f32[3,32,128]{2,1,0:T(8,128)S(1)}, f32[8,128]{1,0:T(8,128)S(1)}, f32[4,16,128]{2,1,0:T(8,128)S(1)}, f32[4,16,128]{2,1,0:T(8,128)S(1)}) custom-call(f32[3,16,16,128]{3,2,1,0:T(8,128)S(1)} %get-tuple-element.68.l_ref, f32[3,32,128]{2,1,0:T(8,128)S(1)} %get-tuple-element.69.sp_ref, ...), custom_call_target="tpu_custom_call" | custom-call | flops 805306368 | bytes 262144 | tf_op jit(solution)/shard_map/second_forces/pallas_call | solution.py:28
  23.3 0.3 %collective-permute-start.8 = (f32[4,16,128]{2,1,0:T(8,128)S(1)}, f32[4,16,128]{2,1,0:T(8,128)S(1)}, u32[]{:S(2)}, u32[]{:S(2)}) collective-permute-start(f32[4,16,128]{2,1,0:T(8,128)S(1)} %get-tuple-element.81), channel_id=1, source_target_pairs={{0,3},{1,2},{2,1},{3,0},{4,7},{5,6},{6,5},{7,4},{8,11},{9,10},{10,... | collective-permute-start | bytes 98312 | tf_op jit(solution)/shard_map/ppermute | solution.py:488
  23.6 0.4 %collective-permute-start.9 = (f32[4,16,128]{2,1,0:T(8,128)S(1)}, f32[4,16,128]{2,1,0:T(8,128)S(1)}, u32[]{:S(2)}, u32[]{:S(2)}) collective-permute-start(f32[4,16,128]{2,1,0:T(8,128)S(1)} %get-tuple-element.82), channel_id=1, source_target_pairs={{0,1},{1,0},{2,3},{3,2},{4,5},{5,4},{6,7},{7,6},{8,9},{9,8},{10,11... | collective-permute-start | bytes 98312 | tf_op jit(solution)/shard_map/ppermute | solution.py:489
  24.0 1.0 %spills.1 = (f32[2,3,16,128]{3,2,1,0:T(8,128)S(1)}, f32[8,128]{1,0:T(8,128)S(1)}) custom-call(f32[3,16,16,128]{3,2,1,0:T(8,128)S(1)} %get-tuple-element.76.v_ref, f32[3,32,128]{2,1,0:T(8,128)S(1)} %get-tuple-element.77.force_ref, s32[32,128]{1,0:T(8,128)S(1)} %get-tuple-element.78.key_ref, s32[32,128]{1,0:T(8,128)S(1)} %get-tuple-element.57.low_ref, ...), custom_call_target="tpu_custom_call" | custom-call | flops 402653184 | bytes 262144 | tf_op jit(solution)/shard_map/spills/pallas_call | solution.py:28
  25.0 1.3 %deposit.3 = (f32[2,256,128]{2,1,0:T(8,128)S(1)}, f32[8,128]{1,0:T(8,128)S(1)}) custom-call(f32[3,32,128]{2,1,0:T(8,128)S(1)} %get-tuple-element.77.force_ref, s32[32,128]{1,0:T(8,128)S(1)} %get-tuple-element.49.row_ref, s32[32,128]{1,0:T(8,128)S(1)} %get-tuple-element.50.depth_ref, f32[8,128]{1,0:T(8,128)S(1)} %get-tuple-element.79.total_ref), custom_call_target="tpu_custom_call" | custom-call | flops 1073741824 | bytes 262144 | tf_op jit(solution)/shard_map/deposit/pallas_call | solution.py:28
  26.3 0.5 %collective-permute-done.8.odd_ref = f32[4,16,128]{2,1,0:T(8,128)S(1)} collective-permute-done((f32[4,16,128]{2,1,0:T(8,128)S(1)}, f32[4,16,128]{2,1,0:T(8,128)S(1)}, u32[]{:S(2)}, u32[]{:S(2)}) %collective-permute-start.8) | collective-permute-done | bytes 32800 | tf_op jit(solution)/shard_map/ppermute | solution.py:488
  26.8 0.0 collective-permute-done.9.even_ref
  26.9 0.2 collective-permute-start.10
  27.0 2.1 %collective-permute-start.11 = (f32[4,16,128]{2,1,0:T(8,128)S(1)}, f32[4,16,128]{2,1,0:T(8,128)S(1)}, u32[]{:S(2)}, u32[]{:S(2)}) collective-permute-start(f32[4,16,128]{2,1,0:T(8,128)S(1)} %get-tuple-element.85.after_ref), channel_id=1, source_target_pairs={{0,4},{1,5},{2,6},{3,7},{4,0},{5,1},{6,2},{7,3},{8,12},{9,13},{10,... | collective-permute-start | bytes 98312 | tf_op jit(solution)/shard_map/ppermute | solution.py:489
  29.1 1.9 %finish.1 = (f32[3,16,16,128]{3,2,1,0:T(8,128)}, f32[3,2,16,128]{3,2,1,0:T(8,128)S(1)}) custom-call(f32[3,16,16,128]{3,2,1,0:T(8,128)S(1)} %get-tuple-element.76.v_ref, f32[2,256,128]{2,1,0:T(8,128)S(1)} %get-tuple-element.80.after_ref.load_ref, f32[4,16,128]{2,1,0:T(8,128)S(1)} %collective-permute-done.8.odd_ref, ...), custom_call_target="tpu_custom_call" | custom-call | flops 536870912 | bytes 262144 | tf_op jit(solution)/shard_map/finish/pallas_call | solution.py:28
  31.0 0.0 collective-permute-done.10.xo_ref
  31.0 0.0 collective-permute-done.11.xe_ref
  31.0 0.8 %last.1 = (f32[3,16]{1,0:T(4,128)}, f32[3,16,16,128]{3,2,1,0:T(8,128)}) custom-call(f32[3,2,16,128]{3,2,1,0:T(8,128)S(1)} %get-tuple-element.86.face_ref, f32[4,16,128]{2,1,0:T(8,128)S(1)} %collective-permute-done.10.xo_ref, f32[4,16,128]{2,1,0:T(8,128)S(1)} %collective-permute-done.11.xe_ref, ...), custom_call_target="tpu_custom_call", output_to_operand_aliasing={{1}: (5, {})} | custom-call | bytes 262144 | tf_op jit(solution)/shard_map/last/pallas_call | solution.py:28
  (4 shorter events, 0.1 us)
Async XLA Ops:
  1.8 8.2 %collective-permute-start.1 = (f32[8,128]{1,0:T(8,128)S(1)}, f32[8,128]{1,0:T(8,128)S(1)}, u32[]{:S(2)}, u32[]{:S(2)}) collective-permute-start(f32[8,128]{1,0:T(8,128)S(1)} %get-tuple-element.58.own_ref), channel_id=1, source_target_pairs={{0,1},{1,0},{2,3},{3,2},{4,8},{5,9},{6,10},{7,11},{8,4},{9,5},{10,... | collective-permute-start | bytes 12296 | tf_op jit(solution)/shard_map/ppermute | solution.py:488
  2.4 7.7 %collective-permute-start = (f32[8,128]{1,0:T(8,128)S(1)}, f32[8,128]{1,0:T(8,128)S(1)}, u32[]{:S(2)}, u32[]{:S(2)}) collective-permute-start(f32[8,128]{1,0:T(8,128)S(1)} %get-tuple-element.58.own_ref), channel_id=1, source_target_pairs={{0,4},{1,5},{2,6},{3,7},{4,0},{5,1},{6,2},{7,3},{8,12},{9,13},{10,... | collective-permute-start | bytes 12296 | tf_op jit(solution)/shard_map/ppermute | solution.py:489
  11.3 3.7 %collective-permute-start.2 = (f32[4,16,128]{2,1,0:T(8,128)S(1)}, f32[4,16,128]{2,1,0:T(8,128)S(1)}, u32[]{:S(2)}, u32[]{:S(2)}) collective-permute-start(f32[4,16,128]{2,1,0:T(8,128)S(1)} %get-tuple-element.62), channel_id=1, source_target_pairs={{0,3},{1,2},{2,1},{3,0},{4,7},{5,6},{6,5},{7,4},{8,11},{9,10},{10,... | collective-permute-start | bytes 98312 | tf_op jit(solution)/shard_map/ppermute | solution.py:488
  11.7 3.1 %collective-permute-start.3 = (f32[4,16,128]{2,1,0:T(8,128)S(1)}, f32[4,16,128]{2,1,0:T(8,128)S(1)}, u32[]{:S(2)}, u32[]{:S(2)}) collective-permute-start(f32[4,16,128]{2,1,0:T(8,128)S(1)} %get-tuple-element.63), channel_id=1, source_target_pairs={{0,1},{1,0},{2,3},{3,2},{4,5},{5,4},{6,7},{7,6},{8,9},{9,8},{10,11... | collective-permute-start | bytes 98312 | tf_op jit(solution)/shard_map/ppermute | solution.py:489
  14.9 3.7 %collective-permute-start.4 = (f32[16,128]{1,0:T(8,128)S(1)}, f32[16,128]{1,0:T(8,128)S(1)}, u32[]{:S(2)}, u32[]{:S(2)}) collective-permute-start(f32[16,128]{1,0:T(8,128)S(1)} %pair.1), channel_id=1, source_target_pairs={{0,4},{1,8},{2,6},{3,10},{4,0},{5,12},{6,2},{7,14},{8,1},{9,16},{1... | collective-permute-start | bytes 24584 | tf_op jit(solution)/shard_map/ppermute | solution.py:549
  15.0 6.7 %collective-permute-start.5 = (f32[4,16,128]{2,1,0:T(8,128)S(1)}, f32[4,16,128]{2,1,0:T(8,128)S(1)}, u32[]{:S(2)}, u32[]{:S(2)}) collective-permute-start(f32[4,16,128]{2,1,0:T(8,128)S(1)} %get-tuple-element.70), channel_id=1, source_target_pairs={{0,1},{1,0},{2,3},{3,2},{4,8},{5,9},{6,10},{7,11},{8,4},{9,5},{10,... | collective-permute-start | bytes 98312 | tf_op jit(solution)/shard_map/ppermute | solution.py:488
  16.7 5.0 %collective-permute-start.6 = (f32[4,16,128]{2,1,0:T(8,128)S(1)}, f32[4,16,128]{2,1,0:T(8,128)S(1)}, u32[]{:S(2)}, u32[]{:S(2)}) collective-permute-start(f32[4,16,128]{2,1,0:T(8,128)S(1)} %get-tuple-element.66.after_ref), channel_id=1, source_target_pairs={{0,4},{1,5},{2,6},{3,7},{4,0},{5,1},{6,2},{7,3},{8,12},{9,13},{10,... | collective-permute-start | bytes 98312 | tf_op jit(solution)/shard_map/ppermute | solution.py:489
  18.6 3.1 %collective-permute-start.7 = (f32[8,128]{1,0:T(8,128)S(1)}, f32[8,128]{1,0:T(8,128)S(1)}, u32[]{:S(2)}, u32[]{:S(2)}) collective-permute-start(f32[8,128]{1,0:T(8,128)S(1)} %get-tuple-element.75), channel_id=1, source_target_pairs={{0,1},{1,0},{2,3},{3,2},{4,5},{5,4},{6,7},{7,6},{8,9},{9,8},{10,11... | collective-permute-start | bytes 12296 | tf_op jit(solution)/shard_map/ppermute | solution.py:552
  23.3 3.6 %collective-permute-start.8 = (f32[4,16,128]{2,1,0:T(8,128)S(1)}, f32[4,16,128]{2,1,0:T(8,128)S(1)}, u32[]{:S(2)}, u32[]{:S(2)}) collective-permute-start(f32[4,16,128]{2,1,0:T(8,128)S(1)} %get-tuple-element.81), channel_id=1, source_target_pairs={{0,3},{1,2},{2,1},{3,0},{4,7},{5,6},{6,5},{7,4},{8,11},{9,10},{10,... | collective-permute-start | bytes 98312 | tf_op jit(solution)/shard_map/ppermute | solution.py:488
  23.6 3.2 %collective-permute-start.9 = (f32[4,16,128]{2,1,0:T(8,128)S(1)}, f32[4,16,128]{2,1,0:T(8,128)S(1)}, u32[]{:S(2)}, u32[]{:S(2)}) collective-permute-start(f32[4,16,128]{2,1,0:T(8,128)S(1)} %get-tuple-element.82), channel_id=1, source_target_pairs={{0,1},{1,0},{2,3},{3,2},{4,5},{5,4},{6,7},{7,6},{8,9},{9,8},{10,11... | collective-permute-start | bytes 98312 | tf_op jit(solution)/shard_map/ppermute | solution.py:489
  26.9 4.2 %collective-permute-start.10 = (f32[4,16,128]{2,1,0:T(8,128)S(1)}, f32[4,16,128]{2,1,0:T(8,128)S(1)}, u32[]{:S(2)}, u32[]{:S(2)}) collective-permute-start(f32[4,16,128]{2,1,0:T(8,128)S(1)} %get-tuple-element.87), channel_id=1, source_target_pairs={{0,1},{1,0},{2,3},{3,2},{4,8},{5,9},{6,10},{7,11},{8,4},{9,5},{10,... | collective-permute-start | bytes 98312 | tf_op jit(solution)/shard_map/ppermute | solution.py:488
  27.0 4.0 %collective-permute-start.11 = (f32[4,16,128]{2,1,0:T(8,128)S(1)}, f32[4,16,128]{2,1,0:T(8,128)S(1)}, u32[]{:S(2)}, u32[]{:S(2)}) collective-permute-start(f32[4,16,128]{2,1,0:T(8,128)S(1)} %get-tuple-element.85.after_ref), channel_id=1, source_target_pairs={{0,4},{1,5},{2,6},{3,7},{4,0},{5,1},{6,2},{7,3},{8,12},{9,13},{10,... | collective-permute-start | bytes 98312 | tf_op jit(solution)/shard_map/ppermute | solution.py:489

commit v8 on v7

--- a/solution.py
+++ b/solution.py
@@ -74,14 +74,13 @@
     rows, z = fields[0].shape
     count = len(fields)
     for k, field in enumerate(fields):
-        table_ref[0, k * z : (k + 1) * z, :], table_ref[1, k * z : (k + 1) * z, :] = split(field.T)
+        table_ref[k, :z, :], table_ref[k, z:, :] = split(field.T)
     for j in range(row_ref.shape[0] // 2):
         hot = hot_rows(wide_row(row_ref, j), rows)
         hit = lax.broadcasted_iota(i32, (z, WIDE), 0) == wide_row(depth_ref, j)
         for k in range(count):
-            part = slice(k * z, (k + 1) * z)
-            product = jnp.dot(table_ref[0, part], hot, preferred_element_type=f32)
-            product = product + jnp.dot(table_ref[1, part], hot, preferred_element_type=f32)
+            product = jnp.dot(table_ref[k], hot, preferred_element_type=f32)
+            product = product[:z] + product[z:]
             store_row(out_ref, k, j, jnp.sum(jnp.where(hit, product, 0.0), axis=0, keepdims=True))
 
 
@@ -505,7 +504,7 @@
     face = real(comps + 1, max(nx, ny), nz)
     spill = real(2, comps, ny, nz)
     product = 12 * nz * rows * lines[0] * LANES
-    table = pltpu.VMEM((2, comps * nz, rows), bf16)
+    table = pltpu.VMEM((comps, 2 * nz, rows), bf16)
 
     (v, old, drag, inertia, slot, row, depth, key, low, xkey, xface, yface, xlow, own) = call(
         "load", functools.partial(load_kernel, held, count_y),
@@ -519,7 +518,7 @@
     own_even, own_odd = exchange(own, own, "gx")
     s, acc = call(
         "samples", sample_kernel, (v, old, row, depth, inertia), [three, three],
-        [pltpu.VMEM((2, 2 * comps * nz, rows), bf16), pltpu.VMEM((6,) + lines, f32)], flops=2 * product,
+        [pltpu.VMEM((2 * comps, 2 * nz, rows), bf16), pltpu.VMEM((6,) + lines, f32)], flops=2 * product,
     )
     slots = -(-3 * held // 16) * 16
     work = [pltpu.VMEM((WIDE, WIDE), bf16), pltpu.VMEM((WIDE + slots, WIDE), f32)]

time: 31.9 us -> 32 us (level)
  no operation moved by 1% of the time
where the time goes in v8:
time: 32 us; the launch traced here: 31.8 us
  Pallas kernels  16.9 us (53%)
  starting transfers between devices  13 us (41%)
  waiting for transfers between devices  1.05 us (3%)
  between operations  0.8 us (2%)
    pallas_call x14, Pallas kernels, call(): pl.pallas_call(body, name=name, out_shape=outs, in_specs=[HBM if k in in_...  16.9 us
    ppermute x5, starting transfers between devices, exchange(): came_even = lax.ppermute(even_msg, both_axes, near_pairs(axis, False))  9.11 us
    ppermute x5, starting transfers between devices, exchange(): came_odd = lax.ppermute(odd_msg, both_axes, near_pairs(axis, True))  3.22 us
  transfers between devices with their start and end apart: 12, of which 2 were waited for; matrix products, arithmetic and copies ran while one was open for 0% of the time, Pallas kernels for 38%

profile of v8, /device:TPU:0, one launch (start us, length us, event | category | flops | bytes accessed | tf_op | source)
XLA Modules:
  0.0 31.8 jit_solution(8975735691615592793)
XLA Ops:
  0.6 1.2 %load.1 = (f32[3,16,16,128]{3,2,1,0:T(8,128)S(1)}, f32[3,16,16,128]{3,2,1,0:T(8,128)S(1)}, f32[32,128]{1,0:T(8,128)S(1)}, f32[32,128]{1,0:T(8,128)S(1)}, s32[32,...) custom-call(f32[3,16,16,128]{3,2,1,0:T(8,128)} %v_any.1, ...), custom_call_target="tpu_custom_call" | custom-call | bytes 262144 | tf_op jit(solution)/shard_map/load/pallas_call | solution.py:28
  1.8 0.5 %collective-permute-start.1 = (f32[8,128]{1,0:T(8,128)S(1)}, f32[8,128]{1,0:T(8,128)S(1)}, u32[]{:S(2)}, u32[]{:S(2)}) collective-permute-start(f32[8,128]{1,0:T(8,128)S(1)} %get-tuple-element.58.own_ref), channel_id=1, source_target_pairs={{0,1},{1,0},{2,3},{3,2},{4,8},{5,9},{6,10},{7,11},{8,4},{9,5},{10,... | collective-permute-start | bytes 12296 | tf_op jit(solution)/shard_map/ppermute | solution.py:487
  2.4 4.0 %collective-permute-start = (f32[8,128]{1,0:T(8,128)S(1)}, f32[8,128]{1,0:T(8,128)S(1)}, u32[]{:S(2)}, u32[]{:S(2)}) collective-permute-start(f32[8,128]{1,0:T(8,128)S(1)} %get-tuple-element.58.own_ref), channel_id=1, source_target_pairs={{0,4},{1,5},{2,6},{3,7},{4,0},{5,1},{6,2},{7,3},{8,12},{9,13},{10,... | collective-permute-start | bytes 12296 | tf_op jit(solution)/shard_map/ppermute | solution.py:488
  6.4 3.6 %samples.1 = (f32[3,32,128]{2,1,0:T(8,128)S(1)}, f32[3,32,128]{2,1,0:T(8,128)S(1)}) custom-call(f32[3,16,16,128]{3,2,1,0:T(8,128)S(1)} %get-tuple-element.47.v_ref, f32[3,16,16,128]{3,2,1,0:T(8,128)S(1)} %get-tuple-element.48.old_ref, s32[32,128]{1,0:T(8,128)S(1)} %get-tuple-element.49.row_ref, s32[32,128]{1,0:T(8,128)S(1)} %get-tuple-element.50.depth_ref, ...), custom_call_target="tpu_custom_call" | custom-call | flops 3221225472 | bytes 262144 | tf_op jit(solution)/shard_map/samples/pallas_call | solution.py:28
  10.0 0.0 collective-permute-done.1.odd_ref
  10.0 0.0 collective-permute-done.even_ref
  10.0 1.2 %first_forces.1 = (f32[3,32,128]{2,1,0:T(8,128)S(1)}, f32[8,128]{1,0:T(8,128)S(1)}, f32[2,3,16,128]{3,2,1,0:T(8,128)S(1)}, f32[4,16,128]{2,1,0:T(8,128)S(1)}, f3...) custom-call(f32[3,16,16,128]{3,2,1,0:T(8,128)S(1)} %get-tuple-element.47.v_ref, f32[3,32,128]{2,1,0:T(8,128)S(1)} %get-tuple-element.52.s_ref, ...), custom_call_target="tpu_custom_call" | custom-call | flops 805306368 | bytes 262144 | tf_op jit(solution)/shard_map/first_forces/pallas_call | solution.py:28
  11.3 0.5 %collective-permute-start.2 = (f32[4,16,128]{2,1,0:T(8,128)S(1)}, f32[4,16,128]{2,1,0:T(8,128)S(1)}, u32[]{:S(2)}, u32[]{:S(2)}) collective-permute-start(f32[4,16,128]{2,1,0:T(8,128)S(1)} %get-tuple-element.62), channel_id=1, source_target_pairs={{0,3},{1,2},{2,1},{3,0},{4,7},{5,6},{6,5},{7,4},{8,11},{9,10},{10,... | collective-permute-start | bytes 98312 | tf_op jit(solution)/shard_map/ppermute | solution.py:487
  11.7 1.2 %collective-permute-start.3 = (f32[4,16,128]{2,1,0:T(8,128)S(1)}, f32[4,16,128]{2,1,0:T(8,128)S(1)}, u32[]{:S(2)}, u32[]{:S(2)}) collective-permute-start(f32[4,16,128]{2,1,0:T(8,128)S(1)} %get-tuple-element.63), channel_id=1, source_target_pairs={{0,1},{1,0},{2,3},{3,2},{4,5},{5,4},{6,7},{7,6},{8,9},{9,8},{10,11... | collective-permute-start | bytes 98312 | tf_op jit(solution)/shard_map/ppermute | solution.py:488
  13.0 1.8 %deposit.2 = (f32[3,256,128]{2,1,0:T(8,128)S(1)}, f32[8,128]{1,0:T(8,128)S(1)}) custom-call(f32[3,32,128]{2,1,0:T(8,128)S(1)} %get-tuple-element.59.force_ref, s32[32,128]{1,0:T(8,128)S(1)} %get-tuple-element.49.row_ref, s32[32,128]{1,0:T(8,128)S(1)} %get-tuple-element.50.depth_ref, f32[8,128]{1,0:T(8,128)S(1)} %get-tuple-element.60.total_ref), custom_call_target="tpu_custom_call" | custom-call | flops 1610612736 | bytes 262144 | tf_op jit(solution)/shard_map/deposit/pallas_call | solution.py:28
  14.8 0.0 collective-permute-done.3.came_ref.even_ref
  14.8 0.1 collective-permute-start.4
  14.9 0.0 collective-permute-done.2.odd_ref
  15.0 1.7 %collective-permute-start.5 = (f32[4,16,128]{2,1,0:T(8,128)S(1)}, f32[4,16,128]{2,1,0:T(8,128)S(1)}, u32[]{:S(2)}, u32[]{:S(2)}) collective-permute-start(f32[4,16,128]{2,1,0:T(8,128)S(1)} %get-tuple-element.70), channel_id=1, source_target_pairs={{0,1},{1,0},{2,3},{3,2},{4,8},{5,9},{6,10},{7,11},{8,4},{9,5},{10,... | collective-permute-start | bytes 98312 | tf_op jit(solution)/shard_map/ppermute | solution.py:487
  16.7 1.4 %collective-permute-start.6 = (f32[4,16,128]{2,1,0:T(8,128)S(1)}, f32[4,16,128]{2,1,0:T(8,128)S(1)}, u32[]{:S(2)}, u32[]{:S(2)}) collective-permute-start(f32[4,16,128]{2,1,0:T(8,128)S(1)} %get-tuple-element.66.after_ref), channel_id=1, source_target_pairs={{0,4},{1,5},{2,6},{3,7},{4,0},{5,1},{6,2},{7,3},{8,12},{9,13},{10,... | collective-permute-start | bytes 98312 | tf_op jit(solution)/shard_map/ppermute | solution.py:488
  18.1 0.5 %collective-permute-done.4.came_ref = f32[16,128]{1,0:T(8,128)S(1)} collective-permute-done((f32[16,128]{1,0:T(8,128)S(1)}, f32[16,128]{1,0:T(8,128)S(1)}, u32[]{:S(2)}, u32[]{:S(2)}) %collective-permute-start.4) | collective-permute-done | bytes 8224 | tf_op jit(solution)/shard_map/ppermute | solution.py:548
  18.6 0.6 %collective-permute-start.7 = (f32[8,128]{1,0:T(8,128)S(1)}, f32[8,128]{1,0:T(8,128)S(1)}, u32[]{:S(2)}, u32[]{:S(2)}) collective-permute-start(f32[8,128]{1,0:T(8,128)S(1)} %get-tuple-element.75), channel_id=1, source_target_pairs={{0,1},{1,0},{2,3},{3,2},{4,5},{5,4},{6,7},{7,6},{8,9},{9,8},{10,11... | collective-permute-start | bytes 12296 | tf_op jit(solution)/shard_map/ppermute | solution.py:551
  19.2 2.5 %middle.1 = (f32[3,16,16,128]{3,2,1,0:T(8,128)S(1)}, f32[3,32,128]{2,1,0:T(8,128)S(1)}) custom-call(f32[3,16,16,128]{3,2,1,0:T(8,128)S(1)} %get-tuple-element.47.v_ref, f32[3,256,128]{2,1,0:T(8,128)S(1)} %get-tuple-element.61.after_ref.load_ref, f32[4,16,128]{2,1,0:T(8,128)S(1)} %collective-permute-done.2.odd_ref, ...), custom_call_target="tpu_custom_call" | custom-call | flops 1610612736 | bytes 262144 | tf_op jit(solution)/shard_map/middle/pallas_call | solution.py:28
  21.7 0.0 collective-permute-done.7.shared_ref
  21.7 0.0 collective-permute-done.5.xo_ref
  21.7 0.0 collective-permute-done.6.xe_ref
  21.7 1.5 %second_forces.1 = (f32[3,16,16,128]{3,2,1,0:T(8,128)S(1)}, f32[3,32,128]{2,1,0:T(8,128)S(1)}, f32[8,128]{1,0:T(8,128)S(1)}, f32[4,16,128]{2,1,0:T(8,128)S(1)}, f32[4,16,128]{2,1,0:T(8,128)S(1)}) custom-call(f32[3,16,16,128]{3,2,1,0:T(8,128)S(1)} %get-tuple-element.68.l_ref, f32[3,32,128]{2,1,0:T(8,128)S(1)} %get-tuple-element.69.sp_ref, ...), custom_call_target="tpu_custom_call" | custom-call | flops 805306368 | bytes 262144 | tf_op jit(solution)/shard_map/second_forces/pallas_call | solution.py:28
  23.3 0.3 %collective-permute-start.8 = (f32[4,16,128]{2,1,0:T(8,128)S(1)}, f32[4,16,128]{2,1,0:T(8,128)S(1)}, u32[]{:S(2)}, u32[]{:S(2)}) collective-permute-start(f32[4,16,128]{2,1,0:T(8,128)S(1)} %get-tuple-element.81), channel_id=1, source_target_pairs={{0,3},{1,2},{2,1},{3,0},{4,7},{5,6},{6,5},{7,4},{8,11},{9,10},{10,... | collective-permute-start | bytes 98312 | tf_op jit(solution)/shard_map/ppermute | solution.py:487
  23.6 0.4 %collective-permute-start.9 = (f32[4,16,128]{2,1,0:T(8,128)S(1)}, f32[4,16,128]{2,1,0:T(8,128)S(1)}, u32[]{:S(2)}, u32[]{:S(2)}) collective-permute-start(f32[4,16,128]{2,1,0:T(8,128)S(1)} %get-tuple-element.82), channel_id=1, source_target_pairs={{0,1},{1,0},{2,3},{3,2},{4,5},{5,4},{6,7},{7,6},{8,9},{9,8},{10,11... | collective-permute-start | bytes 98312 | tf_op jit(solution)/shard_map/ppermute | solution.py:488
  24.0 1.0 %spills.1 = (f32[2,3,16,128]{3,2,1,0:T(8,128)S(1)}, f32[8,128]{1,0:T(8,128)S(1)}) custom-call(f32[3,16,16,128]{3,2,1,0:T(8,128)S(1)} %get-tuple-element.76.v_ref, f32[3,32,128]{2,1,0:T(8,128)S(1)} %get-tuple-element.77.force_ref, s32[32,128]{1,0:T(8,128)S(1)} %get-tuple-element.78.key_ref, s32[32,128]{1,0:T(8,128)S(1)} %get-tuple-element.57.low_ref, ...), custom_call_target="tpu_custom_call" | custom-call | flops 402653184 | bytes 262144 | tf_op jit(solution)/shard_map/spills/pallas_call | solution.py:28
  25.0 1.3 %deposit.3 = (f32[2,256,128]{2,1,0:T(8,128)S(1)}, f32[8,128]{1,0:T(8,128)S(1)}) custom-call(f32[3,32,128]{2,1,0:T(8,128)S(1)} %get-tuple-element.77.force_ref, s32[32,128]{1,0:T(8,128)S(1)} %get-tuple-element.49.row_ref, s32[32,128]{1,0:T(8,128)S(1)} %get-tuple-element.50.depth_ref, f32[8,128]{1,0:T(8,128)S(1)} %get-tuple-element.79.total_ref), custom_call_target="tpu_custom_call" | custom-call | flops 1073741824 | bytes 262144 | tf_op jit(solution)/shard_map/deposit/pallas_call | solution.py:28
  26.3 0.5 %collective-permute-done.8.odd_ref = f32[4,16,128]{2,1,0:T(8,128)S(1)} collective-permute-done((f32[4,16,128]{2,1,0:T(8,128)S(1)}, f32[4,16,128]{2,1,0:T(8,128)S(1)}, u32[]{:S(2)}, u32[]{:S(2)}) %collective-permute-start.8) | collective-permute-done | bytes 32800 | tf_op jit(solution)/shard_map/ppermute | solution.py:487
  26.8 0.0 collective-permute-done.9.even_ref
  26.9 0.2 collective-permute-start.10
  27.0 2.1 %collective-permute-start.11 = (f32[4,16,128]{2,1,0:T(8,128)S(1)}, f32[4,16,128]{2,1,0:T(8,128)S(1)}, u32[]{:S(2)}, u32[]{:S(2)}) collective-permute-start(f32[4,16,128]{2,1,0:T(8,128)S(1)} %get-tuple-element.85.after_ref), channel_id=1, source_target_pairs={{0,4},{1,5},{2,6},{3,7},{4,0},{5,1},{6,2},{7,3},{8,12},{9,13},{10,... | collective-permute-start | bytes 98312 | tf_op jit(solution)/shard_map/ppermute | solution.py:488
  29.1 1.9 %finish.1 = (f32[3,16,16,128]{3,2,1,0:T(8,128)}, f32[3,2,16,128]{3,2,1,0:T(8,128)S(1)}) custom-call(f32[3,16,16,128]{3,2,1,0:T(8,128)S(1)} %get-tuple-element.76.v_ref, f32[2,256,128]{2,1,0:T(8,128)S(1)} %get-tuple-element.80.after_ref.load_ref, f32[4,16,128]{2,1,0:T(8,128)S(1)} %collective-permute-done.8.odd_ref, ...), custom_call_target="tpu_custom_call" | custom-call | flops 536870912 | bytes 262144 | tf_op jit(solution)/shard_map/finish/pallas_call | solution.py:28
  31.0 0.0 collective-permute-done.10.xo_ref
  31.0 0.0 collective-permute-done.11.xe_ref
  31.0 0.8 %last.1 = (f32[3,16]{1,0:T(4,128)}, f32[3,16,16,128]{3,2,1,0:T(8,128)}) custom-call(f32[3,2,16,128]{3,2,1,0:T(8,128)S(1)} %get-tuple-element.86.face_ref, f32[4,16,128]{2,1,0:T(8,128)S(1)} %collective-permute-done.10.xo_ref, f32[4,16,128]{2,1,0:T(8,128)S(1)} %collective-permute-done.11.xe_ref, ...), custom_call_target="tpu_custom_call", output_to_operand_aliasing={{1}: (5, {})} | custom-call | bytes 262144 | tf_op jit(solution)/shard_map/last/pallas_call | solution.py:28
  (4 shorter events, 0.1 us)
Async XLA Ops:
  1.8 8.2 %collective-permute-start.1 = (f32[8,128]{1,0:T(8,128)S(1)}, f32[8,128]{1,0:T(8,128)S(1)}, u32[]{:S(2)}, u32[]{:S(2)}) collective-permute-start(f32[8,128]{1,0:T(8,128)S(1)} %get-tuple-element.58.own_ref), channel_id=1, source_target_pairs={{0,1},{1,0},{2,3},{3,2},{4,8},{5,9},{6,10},{7,11},{8,4},{9,5},{10,... | collective-permute-start | bytes 12296 | tf_op jit(solution)/shard_map/ppermute | solution.py:487
  2.4 7.7 %collective-permute-start = (f32[8,128]{1,0:T(8,128)S(1)}, f32[8,128]{1,0:T(8,128)S(1)}, u32[]{:S(2)}, u32[]{:S(2)}) collective-permute-start(f32[8,128]{1,0:T(8,128)S(1)} %get-tuple-element.58.own_ref), channel_id=1, source_target_pairs={{0,4},{1,5},{2,6},{3,7},{4,0},{5,1},{6,2},{7,3},{8,12},{9,13},{10,... | collective-permute-start | bytes 12296 | tf_op jit(solution)/shard_map/ppermute | solution.py:488
  11.3 3.7 %collective-permute-start.2 = (f32[4,16,128]{2,1,0:T(8,128)S(1)}, f32[4,16,128]{2,1,0:T(8,128)S(1)}, u32[]{:S(2)}, u32[]{:S(2)}) collective-permute-start(f32[4,16,128]{2,1,0:T(8,128)S(1)} %get-tuple-element.62), channel_id=1, source_target_pairs={{0,3},{1,2},{2,1},{3,0},{4,7},{5,6},{6,5},{7,4},{8,11},{9,10},{10,... | collective-permute-start | bytes 98312 | tf_op jit(solution)/shard_map/ppermute | solution.py:487
  11.7 3.1 %collective-permute-start.3 = (f32[4,16,128]{2,1,0:T(8,128)S(1)}, f32[4,16,128]{2,1,0:T(8,128)S(1)}, u32[]{:S(2)}, u32[]{:S(2)}) collective-permute-start(f32[4,16,128]{2,1,0:T(8,128)S(1)} %get-tuple-element.63), channel_id=1, source_target_pairs={{0,1},{1,0},{2,3},{3,2},{4,5},{5,4},{6,7},{7,6},{8,9},{9,8},{10,11... | collective-permute-start | bytes 98312 | tf_op jit(solution)/shard_map/ppermute | solution.py:488
  14.8 3.7 %collective-permute-start.4 = (f32[16,128]{1,0:T(8,128)S(1)}, f32[16,128]{1,0:T(8,128)S(1)}, u32[]{:S(2)}, u32[]{:S(2)}) collective-permute-start(f32[16,128]{1,0:T(8,128)S(1)} %pair.1), channel_id=1, source_target_pairs={{0,4},{1,8},{2,6},{3,10},{4,0},{5,12},{6,2},{7,14},{8,1},{9,16},{1... | collective-permute-start | bytes 24584 | tf_op jit(solution)/shard_map/ppermute | solution.py:548
  15.0 6.7 %collective-permute-start.5 = (f32[4,16,128]{2,1,0:T(8,128)S(1)}, f32[4,16,128]{2,1,0:T(8,128)S(1)}, u32[]{:S(2)}, u32[]{:S(2)}) collective-permute-start(f32[4,16,128]{2,1,0:T(8,128)S(1)} %get-tuple-element.70), channel_id=1, source_target_pairs={{0,1},{1,0},{2,3},{3,2},{4,8},{5,9},{6,10},{7,11},{8,4},{9,5},{10,... | collective-permute-start | bytes 98312 | tf_op jit(solution)/shard_map/ppermute | solution.py:487
  16.7 5.0 %collective-permute-start.6 = (f32[4,16,128]{2,1,0:T(8,128)S(1)}, f32[4,16,128]{2,1,0:T(8,128)S(1)}, u32[]{:S(2)}, u32[]{:S(2)}) collective-permute-start(f32[4,16,128]{2,1,0:T(8,128)S(1)} %get-tuple-element.66.after_ref), channel_id=1, source_target_pairs={{0,4},{1,5},{2,6},{3,7},{4,0},{5,1},{6,2},{7,3},{8,12},{9,13},{10,... | collective-permute-start | bytes 98312 | tf_op jit(solution)/shard_map/ppermute | solution.py:488
  18.6 3.1 %collective-permute-start.7 = (f32[8,128]{1,0:T(8,128)S(1)}, f32[8,128]{1,0:T(8,128)S(1)}, u32[]{:S(2)}, u32[]{:S(2)}) collective-permute-start(f32[8,128]{1,0:T(8,128)S(1)} %get-tuple-element.75), channel_id=1, source_target_pairs={{0,1},{1,0},{2,3},{3,2},{4,5},{5,4},{6,7},{7,6},{8,9},{9,8},{10,11... | collective-permute-start | bytes 12296 | tf_op jit(solution)/shard_map/ppermute | solution.py:551
  23.3 3.6 %collective-permute-start.8 = (f32[4,16,128]{2,1,0:T(8,128)S(1)}, f32[4,16,128]{2,1,0:T(8,128)S(1)}, u32[]{:S(2)}, u32[]{:S(2)}) collective-permute-start(f32[4,16,128]{2,1,0:T(8,128)S(1)} %get-tuple-element.81), channel_id=1, source_target_pairs={{0,3},{1,2},{2,1},{3,0},{4,7},{5,6},{6,5},{7,4},{8,11},{9,10},{10,... | collective-permute-start | bytes 98312 | tf_op jit(solution)/shard_map/ppermute | solution.py:487
  23.6 3.2 %collective-permute-start.9 = (f32[4,16,128]{2,1,0:T(8,128)S(1)}, f32[4,16,128]{2,1,0:T(8,128)S(1)}, u32[]{:S(2)}, u32[]{:S(2)}) collective-permute-start(f32[4,16,128]{2,1,0:T(8,128)S(1)} %get-tuple-element.82), channel_id=1, source_target_pairs={{0,1},{1,0},{2,3},{3,2},{4,5},{5,4},{6,7},{7,6},{8,9},{9,8},{10,11... | collective-permute-start | bytes 98312 | tf_op jit(solution)/shard_map/ppermute | solution.py:488
  26.9 4.2 %collective-permute-start.10 = (f32[4,16,128]{2,1,0:T(8,128)S(1)}, f32[4,16,128]{2,1,0:T(8,128)S(1)}, u32[]{:S(2)}, u32[]{:S(2)}) collective-permute-start(f32[4,16,128]{2,1,0:T(8,128)S(1)} %get-tuple-element.87), channel_id=1, source_target_pairs={{0,1},{1,0},{2,3},{3,2},{4,8},{5,9},{6,10},{7,11},{8,4},{9,5},{10,... | collective-permute-start | bytes 98312 | tf_op jit(solution)/shard_map/ppermute | solution.py:487
  27.0 4.0 %collective-permute-start.11 = (f32[4,16,128]{2,1,0:T(8,128)S(1)}, f32[4,16,128]{2,1,0:T(8,128)S(1)}, u32[]{:S(2)}, u32[]{:S(2)}) collective-permute-start(f32[4,16,128]{2,1,0:T(8,128)S(1)} %get-tuple-element.85.after_ref), channel_id=1, source_target_pairs={{0,4},{1,5},{2,6},{3,7},{4,0},{5,1},{6,2},{7,3},{8,12},{9,13},{10,... | collective-permute-start | bytes 98312 | tf_op jit(solution)/shard_map/ppermute | solution.py:488
